TPU v7x, 512 devices: a whole 4x4x16 slice. The times are simulated.
512 devices in a mesh: tm: 64 (over x, z), col: 8 (over y, core).
Axes of the slice: x: 4, y: 4, z: 16, core: 2. Of those that a mesh axis runs over, the one named last changes fastest.
Arguments:
- observations: bfloat16 [8192, 8192], P(('tm', 'col')), may hold values from -6 to 6
- site_start: int32 [8192], P(('tm', 'col')), may hold values from 0 to 4095
- site_count: int32 [8192], P(('tm', 'col')), may hold values from 2048 to 8192
- site_gain: bfloat16 [8192, 1024], P(('tm', 'col')), may hold values from -0.0625 to 0.0625
- site_loading: bfloat16 [8192, 1024], P(('tm', 'col')), may hold values from -0.1875 to 0.1875
- decay: float32 [8192, 1024], P('tm'), may hold values from 0 to 1, as said below
- persistence: float32 [1024], replicated, may hold values from 0 to 1, as said below
Outputs:
- smoothed: float32 [8192, 1024], P('tm', 'col')
- predicted: bfloat16 [8192, 8192], P(('tm', 'col'))
Inputs may be any that keep to these rules, and one draw needn't show every extreme that they name: Station s reports from step site_start[s] for site_count[s] steps, cut at the last step. Every decay lies strictly between 0 and 1. `persistence`: every factor lies strictly between 0 and 1.
All inputs are finite; a program needn't handle non-finite values.
Results may differ from a plain program's by a relative error of at most 0.0049.
Values may be sent and summed in bfloat16 or wider, within the bound.
No kernel may reach another device: no remote copies, remote signals or barrier semaphores. Data moves between devices by JAX's collectives and lax.ppermute only.
A program may use at most 64 MiB of HBM per device.

v0:
```python
import jax
import jax.numpy as jnp
from jax import lax
from jax.sharding import PartitionSpec as P


def entering_2(part, axis, combine, identity, reverse):
    count = lax.axis_size(axis)
    place = lax.axis_index(axis)
    ahead = count - 1 - place if reverse else place
    gathered = jax.tree.map(lambda a: lax.all_gather(a, axis), part)
    state = jax.tree.map(lambda a, e: jnp.zeros_like(a) + jnp.asarray(e, a.dtype), part, identity)

    def one(turn, state):
        source = count - 1 - turn if reverse else turn
        return combine(
            state, jax.tree.map(lambda a: lax.dynamic_index_in_dim(a, source, 0, False), gathered)
        )

    return lax.fori_loop(0, ahead, one, state)


def combine(earlier, later_half):
    return (later_half[0] * earlier[0], later_half[0] * earlier[1] + later_half[1])


def forward_local(driving, decays):
    inject = jnp.sqrt(1.0 - decays * decays) * driving
    return lax.associative_scan(combine, (decays, inject), axis=0)


def backward_local(filtered, decays, persist):
    carry_rate = persist[None, :] * decays
    weight = (1.0 - carry_rate * decays) * filtered
    return lax.associative_scan(combine, (carry_rate, weight), reverse=True, axis=0)


def folded_drive(site_gain, station_rows):
    return lax.dot_general(
        station_rows,
        lax.all_gather(site_gain, "tm", axis=0, tiled=True),
        (((0,), (0,)), ((), ())),
        preferred_element_type=jnp.float32,
    )


def per_device(observations, site_start, site_count, site_gain, site_loading, decay, persistence):
    epoch_position = lax.broadcasted_iota(jnp.int32, observations.shape, 1)
    start_col = site_start[:, None]
    reporting = (epoch_position >= start_col) & (epoch_position < start_col + site_count[:, None])
    masked = jnp.where(reporting, observations, jnp.zeros_like(observations))
    station_rows = lax.all_to_all(masked, "tm", split_axis=1, concat_axis=0, tiled=True)
    loadings = lax.all_gather(site_loading, "tm", axis=0, tiled=True)
    col_pos = lax.axis_index("col")
    partial_drive = folded_drive(site_gain, station_rows)
    driving = lax.psum_scatter(partial_drive, "col", scatter_dimension=1, tiled=True)
    col_share = driving.shape[1]
    decays = lax.dynamic_slice_in_dim(decay, col_pos * col_share, col_share, 1)
    persist = lax.dynamic_slice_in_dim(persistence, col_pos * col_share, col_share, 0)
    identity = (jnp.ones((col_share,), jnp.float32), jnp.zeros((col_share,), jnp.float32))
    decayed, local_state = forward_local(driving, decays)
    entering = entering_2((decayed[-1], local_state[-1]), "tm", combine, identity, False)
    filtered = local_state + decayed * entering[1][None, :]
    products, local_smooth = backward_local(filtered, decays, persist)
    leaving = entering_2((products[0], local_smooth[0]), "tm", combine, identity, True)
    smoothed = local_smooth + products * leaving[1][None, :]
    rounded = smoothed.astype(jnp.bfloat16)
    predicted = lax.dot_general(
        loadings,
        lax.all_gather(rounded, "col", axis=1, tiled=True),
        (((1,), (1,)), ((), ())),
        preferred_element_type=jnp.float32,
    )
    outgoing = predicted.astype(jnp.bfloat16)
    returned = lax.all_to_all(outgoing, "tm", split_axis=0, concat_axis=1, tiled=True)
    return (smoothed, returned)


def solution(mesh):
    return jax.shard_map(
        per_device,
        mesh=mesh,
        in_specs=(
            P(("tm", "col"), None),
            P(("tm", "col")),
            P(("tm", "col")),
            P(("tm", "col"), None),
            P(("tm", "col"), None),
            P("tm", None),
            P(),
        ),
        out_specs=(P("tm", "col"), P(("tm", "col"), None)),
        check_vma=False,
    )
```

profile of v0, /device:TPU:1, one launch (start us, length us, event | category | flops | bytes accessed | tf_op | source)
XLA Modules:
  0.0 546.1 jit_solution(5465234625467132092)
XLA Ops:
  7.2 0.0 all-gather.7.cloned.1.call-start
  7.2 0.7 all-gather.7.cloned.1.call-update
  7.9 0.0 reduce-scatter.2.cloned.1.call-start
  7.9 0.7 add.328
  8.6 1.2 copy_bitcast_fusion.1
  9.8 38.3 %all_to_all.38 = bf16[16,64,128]{2,0,1:T(8,128)(2,1)S(1)} all-to-all(bf16[16,64,128]{2,0,1:T(8,128)(2,1)S(1)} %copy_bitcast_fusion.1), channel_id=1, replica_groups=mesh['tm'=64,'col'=8] {'tm'}, dimensions={1} | all-to-all | bytes 524288 | tf_op jit(solution)/shard_map/all_to_all | solution.py:52
  48.1 100.6 %all-gather.7.cloned.1.call-done = bf16[1024,1024]{1,0:T(8,128)(2,1)} async-done(((bf16[16,1024]{1,0:T(8,128)(2,1)}), bf16[1024,1024]{1,0:T(8,128)(2,1)}) %all-gather.7.cloned.1.call-update) | async-done | bytes 2097168 | tf_op jit(solution)/shard_map/all_gather | solution.py:41
  148.7 2.9 fusion.19
  151.6 0.0 reduce-scatter.2.cloned.1.call-update
  151.6 0.0 all-gather.9.cloned.1.call-start
  151.6 0.7 all-gather.9.cloned.1.call-update
  152.3 0.8 dynamic_slice.30
  153.1 0.8 broadcast_multiply_fusion
  154.0 0.7 constant_dynamic-slice_fusion
  154.8 38.7 %reduce-scatter.2.cloned.1.call-done = f32[128,128]{1,0:T(8,128)} async-done(((f32[128,1024]{1,0:T(8,128)}), f32[128,128]{1,0:T(8,128)}) %reduce-scatter.2.cloned.1.call-update) | async-done | bytes 65552 | tf_op jit(solution)/shard_map/reduce_scatter | solution.py:56
  193.5 0.9 sqrt_multiply_fusion
  195.8 65.2 %all-gather.1 = f32[64,1,128]{2,1,0:T(1,128)S(1)} all-gather(f32[1,1,128]{2,1,0:T(1,128)S(1)} %add_bitcast_fusion.2), channel_id=1, replica_groups=mesh['tm'=64,'col'=8] {'tm'}, dimensions={0}, use_global_device_ids=true | all-gather | bytes 33280 | tf_op jit(solution)/shard_map/all_gather | solution.py:11
  261.1 58.9 %all-gather = f32[64,1,128]{2,1,0:T(1,128)S(1)} all-gather(f32[1,1,128]{2,1,0:T(1,128)S(1)} %add_bitcast_fusion.3), channel_id=1, replica_groups=mesh['tm'=64,'col'=8] {'tm'}, dimensions={0}, use_global_device_ids=true | all-gather | bytes 33280 | tf_op jit(solution)/shard_map/all_gather | solution.py:11
  321.7 58.0 %all-gather.3 = f32[64,1,128]{2,1,0:T(1,128)S(1)} all-gather(f32[1,1,128]{2,1,0:T(1,128)S(1)} %add_bitcast_fusion), channel_id=1, replica_groups=mesh['tm'=64,'col'=8] {'tm'}, dimensions={0}, use_global_device_ids=true | all-gather | bytes 33280 | tf_op jit(solution)/shard_map/all_gather | solution.py:11
  379.7 54.3 %all-gather.2 = f32[64,1,128]{2,1,0:T(1,128)S(1)} all-gather(f32[1,1,128]{2,1,0:T(1,128)S(1)} %add_bitcast_fusion.1), channel_id=1, replica_groups=mesh['tm'=64,'col'=8] {'tm'}, dimensions={0}, use_global_device_ids=true | all-gather | bytes 33280 | tf_op jit(solution)/shard_map/all_gather | solution.py:11
  434.0 2.8 while.27
  436.8 0.6 fusion.10
  437.4 71.2 %all_gather.26 = bf16[128,1024]{1,0:T(8,128)(2,1)S(1)} all-gather(bf16[128,128]{1,0:T(8,128)(2,1)S(1)} %get-tuple-element.152), channel_id=1, replica_groups=mesh['tm'=64,'col'=8] {'col'}, dimensions={1}, use_global_device_ids=true | all-gather | bytes 294912 | tf_op jit(solution)/shard_map/all_gather | solution.py:70
  508.6 0.0 all-gather.9.cloned.1.call-done
  508.6 2.4 fusion
  511.1 0.2 copy.15
  511.2 27.6 %all_to_all.39 = bf16[64,16,128]{2,1,0:T(8,128)(2,1)S(1)} all-to-all(bf16[64,16,128]{2,1,0:T(8,128)(2,1)S(1)} %bitcast.53), channel_id=1, replica_groups=mesh['tm'=64,'col'=8] {'tm'}, dimensions={0} | all-to-all | bytes 524288 | tf_op jit(solution)/shard_map/all_to_all | solution.py:75
  538.9 0.7 copy_bitcast_fusion
  (289 shorter events, 3.4 us)
Async XLA Ops:
  7.2 141.5 %all-gather.7.cloned.1.call-start = ((), (), s32[]{:S(2)}) async-start(), calls=%async_computation.3 | async-start | bytes 2129920 | tf_op jit(solution)/shard_map/all_gather | solution.py:41
  7.9 185.6 %reduce-scatter.2.cloned.1.call-start = ((), (), s32[]{:S(2)}) async-start(), calls=%async_computation.4 | async-start | bytes 589824 | tf_op jit(solution)/shard_map/reduce_scatter | solution.py:56
  151.6 357.0 %all-gather.9.cloned.1.call-start = ((), (), s32[]{:S(2)}) async-start(), calls=%async_computation.5 | async-start | bytes 2129920 | tf_op jit(solution)/shard_map/all_gather | solution.py:53
Sparse Core Ops, SparseCore 0:
  10.9 137.7 all-gather.6
  151.7 41.7 reduce-scatter.1
  196.9 132.6 all-gather.8
where the time goes:
time: 547 us; the launch traced here: 546 us
  blocking collectives  374 us (68%)
  waiting for transfers between devices  141 us (26%)
  between operations  14.9 us (3%)
  other arithmetic  6 us (1%)
    all_gather x4, blocking collectives, entering_2(): gathered = jax.tree.map(lambda a: lax.all_gather(a, axis), part)  236 us
    all_gather x1, waiting for transfers between devices, folded_drive(): lax.all_gather(site_gain, 'tm', axis=0, tiled=True)  101 us
    all_gather x1, blocking collectives, per_device(): lax.all_gather(rounded, 'col', axis=1, tiled=True)  71.2 us
    reduce_scatter x1, waiting for transfers between devices, per_device(): lax.psum_scatter(partial_drive, 'col', scatter_dimension=1, tiled=True)  38.7 us
    all_to_all x1, blocking collectives, per_device(): lax.all_to_all(masked, 'tm', split_axis=1, concat_axis=0, tiled=True)  38.3 us
    all_to_all x1, blocking collectives, per_device(): lax.all_to_all(outgoing, 'tm', split_axis=0, concat_axis=1, tiled=True)  27.6 us
  transfers between devices with their start and end apart: 3, of which 2 were waited for; matrix products, arithmetic and copies ran while one was open for 2% of the time, Pallas kernels for 0%

commit v1 on v0

v1 whole, which is shorter than its diff:
```python
import jax
import jax.numpy as jnp
from jax import lax
from jax.experimental import pallas as pl
from jax.experimental.pallas import tpu as pltpu
from jax.sharding import Mesh, PartitionSpec as P

ROWS = 8
STEPS = 4


def front_kernel(start_ref, count_ref, values_ref, gain_ref, out_ref):
    devices, sites, width = out_ref.shape
    span = width - gain_ref.shape[1]
    first = pl.program_id(0) * devices
    site = lax.broadcasted_iota(jnp.int32, (sites, span), 0)
    start = end = jnp.zeros((sites, span), jnp.int32)
    for s in range(sites):
        start = jnp.where(site == s, start_ref[s], start)
        end = jnp.where(site == s, start_ref[s] + count_ref[s], end)
    epoch = lax.broadcasted_iota(jnp.int32, (sites, span), 1) + first * span
    for to in range(devices):
        values = values_ref[:, to * span:(to + 1) * span].astype(jnp.float32)
        inside = (epoch + to * span >= start) & (epoch + to * span < end)
        out_ref[to, :, :span] = jnp.where(inside, values, 0.0).astype(out_ref.dtype)
        out_ref[to, :, span:] = gain_ref[...]


def drive_kernel(got_ref, out_ref):
    sources, sites, _ = got_ref.shape
    blocks, parts, slab, share = out_ref.shape
    span = parts * slab
    rows = got_ref[:, :, :span].reshape(sources * sites, span)
    gains = got_ref[:, :, span:].reshape(sources * sites, blocks * share)
    partial = lax.dot_general(rows, gains, (((0,), (0,)), ((), ())), preferred_element_type=jnp.float32)
    partial = partial.astype(out_ref.dtype)
    for block in range(blocks):
        for part in range(parts):
            out_ref[block, part] = partial[part * slab:(part + 1) * slab, block * share:(block + 1) * share]


def shifted(value, by, fill):
    count = value.shape[0]
    row = lax.broadcasted_iota(jnp.int32, value.shape, 0)
    moved = pltpu.roll(value, by % count, 0)
    inside = row >= by if by > 0 else row < count + by
    return jnp.where(inside, moved, fill)


def across(rate, states, sign):
    step = 1
    while step < ROWS:
        states = [s + rate * shifted(s, sign * step, 0.0) for s in states]
        rate = rate * shifted(rate, sign * step, 1.0)
        step *= 2
    return shifted(rate, sign, 1.0), [shifted(s, sign, 0.0) for s in states]


def scan_kernel(parts_ref, decay_ref, persist_ref, smooth_ref, entry_ref, product_ref, summary_ref, inj):
    sources, slab, width = parts_ref.shape
    total = parts_ref[0].astype(jnp.float32)
    for source in range(1, sources):
        total = total + parts_ref[source].astype(jnp.float32)
    inj[...] = jnp.sqrt(1.0 - decay_ref[...] * decay_ref[...]) * total
    depth = slab // ROWS
    persist = persist_ref[...]

    def rows(ref, j):
        return ref[pl.ds(j, ROWS, stride=depth), :]

    decays = [rows(decay_ref, j) for j in range(depth)]
    decayed, local = [decays[0]], [rows(inj, 0)]
    for j in range(1, depth):
        decayed.append(decays[j] * decayed[-1])
        local.append(decays[j] * local[-1] + rows(inj, j))
    enter_rate, (enter,) = across(decayed[-1], [local[-1]], 1)
    local = [h + a * enter for h, a in zip(local, decayed)]
    decayed = [a * enter_rate for a in decayed]
    products, smooth, entry = [None] * depth, [None] * depth, [None] * depth
    for j in reversed(range(depth)):
        rate = persist * decays[j]
        keep = 1.0 - rate * decays[j]
        if j == depth - 1:
            products[j], smooth[j], entry[j] = rate, keep * local[j], keep * decayed[j]
        else:
            products[j] = rate * products[j + 1]
            smooth[j] = rate * smooth[j + 1] + keep * local[j]
            entry[j] = rate * entry[j + 1] + keep * decayed[j]
    leave_rate, (leave_smooth, leave_entry) = across(products[0], [smooth[0], entry[0]], -1)
    for j in range(depth):
        smooth[j] = smooth[j] + products[j] * leave_smooth
        entry[j] = entry[j] + products[j] * leave_entry
        products[j] = products[j] * leave_rate
        smooth_ref[pl.ds(j, ROWS, stride=depth), :] = smooth[j]
        entry_ref[pl.ds(j, ROWS, stride=depth), :] = entry[j]
        product_ref[pl.ds(j, ROWS, stride=depth), :] = products[j]
    summary = [decayed[-1][ROWS - 1:], local[-1][ROWS - 1:], products[0][:1], smooth[0][:1], entry[0][:1]]
    summary = jnp.concatenate(summary + [jnp.zeros((3, width), jnp.float32)], axis=0)
    for to in range(summary_ref.shape[0]):
        summary_ref[to] = summary


def finish_kernel(place_ref, slabs_ref, smooth_ref, entry_ref, product_ref, out_ref, rounded_ref, fwd, bwd):
    count, _, width = slabs_ref.shape

    def of(at, what):
        return slabs_ref[at, what:what + 1, :]

    state = jnp.zeros((1, width), jnp.float32)
    for at in range(count):
        fwd[at:at + 1, :] = state
        state = of(at, 0) * state + of(at, 1)
    state = jnp.zeros((1, width), jnp.float32)
    for at in reversed(range(count)):
        bwd[at:at + 1, :] = state
        state = of(at, 2) * state + (of(at, 3) + of(at, 4) * fwd[at:at + 1, :])
    place = place_ref[0]
    f_in, g_in = fwd[pl.ds(place, 1), :], bwd[pl.ds(place, 1), :]
    smoothed = smooth_ref[...] + entry_ref[...] * f_in + product_ref[...] * g_in
    out_ref[...] = smoothed
    rounded_ref[...] = smoothed.T.astype(rounded_ref.dtype)


def predict_kernel(loading_ref, rounded_ref, out_ref):
    blocks, parts, share, slab = rounded_ref.shape
    devices, sites, _ = out_ref.shape
    loadings = loading_ref[...]
    for part in range(parts):
        states = rounded_ref[:, part].reshape(blocks * share, slab)
        predicted = jnp.dot(loadings, states, preferred_element_type=jnp.float32)
        out_ref[:, :, part * slab:(part + 1) * slab] = predicted.astype(out_ref.dtype).reshape(devices, sites, slab)


def call(kernel, name, out_shape, *args, scratch=(), scalars=0, **grid):
    if not grid:
        specs = [pl.BlockSpec(memory_space=pltpu.SMEM)] * scalars
        specs += [pl.BlockSpec(memory_space=pltpu.VMEM)] * (len(args) - scalars)
        grid = dict(in_specs=specs)
    return pl.pallas_call(
        kernel,
        out_shape=out_shape,
        scratch_shapes=list(scratch),
        compiler_params=pltpu.CompilerParams(vmem_limit_bytes=32 << 20),
        name=name,
        **grid,
    )(*args)


def per_device(observations, site_start, site_count, site_gain, site_loading, decay, persistence):
    planes, col, plane = ("zh", "zl"), ("y", "core"), ("x", "y", "core")
    line = plane + ("zl",)
    blocks, parts, nc = lax.axis_size("zh"), lax.axis_size("zl"), lax.axis_size(col)
    devices, slabs = lax.axis_size(plane), lax.axis_size(line)
    sites, epochs = observations.shape
    slab, span = epochs // slabs, epochs // devices
    basis = site_gain.shape[1]
    share = basis // blocks
    f32, bf16 = jnp.float32, jnp.bfloat16
    shape = jax.ShapeDtypeStruct
    turn = [
        ((h * parts + l) * nc + c, (c * parts + l) * nc + h)
        for h in range(blocks) for l in range(parts) for c in range(nc)
    ]

    loadings = lax.all_gather(site_loading, plane, axis=0, tiled=True)

    sent = call(
        front_kernel, "front", shape((devices, sites, span + basis), bf16),
        site_start, site_count, observations, site_gain, grid=(STEPS,),
        in_specs=[pl.BlockSpec(memory_space=pltpu.SMEM)] * 2
        + [pl.BlockSpec((sites, epochs // STEPS), lambda i: (0, i)), pl.BlockSpec((sites, basis), lambda i: (0, 0))],
        out_specs=pl.BlockSpec((devices // STEPS, sites, span + basis), lambda i: (i, 0, 0)),
    )
    got = lax.all_to_all(sent, plane, 0, 0, tiled=True)
    own = lax.dynamic_slice_in_dim(decay, lax.axis_index(col) * share, share, 1)
    decays = lax.ppermute(own, planes + col, turn)
    persist = lax.dynamic_slice_in_dim(persistence, lax.axis_index("zh") * share, share, 0)[None]
    got, decays, persist = lax.optimization_barrier((got, decays, persist))

    partial = call(drive_kernel, "drive", shape((blocks, parts, slab, share), bf16), got)
    summed = lax.all_to_all(partial.reshape(blocks * parts, slab, share), planes, 0, 0, tiled=True)
    summed, loadings = lax.optimization_barrier((summed, loadings))
    square = shape((slab, share), f32)
    smooth, entry, product, summary = call(
        scan_kernel, "scan", (square, square, square, shape((slabs, 8, share), f32)), summed, decays, persist,
        scratch=[pltpu.VMEM((slab, share), f32)],
    )
    summaries = lax.all_to_all(summary, line, 0, 0, tiled=True)
    smoothed, rounded = call(
        finish_kernel, "finish", (square, shape((share, slab), bf16)),
        lax.axis_index(line).astype(jnp.int32)[None], summaries, smooth, entry, product,
        scratch=[pltpu.VMEM((slabs, share), f32)] * 2, scalars=1,
    )

    every = lax.all_gather(rounded, planes, axis=0, tiled=False)
    every, smoothed = lax.optimization_barrier((every, smoothed))
    out = lax.ppermute(smoothed, planes + col, turn)
    predicted = call(
        predict_kernel, "predict", shape((devices, sites, span), bf16),
        loadings, every.reshape(blocks, parts, share, slab), grid=(STEPS,),
        in_specs=[
            pl.BlockSpec((devices * sites // STEPS, basis), lambda i: (i, 0)),
            pl.BlockSpec((blocks, parts, share, slab), lambda i: (0, 0, 0, 0)),
        ],
        out_specs=pl.BlockSpec((devices // STEPS, sites, span), lambda i: (i, 0, 0)),
    )
    back = lax.all_to_all(predicted, plane, 0, 0, tiled=True)
    return (out, back.transpose(1, 0, 2).reshape(sites, epochs))


def solution(mesh):
    fine = Mesh(mesh.devices.reshape(4, 8, 2, 4, 2), ("x", "zh", "zl", "y", "core"))
    tm, col = ("x", "zh", "zl"), ("y", "core")
    every = tm + col
    return jax.shard_map(
        per_device,
        mesh=fine,
        in_specs=(P(every, None), P(every), P(every), P(every, None), P(every, None), P(tm, None), P()),
        out_specs=(P(tm, col), P(every, None)),
        check_vma=False,
    )
```

time: 547 us -> 171 us (0.31)
  the two profiles are of different devices: /device:TPU:1 before, /device:TPU:16 now
where the time goes in v1:
time: 171 us
  starting transfers between devices  58.2 us (34%)
  waiting for transfers between devices  53.6 us (31%)
  blocking collectives  32.5 us (19%)
  between operations  14.2 us (8%)
  Pallas kernels  6.94 us (4%)
  local copies, waits for them, and re-layouts  5.21 us (3%)
    all_gather x1, waiting for transfers between devices, per_device(): loadings = lax.all_gather(site_loading, plane, axis=0, tiled=True)  33.3 us
    all_gather x1, blocking collectives, per_device(): every = lax.all_gather(rounded, planes, axis=0, tiled=False)  32.5 us
    ppermute x1, starting transfers between devices, per_device(): decays = lax.ppermute(own, planes + col, turn)  13.5 us
    all_to_all x1, starting transfers between devices, per_device(): lax.all_to_all(partial.reshape(blocks * parts, slab, share), planes, 0, 0...  12.9 us
    all_to_all x1, starting transfers between devices, per_device(): got = lax.all_to_all(sent, plane, 0, 0, tiled=True)  9.33 us
    ppermute x1, starting transfers between devices, per_device(): out = lax.ppermute(smoothed, planes + col, turn)  8.88 us
    ppermute x1, waiting for transfers between devices, per_device(): out = lax.ppermute(smoothed, planes + col, turn)  8.39 us
    all_to_all x1, waiting for transfers between devices, per_device(): summaries = lax.all_to_all(summary, line, 0, 0, tiled=True)  7.75 us
  transfers between devices with their start and end apart: 7, of which 4 were waited for; matrix products, arithmetic and copies ran while one was open for 0% of the time, Pallas kernels for 1%

profile of v1, /device:TPU:16, one launch (start us, length us, event | category | flops | bytes accessed | tf_op | source)
XLA Modules:
  0.0 170.6 jit_solution(1794590077453215625)
XLA Ops:
  7.2 0.0 copy-start
  7.2 0.0 copy-start.2
  7.2 1.0 copy-done.2
  8.2 0.0 copy-start.3
  8.2 0.8 copy-done.3
  8.9 0.0 copy-start.4
  8.9 0.7 copy-done.4
  9.6 0.0 copy-start.5
  9.6 0.7 copy-done.5
  10.3 2.2 %front.1 = bf16[32,16,1280]{2,1,0:T(8,128)(2,1)} custom-call(s32[16]{0:T(128)S(1)} %copy-done.4, s32[16]{0:T(128)S(1)} %copy-done.5, bf16[16,8192]{1,0:T(8,128)(2,1)S(1)} %copy-done.2, bf16[16,1024]{1,0:T(8,128)(2,1)S(1)} %copy-done.3), custom_call_target="tpu_custom_call" | custom-call | tf_op jit(solution)/shard_map/front/pallas_call | solution.py:139
  12.5 9.3 %all-to-all-start = ((bf16[32,16,1280]{2,1,0:T(8,128)(2,1)}), bf16[32,16,1280]{2,1,0:T(8,128)(2,1)S(1)}, u32[]{:S(2)}, u32[]{:S(2)}) async-start(bf16[32,16,1280]{2,1,0:T(8,128)(2,1)} %front.1), calls=%async_computation | async-start | bytes 2621440 | tf_op jit(solution)/shard_map/all_to_all | solution.py:174
  21.8 0.0 all-gather.3.cloned.1.call-start
  21.9 0.0 copy-done
  21.9 13.5 %collective-permute-start = (f32[128,128]{1,0:T(8,128)S(1)}, f32[128,128]{1,0:T(8,128)S(1)}, u32[]{:S(2)}, u32[]{:S(2)}) collective-permute-start(f32[128,128]{1,0:T(8,128)S(1)} %constant_dynamic-slice_fusion), channel_id=1, source_target_pairs={{0,0},{1,16},{2,32},{3,48},{4,64},{5,80},{6,96},{7,112},{8,8},{9,2... | collective-permute-start | bytes 196616 | tf_op jit(solution)/shard_map/ppermute | solution.py:176
  35.4 0.0 all-gather.3.cloned.1.call-update
  35.4 0.8 dynamic-slice_bitcast_fusion.persist_ref
  36.2 4.1 %collective-permute-done.decay_ref = f32[128,128]{1,0:T(8,128)S(1)} collective-permute-done((f32[128,128]{1,0:T(8,128)S(1)}, f32[128,128]{1,0:T(8,128)S(1)}, u32[]{:S(2)}, u32[]{:S(2)}) %collective-permute-start) | collective-permute-done | bytes 65568 | tf_op jit(solution)/shard_map/ppermute | solution.py:176
  40.3 0.0 all-to-all-done.got_ref
  40.3 1.3 drive.1
  41.5 12.9 %all-to-all-start.1 = ((bf16[16,128,128]{2,1,0:T(8,128)(2,1)}), bf16[16,128,128]{2,1,0:T(8,128)(2,1)S(1)}, u32[]{:S(2)}, u32[]{:S(2)}) async-start(bf16[16,128,128]{2,1,0:T(8,128)(2,1)} %bitcast.2), calls=%async_computation.1 | async-start | bytes 1048576 | tf_op jit(solution)/shard_map/all_to_all | solution.py:181
  54.5 33.3 %all-gather.3.cloned.1.call-done.loading_ref = bf16[512,1024]{1,0:T(8,128)(2,1)} async-done(((bf16[16,1024]{1,0:T(8,128)(2,1)}), bf16[512,1024]{1,0:T(8,128)(2,1)}) %all-gather.3.cloned.1.call-update) | async-done | bytes 1048592 | tf_op jit(solution)/shard_map/all_gather | solution.py:165
  87.8 0.0 copy-start.1
  87.8 0.0 all-to-all-done.1.parts_ref
  87.8 1.0 scan.1
  88.8 7.3 %all-to-all-start.2 = ((f32[64,8,128]{2,1,0:T(8,128)}), f32[64,8,128]{2,1,0:T(8,128)S(1)}, u32[]{:S(2)}, u32[]{:S(2)}) async-start(f32[64,8,128]{2,1,0:T(8,128)} %get-tuple-element.19), calls=%async_computation.2 | async-start | bytes 524288 | tf_op jit(solution)/shard_map/all_to_all | solution.py:188
  96.1 7.7 %all-to-all-done.2.slabs_ref = f32[64,8,128]{2,1,0:T(8,128)S(1)} async-done(((f32[64,8,128]{2,1,0:T(8,128)}), f32[64,8,128]{2,1,0:T(8,128)S(1)}, u32[]{:S(2)}, u32[]{:S(2)}) %all-to-all-start.2) | async-done | bytes 262176 | tf_op jit(solution)/shard_map/all_to_all | solution.py:188
  103.9 0.4 finish.1
  104.3 32.5 %all-gather = bf16[2048,128]{1,0:T(8,128)(2,1)S(1)} all-gather(bf16[128,128]{1,0:T(8,128)(2,1)S(1)} %get-tuple-element.23), channel_id=2, replica_groups=mesh['x'=4,'zh'=8,'zl'=2,'y'=4,'core'=2] {'zh','zl'}, dimensions={0}, use_global_device_ids=true | all-gather | bytes 557056 | tf_op jit(solution)/shard_map/all_gather | solution.py:195
  136.8 0.0 copy-done.1
  136.8 2.1 %predict.1 = bf16[32,16,256]{2,1,0:T(8,128)(2,1)} custom-call(bf16[512,1024]{1,0:T(8,128)(2,1)S(1)} %copy-done.1, bf16[8,2,128,128]{3,2,1,0:T(8,128)(2,1)S(1)} %bitcast.9), custom_call_target="tpu_custom_call" | custom-call | tf_op jit(solution)/shard_map/predict/pallas_call | solution.py:139
  139.0 6.2 %all-to-all-start.3 = ((bf16[32,16,256]{2,1,0:T(8,128)(2,1)}), bf16[32,16,256]{2,1,0:T(8,128)(2,1)S(1)}, u32[]{:S(2)}, u32[]{:S(2)}) async-start(bf16[32,16,256]{2,1,0:T(8,128)(2,1)} %predict.1), calls=%async_computation.3 | async-start | bytes 524288 | tf_op jit(solution)/shard_map/all_to_all | solution.py:207
  145.1 8.9 %collective-permute-start.1 = (f32[128,128]{1,0:T(8,128)S(1)}, f32[128,128]{1,0:T(8,128)S(1)}, u32[]{:S(2)}, u32[]{:S(2)}) collective-permute-start(f32[128,128]{1,0:T(8,128)S(1)} %get-tuple-element.25), channel_id=1, source_target_pairs={{0,0},{1,16},{2,32},{3,48},{4,64},{5,80},{6,96},{7,112},{8,8},{9,2... | collective-permute-start | bytes 196616 | tf_op jit(solution)/shard_map/ppermute | solution.py:197
  154.0 8.4 %collective-permute-done.1 = f32[128,128]{1,0:T(8,128)S(1)} collective-permute-done((f32[128,128]{1,0:T(8,128)S(1)}, f32[128,128]{1,0:T(8,128)S(1)}, u32[]{:S(2)}, u32[]{:S(2)}) %collective-permute-start.1) | collective-permute-done | bytes 65568 | tf_op jit(solution)/shard_map/ppermute | solution.py:197
  162.4 0.0 all-to-all-done.3
  162.4 0.7 copy.10
  163.1 0.6 copy.12
  (1 shorter events, 0.0 us)
Async XLA Ops:
  7.2 14.7 %copy-start = (f32[128,1024]{1,0:T(8,128)S(1)}, f32[128,1024]{1,0:T(8,128)}, u32[]{:S(2)}) copy-start(f32[128,1024]{1,0:T(8,128)} %param.12) | copy-start | bytes 1572868
  7.2 1.0 copy-start.2
  8.2 0.8 copy-start.3
  8.9 0.7 copy-start.4
  9.6 0.7 copy-start.5
  12.5 27.8 %all-to-all-start = ((bf16[32,16,1280]{2,1,0:T(8,128)(2,1)}), bf16[32,16,1280]{2,1,0:T(8,128)(2,1)S(1)}, u32[]{:S(2)}, u32[]{:S(2)}) async-start(bf16[32,16,1280]{2,1,0:T(8,128)(2,1)} %front.1), calls=%async_computation | async-start | bytes 2621440 | tf_op jit(solution)/shard_map/all_to_all | solution.py:174
  21.8 66.0 %all-gather.3.cloned.1.call-start = ((), (), s32[]{:S(2)}) async-start(), calls=%async_computation.4 | async-start | bytes 1081344 | tf_op jit(solution)/shard_map/all_gather | solution.py:165
  21.9 18.4 %collective-permute-start = (f32[128,128]{1,0:T(8,128)S(1)}, f32[128,128]{1,0:T(8,128)S(1)}, u32[]{:S(2)}, u32[]{:S(2)}) collective-permute-start(f32[128,128]{1,0:T(8,128)S(1)} %constant_dynamic-slice_fusion), channel_id=1, source_target_pairs={{0,0},{1,16},{2,32},{3,48},{4,64},{5,80},{6,96},{7,112},{8,8},{9,2... | collective-permute-start | bytes 196616 | tf_op jit(solution)/shard_map/ppermute | solution.py:176
  41.5 46.3 %all-to-all-start.1 = ((bf16[16,128,128]{2,1,0:T(8,128)(2,1)}), bf16[16,128,128]{2,1,0:T(8,128)(2,1)S(1)}, u32[]{:S(2)}, u32[]{:S(2)}) async-start(bf16[16,128,128]{2,1,0:T(8,128)(2,1)} %bitcast.2), calls=%async_computation.1 | async-start | bytes 1048576 | tf_op jit(solution)/shard_map/all_to_all | solution.py:181
  87.8 49.0 %copy-start.1 = (bf16[512,1024]{1,0:T(8,128)(2,1)S(1)}, bf16[512,1024]{1,0:T(8,128)(2,1)}, u32[]{:S(2)}) copy-start(bf16[512,1024]{1,0:T(8,128)(2,1)} %all-gather.3.cloned.1.call-done.loading_ref) | copy-start | bytes 3145732
  88.8 15.1 %all-to-all-start.2 = ((f32[64,8,128]{2,1,0:T(8,128)}), f32[64,8,128]{2,1,0:T(8,128)S(1)}, u32[]{:S(2)}, u32[]{:S(2)}) async-start(f32[64,8,128]{2,1,0:T(8,128)} %get-tuple-element.19), calls=%async_computation.2 | async-start | bytes 524288 | tf_op jit(solution)/shard_map/all_to_all | solution.py:188
  139.0 23.4 %all-to-all-start.3 = ((bf16[32,16,256]{2,1,0:T(8,128)(2,1)}), bf16[32,16,256]{2,1,0:T(8,128)(2,1)S(1)}, u32[]{:S(2)}, u32[]{:S(2)}) async-start(bf16[32,16,256]{2,1,0:T(8,128)(2,1)} %predict.1), calls=%async_computation.3 | async-start | bytes 524288 | tf_op jit(solution)/shard_map/all_to_all | solution.py:207
  145.1 17.3 %collective-permute-start.1 = (f32[128,128]{1,0:T(8,128)S(1)}, f32[128,128]{1,0:T(8,128)S(1)}, u32[]{:S(2)}, u32[]{:S(2)}) collective-permute-start(f32[128,128]{1,0:T(8,128)S(1)} %get-tuple-element.25), channel_id=1, source_target_pairs={{0,0},{1,16},{2,32},{3,48},{4,64},{5,80},{6,96},{7,112},{8,8},{9,2... | collective-permute-start | bytes 196616 | tf_op jit(solution)/shard_map/ppermute | solution.py:197
Sparse Core Ops, SparseCore 0:
  35.6 52.2 all-gather.2

commit v2 on v1

--- a/solution.py
+++ b/solution.py
@@ -9,21 +9,43 @@
 STEPS = 4
 
 
-def front_kernel(start_ref, count_ref, values_ref, gain_ref, out_ref):
-    devices, sites, width = out_ref.shape
-    span = width - gain_ref.shape[1]
-    first = pl.program_id(0) * devices
+def front_kernel(start_hbm, count_hbm, values_hbm, gain_hbm, out_hbm, start, count, values, gain, out, small, large, sent):
+    devices, sites, width = out.shape
+    span = width - gain.shape[1]
+    wide, each = values.shape[1] // STEPS, devices // STEPS
+    arriving = [
+        pltpu.make_async_copy(start_hbm, start, small.at[0]),
+        pltpu.make_async_copy(count_hbm, count, small.at[1]),
+        pltpu.make_async_copy(gain_hbm, gain, small.at[2]),
+    ]
+    chunks = []
+    for step in range(STEPS):
+        part = (slice(None), pl.ds(step * wide, wide))
+        chunks.append(pltpu.make_async_copy(values_hbm.at[part], values.at[part], large.at[step]))
+    for copy in arriving + chunks:
+        copy.start()
+    for copy in arriving:
+        copy.wait()
     site = lax.broadcasted_iota(jnp.int32, (sites, span), 0)
-    start = end = jnp.zeros((sites, span), jnp.int32)
+    first = end = jnp.zeros((sites, span), jnp.int32)
     for s in range(sites):
-        start = jnp.where(site == s, start_ref[s], start)
-        end = jnp.where(site == s, start_ref[s] + count_ref[s], end)
-    epoch = lax.broadcasted_iota(jnp.int32, (sites, span), 1) + first * span
-    for to in range(devices):
-        values = values_ref[:, to * span:(to + 1) * span].astype(jnp.float32)
-        inside = (epoch + to * span >= start) & (epoch + to * span < end)
-        out_ref[to, :, :span] = jnp.where(inside, values, 0.0).astype(out_ref.dtype)
-        out_ref[to, :, span:] = gain_ref[...]
+        first = jnp.where(site == s, start[s], first)
+        end = jnp.where(site == s, start[s] + count[s], end)
+    epoch = lax.broadcasted_iota(jnp.int32, (sites, span), 1)
+    gains = gain[...]
+    leaving = []
+    for step in range(STEPS):
+        chunks[step].wait()
+        for to in range(step * each, (step + 1) * each):
+            own = values[:, to * span:(to + 1) * span].astype(jnp.float32)
+            inside = (epoch + to * span >= first) & (epoch + to * span < end)
+            out[to, :, :span] = jnp.where(inside, own, 0.0).astype(out.dtype)
+            out[to, :, span:] = gains
+        part = pl.ds(step * each, each)
+        leaving.append(pltpu.make_async_copy(out.at[part], out_hbm.at[part], sent.at[step]))
+        leaving[-1].start()
+    for copy in leaving:
+        copy.wait()
 
 
 def drive_kernel(got_ref, out_ref):
@@ -100,7 +122,7 @@
         summary_ref[to] = summary
 
 
-def finish_kernel(place_ref, slabs_ref, smooth_ref, entry_ref, product_ref, out_ref, rounded_ref, fwd, bwd):
+def finish_kernel(place_ref, slabs_ref, smooth_ref, entry_ref, product_ref, rounded_ref, fwd, bwd):
     count, _, width = slabs_ref.shape
 
     def of(at, what):
@@ -117,22 +139,26 @@
     place = place_ref[0]
     f_in, g_in = fwd[pl.ds(place, 1), :], bwd[pl.ds(place, 1), :]
     smoothed = smooth_ref[...] + entry_ref[...] * f_in + product_ref[...] * g_in
-    out_ref[...] = smoothed
     rounded_ref[...] = smoothed.T.astype(rounded_ref.dtype)
 
 
-def predict_kernel(loading_ref, rounded_ref, out_ref):
+def predict_kernel(where_ref, near_ref, far_ref, rounded_ref, out_ref, own_ref):
     blocks, parts, share, slab = rounded_ref.shape
-    devices, sites, _ = out_ref.shape
-    loadings = loading_ref[...]
-    for part in range(parts):
-        states = rounded_ref[:, part].reshape(blocks * share, slab)
-        predicted = jnp.dot(loadings, states, preferred_element_type=jnp.float32)
-        out_ref[:, :, part * slab:(part + 1) * slab] = predicted.astype(out_ref.dtype).reshape(devices, sites, slab)
-
-
-def call(kernel, name, out_shape, *args, scratch=(), scalars=0, **grid):
-    if not grid:
+    pairs, _, sites, _ = out_ref.shape
+    part, y, core = where_ref[0], where_ref[1], where_ref[2]
+    loadings = jnp.concatenate([near_ref[...], far_ref[...]], axis=0)
+    for at in range(parts):
+        states = rounded_ref[:, at].reshape(blocks * share, slab)
+        predicted = jnp.dot(loadings, states, preferred_element_type=jnp.float32).astype(out_ref.dtype)
+        predicted = predicted.reshape(2, pairs, sites, slab)
+        for other in range(2):
+            out_ref[:, core ^ other, :, at * slab:(at + 1) * slab] = predicted[other]
+    for other in range(own_ref.shape[1]):
+        own_ref[0, other] = rounded_ref[(y ^ pl.program_id(0)) * own_ref.shape[1] + (core ^ other), part]
+
+
+def call(kernel, name, out_shape, *args, scratch=(), scalars=0, vmem=32, **grid):
+    if "in_specs" not in grid:
         specs = [pl.BlockSpec(memory_space=pltpu.SMEM)] * scalars
         specs += [pl.BlockSpec(memory_space=pltpu.VMEM)] * (len(args) - scalars)
         grid = dict(in_specs=specs)
@@ -140,7 +166,7 @@
         kernel,
         out_shape=out_shape,
         scratch_shapes=list(scratch),
-        compiler_params=pltpu.CompilerParams(vmem_limit_bytes=32 << 20),
+        compiler_params=pltpu.CompilerParams(vmem_limit_bytes=vmem << 20),
         name=name,
         **grid,
     )(*args)
@@ -162,49 +188,69 @@
         for h in range(blocks) for l in range(parts) for c in range(nc)
     ]
 
-    loadings = lax.all_gather(site_loading, plane, axis=0, tiled=True)
-
+    hbm, smem = pl.BlockSpec(memory_space=pl.ANY), pltpu.SMEM
     sent = call(
         front_kernel, "front", shape((devices, sites, span + basis), bf16),
-        site_start, site_count, observations, site_gain, grid=(STEPS,),
-        in_specs=[pl.BlockSpec(memory_space=pltpu.SMEM)] * 2
-        + [pl.BlockSpec((sites, epochs // STEPS), lambda i: (0, i)), pl.BlockSpec((sites, basis), lambda i: (0, 0))],
-        out_specs=pl.BlockSpec((devices // STEPS, sites, span + basis), lambda i: (i, 0, 0)),
+        site_start, site_count, observations, site_gain, in_specs=[hbm] * 4, out_specs=hbm, vmem=60,
+        scratch=[
+            smem((sites,), jnp.int32), smem((sites,), jnp.int32),
+            pltpu.VMEM((sites, epochs), bf16), pltpu.VMEM((sites, basis), bf16),
+            pltpu.VMEM((devices, sites, span + basis), bf16),
+            pltpu.SemaphoreType.DMA((3,)), pltpu.SemaphoreType.DMA((STEPS,)), pltpu.SemaphoreType.DMA((STEPS,)),
+        ],
     )
     got = lax.all_to_all(sent, plane, 0, 0, tiled=True)
     own = lax.dynamic_slice_in_dim(decay, lax.axis_index(col) * share, share, 1)
     decays = lax.ppermute(own, planes + col, turn)
     persist = lax.dynamic_slice_in_dim(persistence, lax.axis_index("zh") * share, share, 0)[None]
     got, decays, persist = lax.optimization_barrier((got, decays, persist))
+    loadings, got = lax.optimization_barrier((site_loading, got))
+    near = lax.all_gather(loadings, ("x", "y"), axis=0, tiled=True)
 
     partial = call(drive_kernel, "drive", shape((blocks, parts, slab, share), bf16), got)
     summed = lax.all_to_all(partial.reshape(blocks * parts, slab, share), planes, 0, 0, tiled=True)
-    summed, loadings = lax.optimization_barrier((summed, loadings))
+    summed, near = lax.optimization_barrier((summed, near))
+    far = lax.ppermute(near, "core", [(0, 1), (1, 0)])
     square = shape((slab, share), f32)
     smooth, entry, product, summary = call(
         scan_kernel, "scan", (square, square, square, shape((slabs, 8, share), f32)), summed, decays, persist,
         scratch=[pltpu.VMEM((slab, share), f32)],
     )
     summaries = lax.all_to_all(summary, line, 0, 0, tiled=True)
-    smoothed, rounded = call(
-        finish_kernel, "finish", (square, shape((share, slab), bf16)),
+    rounded = call(
+        finish_kernel, "finish", shape((share, slab), bf16),
         lax.axis_index(line).astype(jnp.int32)[None], summaries, smooth, entry, product,
         scratch=[pltpu.VMEM((slabs, share), f32)] * 2, scalars=1,
     )
 
     every = lax.all_gather(rounded, planes, axis=0, tiled=False)
-    every, smoothed = lax.optimization_barrier((every, smoothed))
-    out = lax.ppermute(smoothed, planes + col, turn)
-    predicted = call(
-        predict_kernel, "predict", shape((devices, sites, span), bf16),
-        loadings, every.reshape(blocks, parts, share, slab), grid=(STEPS,),
+    ny, cores = lax.axis_size("y"), lax.axis_size("core")
+    y, core = lax.axis_index("y"), lax.axis_index("core")
+    rows = near.shape[0] // ny
+    predicted, own = call(
+        predict_kernel, "predict",
+        (shape((devices // cores, cores, sites, span), bf16), shape((ny, cores, share, slab), bf16)),
+        jnp.stack([lax.axis_index("zl"), y, core]).astype(jnp.int32), near, far,
+        every.reshape(blocks, parts, share, slab), grid=(ny,),
         in_specs=[
-            pl.BlockSpec((devices * sites // STEPS, basis), lambda i: (i, 0)),
+            pl.BlockSpec(memory_space=smem),
+            pl.BlockSpec((rows, basis), lambda i: (i, 0)),
+            pl.BlockSpec((rows, basis), lambda i: (i, 0)),
             pl.BlockSpec((blocks, parts, share, slab), lambda i: (0, 0, 0, 0)),
         ],
-        out_specs=pl.BlockSpec((devices // STEPS, sites, span), lambda i: (i, 0, 0)),
-    )
-    back = lax.all_to_all(predicted, plane, 0, 0, tiled=True)
+        out_specs=(
+            pl.BlockSpec((devices // cores // ny, cores, sites, span), lambda i: (i, 0, 0, 0)),
+            pl.BlockSpec((1, cores, share, slab), lambda i: (i, 0, 0, 0)),
+        ),
+    )
+    back = lax.all_to_all(predicted.reshape(devices, sites, span), plane, 0, 0, tiled=True)
+    holder = lax.axis_index("zh")
+    got = own[0]
+    for step in range(1, ny):
+        moved = lax.ppermute(own[step], "y", [(i, i ^ step) for i in range(ny)])
+        got = jnp.where((holder // cores) ^ y == step, moved, got)
+    swapped = lax.ppermute(got[1], "core", [(0, 1), (1, 0)])
+    out = jnp.where(holder % cores == core, got[0], swapped).T.astype(f32)
     return (out, back.transpose(1, 0, 2).reshape(sites, epochs))
 
 

time: 171 us -> 161 us (0.942)
  the two profiles are of different devices: /device:TPU:16 before, /device:TPU:1 now
where the time goes in v2:
time: 161 us; the launch traced here: 160 us
  starting transfers between devices  68.2 us (42%)
  blocking collectives  44.3 us (28%)
  waiting for transfers between devices  36.8 us (23%)
  Pallas kernels  7.43 us (5%)
  local copies, waits for them, and re-layouts  2.26 us (1%)
    all_gather x1, blocking collectives, per_device(): every = lax.all_gather(rounded, planes, axis=0, tiled=False)  25.3 us
    all_gather x1, blocking collectives, per_device(): near = lax.all_gather(loadings, ('x', 'y'), axis=0, tiled=True)  19 us
    all_to_all x1, starting transfers between devices, per_device(): lax.all_to_all(partial.reshape(blocks * parts, slab, share), planes, 0, 0...  13.8 us
    all_to_all x1, starting transfers between devices, per_device(): summaries = lax.all_to_all(summary, line, 0, 0, tiled=True)  13.6 us
    all_to_all x1, waiting for transfers between devices, per_device(): got = lax.all_to_all(sent, plane, 0, 0, tiled=True)  12.4 us
    ppermute x1, starting transfers between devices, per_device(): swapped = lax.ppermute(got[1], 'core', [(0, 1), (1, 0)])  11 us
    all_to_all x1, starting transfers between devices, per_device(): got = lax.all_to_all(sent, plane, 0, 0, tiled=True)  10.5 us
    ppermute x3, starting transfers between devices, per_device(): moved = lax.ppermute(own[step], 'y', [(i, i ^ step) for i in range(ny)])  8.98 us
  transfers between devices with their start and end apart: 10, of which 7 were waited for; matrix products, arithmetic and copies ran while one was open for 1% of the time, Pallas kernels for 0%

profile of v2, /device:TPU:1, one launch (start us, length us, event | category | flops | bytes accessed | tf_op | source)
XLA Modules:
  0.0 159.9 jit_solution(5451076859219627331)
XLA Ops:
  0.6 0.0 copy-start
  0.6 2.1 %front.1 = bf16[32,16,1280]{2,1,0:T(8,128)(2,1)} custom-call(s32[16]{0:T(128)} %start_hbm.1, s32[16]{0:T(128)} %count_hbm.1, bf16[16,8192]{1,0:T(8,128)(2,1)} %values_hbm.1, bf16[16,1024]{1,0:T(8,128)(2,1)} %gain_hbm.1), custom_call_target="tpu_custom_call" | custom-call | tf_op jit(solution)/shard_map/front/pallas_call | solution.py:165
  2.8 10.5 %all-to-all-start = ((bf16[32,16,1280]{2,1,0:T(8,128)(2,1)}), bf16[32,16,1280]{2,1,0:T(8,128)(2,1)S(1)}, u32[]{:S(2)}, u32[]{:S(2)}) async-start(bf16[32,16,1280]{2,1,0:T(8,128)(2,1)} %front.1), calls=%async_computation | async-start | bytes 2621440 | tf_op jit(solution)/shard_map/all_to_all | solution.py:202
  13.3 0.0 copy-done
  13.3 3.1 %collective-permute-start = (f32[128,128]{1,0:T(8,128)S(1)}, f32[128,128]{1,0:T(8,128)S(1)}, u32[]{:S(2)}, u32[]{:S(2)}) collective-permute-start(f32[128,128]{1,0:T(8,128)S(1)} %constant_dynamic-slice_fusion), channel_id=1, source_target_pairs={{0,0},{1,16},{2,32},{3,48},{4,64},{5,80},{6,96},{7,112},{8,8},{9,2... | collective-permute-start | bytes 196616 | tf_op jit(solution)/shard_map/ppermute | solution.py:204
  16.5 0.8 dynamic-slice_bitcast_fusion.persist_ref
  17.2 0.0 copy-start.1
  17.2 3.5 %collective-permute-done.decay_ref = f32[128,128]{1,0:T(8,128)S(1)} collective-permute-done((f32[128,128]{1,0:T(8,128)S(1)}, f32[128,128]{1,0:T(8,128)S(1)}, u32[]{:S(2)}, u32[]{:S(2)}) %collective-permute-start) | collective-permute-done | bytes 65568 | tf_op jit(solution)/shard_map/ppermute | solution.py:204
  20.8 12.4 %all-to-all-done.got_ref = bf16[32,16,1280]{2,1,0:T(8,128)(2,1)S(1)} async-done(((bf16[32,16,1280]{2,1,0:T(8,128)(2,1)}), bf16[32,16,1280]{2,1,0:T(8,128)(2,1)S(1)}, u32[]{:S(2)}, u32[]{:S(2)}) %all-to-all-start) | async-done | bytes 1310752 | tf_op jit(solution)/shard_map/all_to_all | solution.py:202
  33.2 1.3 drive.1
  34.4 13.8 %all-to-all-start.1 = ((bf16[16,128,128]{2,1,0:T(8,128)(2,1)}), bf16[16,128,128]{2,1,0:T(8,128)(2,1)S(1)}, u32[]{:S(2)}, u32[]{:S(2)}) async-start(bf16[16,128,128]{2,1,0:T(8,128)(2,1)} %bitcast.4), calls=%async_computation.1 | async-start | bytes 1048576 | tf_op jit(solution)/shard_map/all_to_all | solution.py:211
  48.2 0.0 copy-done.1
  48.2 19.0 %all_gather.9.near_ref = bf16[256,1024]{1,0:T(8,128)(2,1)S(1)} all-gather(bf16[16,1024]{1,0:T(8,128)(2,1)S(1)} %copy-done.1), channel_id=1, replica_groups=mesh['x'=4,'zh'=8,'zl'=2,'y'=4,'core'=2] {'x','y'}, dimensions={0}, use_global_device_ids=true | all-gather | bytes 557056 | tf_op jit(solution)/shard_map/all_gather | solution.py:208
  67.2 3.9 %all-to-all-done.1.parts_ref = bf16[16,128,128]{2,1,0:T(8,128)(2,1)S(1)} async-done(((bf16[16,128,128]{2,1,0:T(8,128)(2,1)}), bf16[16,128,128]{2,1,0:T(8,128)(2,1)S(1)}, u32[]{:S(2)}, u32[]{:S(2)}) %all-to-all-start.1) | async-done | bytes 524320 | tf_op jit(solution)/shard_map/all_to_all | solution.py:211
  71.1 1.0 scan.1
  72.0 13.6 %all-to-all-start.2 = ((f32[64,8,128]{2,1,0:T(8,128)}), f32[64,8,128]{2,1,0:T(8,128)S(1)}, u32[]{:S(2)}, u32[]{:S(2)}) async-start(f32[64,8,128]{2,1,0:T(8,128)} %get-tuple-element.22), calls=%async_computation.2 | async-start | bytes 524288 | tf_op jit(solution)/shard_map/all_to_all | solution.py:219
  85.6 2.4 %collective-permute-start.1 = (bf16[256,1024]{1,0:T(8,128)(2,1)S(1)}, bf16[256,1024]{1,0:T(8,128)(2,1)S(1)}, u32[]{:S(2)}, u32[]{:S(2)}) collective-permute-start(bf16[256,1024]{1,0:T(8,128)(2,1)S(1)} %all_gather.9.near_ref), channel_id=1, source_target_pairs={{0,1},{1,0},{2,3},{3,2},{4,5},{5,4},{6,7},{7,6},{8,9},{9,8},{10,11... | collective-permute-start | bytes 1572872 | tf_op jit(solution)/shard_map/ppermute | solution.py:213
  88.0 0.1 pad_add_fusion.where_ref
  88.0 7.2 %all-to-all-done.2.slabs_ref = f32[64,8,128]{2,1,0:T(8,128)S(1)} async-done(((f32[64,8,128]{2,1,0:T(8,128)}), f32[64,8,128]{2,1,0:T(8,128)S(1)}, u32[]{:S(2)}, u32[]{:S(2)}) %all-to-all-start.2) | async-done | bytes 262176 | tf_op jit(solution)/shard_map/all_to_all | solution.py:219
  95.2 0.4 finish.1
  95.6 25.3 %all-gather = bf16[2048,128]{1,0:T(8,128)(2,1)S(1)} all-gather(bf16[128,128]{1,0:T(8,128)(2,1)S(1)} %finish.1), channel_id=2, replica_groups=mesh['x'=4,'zh'=8,'zl'=2,'y'=4,'core'=2] {'zh','zl'}, dimensions={0}, use_global_device_ids=true | all-gather | bytes 557056 | tf_op jit(solution)/shard_map/all_gather | solution.py:226
  120.9 0.0 collective-permute-done.1.far_ref
  120.9 2.7 %predict.1 = (bf16[16,2,16,256]{3,2,1,0:T(8,128)(2,1)}, bf16[4,2,128,128]{3,2,1,0:T(8,128)(2,1)S(1)}) custom-call(s32[3]{0:T(128)S(1)} %pad_add_fusion.where_ref, bf16[256,1024]{1,0:T(8,128)(2,1)S(1)} %all_gather.9.near_ref, bf16[256,1024]{1,0:T(8,128)(2,1)S(1)} %collective-permute-done.1.far_ref, bf16[8,2,128,128]{3,2,1,0:T(8,128)(2,1)S(1)} %bitcast.34), custom_call_target="tpu_custom_call" | custom-call | tf_op jit(solution)/shard_map/predict/pallas_call | solution.py:165
  123.6 2.8 %collective-permute-start.2 = (bf16[2,128,128]{2,1,0:T(8,128)(2,1)S(1)}, bf16[2,128,128]{2,1,0:T(8,128)(2,1)S(1)}, u32[]{:S(2)}, u32[]{:S(2)}) collective-permute-start(bf16[2,128,128]{2,1,0:T(8,128)(2,1)S(1)} %get-tuple-element.32), channel_id=1, source_target_pairs={{0,6},{2,4},{4,2},{6,0},{1,7},{3,5},{5,3},{7,1},{8,14},{10,12},{12... | collective-permute-start | bytes 196616 | tf_op jit(solution)/shard_map/ppermute | solution.py:250
  126.4 2.8 %collective-permute-start.3 = (bf16[2,128,128]{2,1,0:T(8,128)(2,1)S(1)}, bf16[2,128,128]{2,1,0:T(8,128)(2,1)S(1)}, u32[]{:S(2)}, u32[]{:S(2)}) collective-permute-start(bf16[2,128,128]{2,1,0:T(8,128)(2,1)S(1)} %get-tuple-element.31), channel_id=1, source_target_pairs={{0,4},{2,6},{4,0},{6,2},{1,5},{3,7},{5,1},{7,3},{8,12},{10,14},{12... | collective-permute-start | bytes 196616 | tf_op jit(solution)/shard_map/ppermute | solution.py:250
  129.2 3.4 %collective-permute-start.4 = (bf16[2,128,128]{2,1,0:T(8,128)(2,1)S(1)}, bf16[2,128,128]{2,1,0:T(8,128)(2,1)S(1)}, u32[]{:S(2)}, u32[]{:S(2)}) collective-permute-start(bf16[2,128,128]{2,1,0:T(8,128)(2,1)S(1)} %get-tuple-element.30), channel_id=1, source_target_pairs={{0,2},{2,0},{4,6},{6,4},{1,3},{3,1},{5,7},{7,5},{8,10},{10,8},{12,... | collective-permute-start | bytes 196616 | tf_op jit(solution)/shard_map/ppermute | solution.py:250
  132.6 0.0 collective-permute-done.2
  132.6 0.3 collective-permute-done.3
  132.9 1.3 collective-permute-done.4
  134.3 11.0 %collective-permute-start.5 = (bf16[128,128]{1,0:T(8,128)(2,1)S(1)}, bf16[128,128]{1,0:T(8,128)(2,1)S(1)}, u32[]{:S(2)}, u32[]{:S(2)}) collective-permute-start(bf16[128,128]{1,0:T(8,128)(2,1)S(1)} %slice_bitcast_fusion.3), channel_id=1, source_target_pairs={{0,1},{1,0},{2,3},{3,2},{4,5},{5,4},{6,7},{7,6},{8,9},{9,8},{10,11... | collective-permute-start | bytes 98312 | tf_op jit(solution)/shard_map/ppermute | solution.py:252
  145.3 4.9 %all-to-all-start.3 = ((bf16[32,16,256]{2,1,0:T(8,128)(2,1)}), bf16[32,16,256]{2,1,0:T(8,128)(2,1)S(1)}, u32[]{:S(2)}, u32[]{:S(2)}) async-start(bf16[32,16,256]{2,1,0:T(8,128)(2,1)} %bitcast.14), calls=%async_computation.3 | async-start | bytes 524288 | tf_op jit(solution)/shard_map/all_to_all | solution.py:246
  150.2 0.0 collective-permute-done.5
  150.3 0.7 copy.10
  151.0 8.2 %all-to-all-done.3 = bf16[32,16,256]{2,1,0:T(8,128)(2,1)S(1)} async-done(((bf16[32,16,256]{2,1,0:T(8,128)(2,1)}), bf16[32,16,256]{2,1,0:T(8,128)(2,1)S(1)}, u32[]{:S(2)}, u32[]{:S(2)}) %all-to-all-start.3) | async-done | bytes 262176 | tf_op jit(solution)/shard_map/all_to_all | solution.py:246
  159.2 0.7 copy.11
  (5 shorter events, 0.1 us)
Async XLA Ops:
  0.6 12.7 %copy-start = (f32[128,1024]{1,0:T(8,128)S(1)}, f32[128,1024]{1,0:T(8,128)}, u32[]{:S(2)}) copy-start(f32[128,1024]{1,0:T(8,128)} %param.12) | copy-start | bytes 1572868
  2.8 30.4 %all-to-all-start = ((bf16[32,16,1280]{2,1,0:T(8,128)(2,1)}), bf16[32,16,1280]{2,1,0:T(8,128)(2,1)S(1)}, u32[]{:S(2)}, u32[]{:S(2)}) async-start(bf16[32,16,1280]{2,1,0:T(8,128)(2,1)} %front.1), calls=%async_computation | async-start | bytes 2621440 | tf_op jit(solution)/shard_map/all_to_all | solution.py:202
  13.3 7.4 %collective-permute-start = (f32[128,128]{1,0:T(8,128)S(1)}, f32[128,128]{1,0:T(8,128)S(1)}, u32[]{:S(2)}, u32[]{:S(2)}) collective-permute-start(f32[128,128]{1,0:T(8,128)S(1)} %constant_dynamic-slice_fusion), channel_id=1, source_target_pairs={{0,0},{1,16},{2,32},{3,48},{4,64},{5,80},{6,96},{7,112},{8,8},{9,2... | collective-permute-start | bytes 196616 | tf_op jit(solution)/shard_map/ppermute | solution.py:204
  17.2 31.0 %copy-start.1 = (bf16[16,1024]{1,0:T(8,128)(2,1)S(1)}, bf16[16,1024]{1,0:T(8,128)(2,1)}, u32[]{:S(2)}) copy-start(bf16[16,1024]{1,0:T(8,128)(2,1)} %param.11) | copy-start | bytes 98308
  34.4 36.6 %all-to-all-start.1 = ((bf16[16,128,128]{2,1,0:T(8,128)(2,1)}), bf16[16,128,128]{2,1,0:T(8,128)(2,1)S(1)}, u32[]{:S(2)}, u32[]{:S(2)}) async-start(bf16[16,128,128]{2,1,0:T(8,128)(2,1)} %bitcast.4), calls=%async_computation.1 | async-start | bytes 1048576 | tf_op jit(solution)/shard_map/all_to_all | solution.py:211
  72.0 23.2 %all-to-all-start.2 = ((f32[64,8,128]{2,1,0:T(8,128)}), f32[64,8,128]{2,1,0:T(8,128)S(1)}, u32[]{:S(2)}, u32[]{:S(2)}) async-start(f32[64,8,128]{2,1,0:T(8,128)} %get-tuple-element.22), calls=%async_computation.2 | async-start | bytes 524288 | tf_op jit(solution)/shard_map/all_to_all | solution.py:219
  85.6 35.3 %collective-permute-start.1 = (bf16[256,1024]{1,0:T(8,128)(2,1)S(1)}, bf16[256,1024]{1,0:T(8,128)(2,1)S(1)}, u32[]{:S(2)}, u32[]{:S(2)}) collective-permute-start(bf16[256,1024]{1,0:T(8,128)(2,1)S(1)} %all_gather.9.near_ref), channel_id=1, source_target_pairs={{0,1},{1,0},{2,3},{3,2},{4,5},{5,4},{6,7},{7,6},{8,9},{9,8},{10,11... | collective-permute-start | bytes 1572872 | tf_op jit(solution)/shard_map/ppermute | solution.py:213
  123.6 9.0 %collective-permute-start.2 = (bf16[2,128,128]{2,1,0:T(8,128)(2,1)S(1)}, bf16[2,128,128]{2,1,0:T(8,128)(2,1)S(1)}, u32[]{:S(2)}, u32[]{:S(2)}) collective-permute-start(bf16[2,128,128]{2,1,0:T(8,128)(2,1)S(1)} %get-tuple-element.32), channel_id=1, source_target_pairs={{0,6},{2,4},{4,2},{6,0},{1,7},{3,5},{5,3},{7,1},{8,14},{10,12},{12... | collective-permute-start | bytes 196616 | tf_op jit(solution)/shard_map/ppermute | solution.py:250
  126.4 6.5 %collective-permute-start.3 = (bf16[2,128,128]{2,1,0:T(8,128)(2,1)S(1)}, bf16[2,128,128]{2,1,0:T(8,128)(2,1)S(1)}, u32[]{:S(2)}, u32[]{:S(2)}) collective-permute-start(bf16[2,128,128]{2,1,0:T(8,128)(2,1)S(1)} %get-tuple-element.31), channel_id=1, source_target_pairs={{0,4},{2,6},{4,0},{6,2},{1,5},{3,7},{5,1},{7,3},{8,12},{10,14},{12... | collective-permute-start | bytes 196616 | tf_op jit(solution)/shard_map/ppermute | solution.py:250
  129.2 5.0 %collective-permute-start.4 = (bf16[2,128,128]{2,1,0:T(8,128)(2,1)S(1)}, bf16[2,128,128]{2,1,0:T(8,128)(2,1)S(1)}, u32[]{:S(2)}, u32[]{:S(2)}) collective-permute-start(bf16[2,128,128]{2,1,0:T(8,128)(2,1)S(1)} %get-tuple-element.30), channel_id=1, source_target_pairs={{0,2},{2,0},{4,6},{6,4},{1,3},{3,1},{5,7},{7,5},{8,10},{10,8},{12,... | collective-permute-start | bytes 196616 | tf_op jit(solution)/shard_map/ppermute | solution.py:250
  134.3 16.0 %collective-permute-start.5 = (bf16[128,128]{1,0:T(8,128)(2,1)S(1)}, bf16[128,128]{1,0:T(8,128)(2,1)S(1)}, u32[]{:S(2)}, u32[]{:S(2)}) collective-permute-start(bf16[128,128]{1,0:T(8,128)(2,1)S(1)} %slice_bitcast_fusion.3), channel_id=1, source_target_pairs={{0,1},{1,0},{2,3},{3,2},{4,5},{5,4},{6,7},{7,6},{8,9},{9,8},{10,11... | collective-permute-start | bytes 98312 | tf_op jit(solution)/shard_map/ppermute | solution.py:252
  145.3 13.9 %all-to-all-start.3 = ((bf16[32,16,256]{2,1,0:T(8,128)(2,1)}), bf16[32,16,256]{2,1,0:T(8,128)(2,1)S(1)}, u32[]{:S(2)}, u32[]{:S(2)}) async-start(bf16[32,16,256]{2,1,0:T(8,128)(2,1)} %bitcast.14), calls=%async_computation.3 | async-start | bytes 524288 | tf_op jit(solution)/shard_map/all_to_all | solution.py:246

commit v3 on v2

--- a/solution.py
+++ b/solution.py
@@ -142,19 +142,20 @@
     rounded_ref[...] = smoothed.T.astype(rounded_ref.dtype)
 
 
-def predict_kernel(where_ref, near_ref, far_ref, rounded_ref, out_ref, own_ref):
-    blocks, parts, share, slab = rounded_ref.shape
+def predict_kernel(where_ref, near_ref, far_ref, mine_ref, pair_ref, out_ref):
+    blocks, share, slab = mine_ref.shape
     pairs, _, sites, _ = out_ref.shape
-    part, y, core = where_ref[0], where_ref[1], where_ref[2]
+    part, core = where_ref[0], where_ref[1]
     loadings = jnp.concatenate([near_ref[...], far_ref[...]], axis=0)
-    for at in range(parts):
-        states = rounded_ref[:, at].reshape(blocks * share, slab)
-        predicted = jnp.dot(loadings, states, preferred_element_type=jnp.float32).astype(out_ref.dtype)
-        predicted = predicted.reshape(2, pairs, sites, slab)
+    predicted = []
+    for ref in (mine_ref, pair_ref):
+        states = ref[...].reshape(blocks * share, slab)
+        predicted.append(jnp.dot(loadings, states, preferred_element_type=jnp.float32))
+    mine, pair = predicted
+    for at in range(2):
+        chosen = jnp.where(part == at, mine, pair).astype(out_ref.dtype).reshape(2, pairs, sites, slab)
         for other in range(2):
-            out_ref[:, core ^ other, :, at * slab:(at + 1) * slab] = predicted[other]
-    for other in range(own_ref.shape[1]):
-        own_ref[0, other] = rounded_ref[(y ^ pl.program_id(0)) * own_ref.shape[1] + (core ^ other), part]
+            out_ref[:, core ^ other, :, at * slab:(at + 1) * slab] = chosen[other]
 
 
 def call(kernel, name, out_shape, *args, scratch=(), scalars=0, vmem=32, **grid):
@@ -223,34 +224,23 @@
         scratch=[pltpu.VMEM((slabs, share), f32)] * 2, scalars=1,
     )
 
-    every = lax.all_gather(rounded, planes, axis=0, tiled=False)
-    ny, cores = lax.axis_size("y"), lax.axis_size("core")
-    y, core = lax.axis_index("y"), lax.axis_index("core")
-    rows = near.shape[0] // ny
-    predicted, own = call(
-        predict_kernel, "predict",
-        (shape((devices // cores, cores, sites, span), bf16), shape((ny, cores, share, slab), bf16)),
-        jnp.stack([lax.axis_index("zl"), y, core]).astype(jnp.int32), near, far,
-        every.reshape(blocks, parts, share, slab), grid=(ny,),
-        in_specs=[
-            pl.BlockSpec(memory_space=smem),
-            pl.BlockSpec((rows, basis), lambda i: (i, 0)),
-            pl.BlockSpec((rows, basis), lambda i: (i, 0)),
-            pl.BlockSpec((blocks, parts, share, slab), lambda i: (0, 0, 0, 0)),
-        ],
-        out_specs=(
-            pl.BlockSpec((devices // cores // ny, cores, sites, span), lambda i: (i, 0, 0, 0)),
-            pl.BlockSpec((1, cores, share, slab), lambda i: (i, 0, 0, 0)),
-        ),
+    mine = lax.all_gather(rounded, "zh", axis=0, tiled=False)
+    pair = lax.ppermute(mine, "zl", [(0, 1), (1, 0)])
+    own = lax.all_to_all(mine, col, 0, 0, tiled=True)
+    pair, own = lax.optimization_barrier((pair, own))
+    out = lax.dynamic_index_in_dim(own, lax.axis_index("zh"), 0, False).T.astype(f32)
+
+    cores = lax.axis_size("core")
+    where = jnp.stack([lax.axis_index("zl"), lax.axis_index("core")]).astype(jnp.int32)
+    whole = pl.BlockSpec((blocks, share, slab), lambda i: (0, 0, 0))
+    rows = pl.BlockSpec((near.shape[0] // STEPS, basis), lambda i: (i, 0))
+    predicted = call(
+        predict_kernel, "predict", shape((devices // cores, cores, sites, span), bf16),
+        where, near, far, mine, pair, grid=(STEPS,),
+        in_specs=[pl.BlockSpec(memory_space=smem), rows, rows, whole, whole],
+        out_specs=pl.BlockSpec((devices // cores // STEPS, cores, sites, span), lambda i: (i, 0, 0, 0)),
     )
     back = lax.all_to_all(predicted.reshape(devices, sites, span), plane, 0, 0, tiled=True)
-    holder = lax.axis_index("zh")
-    got = own[0]
-    for step in range(1, ny):
-        moved = lax.ppermute(own[step], "y", [(i, i ^ step) for i in range(ny)])
-        got = jnp.where((holder // cores) ^ y == step, moved, got)
-    swapped = lax.ppermute(got[1], "core", [(0, 1), (1, 0)])
-    out = jnp.where(holder % cores == core, got[0], swapped).T.astype(f32)
     return (out, back.transpose(1, 0, 2).reshape(sites, epochs))
 
 

time: 161 us -> 158 us (0.981)
  starting transfers between devices: 68.2 us -> 60.1 us
  waiting for transfers between devices: 36.8 us -> 41.9 us
    ppermute x4 -> x1, starting transfers between devices: 20 us -> 1.98 us  [per_device(): pair = lax.ppermute(mine, 'zl', [(0, 1), (1, 0)])]
    all_to_all x0 -> x1, starting transfers between devices: none -> 10.2 us  [per_device(): own = lax.all_to_all(mine, col, 0, 0, tiled=True)]
    all_to_all x0 -> x1, waiting for transfers between devices: none -> 6.45 us  [per_device(): own = lax.all_to_all(mine, col, 0, 0, tiled=True)]
    ppermute x4 -> x1, waiting for transfers between devices: 1.61 us -> 0.01 us  [per_device(): pair = lax.ppermute(mine, 'zl', [(0, 1), (1, 0)])]
  transfers between devices with their start and end apart: 10 -> 8, of which waited for: 7 -> 6; matrix products, arithmetic and copies ran while one was open for 1% -> 1% of each run, Pallas kernels for 0% -> 0%
where the time goes in v3:
time: 158 us; the launch traced here: 157 us
  starting transfers between devices  60.1 us (38%)
  blocking collectives  44.1 us (28%)
  waiting for transfers between devices  41.9 us (27%)
  Pallas kernels  7.84 us (5%)
  local copies, waits for them, and re-layouts  2.24 us (1%)
    all_gather x1, blocking collectives, per_device(): mine = lax.all_gather(rounded, 'zh', axis=0, tiled=False)  25.2 us
    all_gather x1, blocking collectives, per_device(): near = lax.all_gather(loadings, ('x', 'y'), axis=0, tiled=True)  19 us
    all_to_all x1, starting transfers between devices, per_device(): lax.all_to_all(partial.reshape(blocks * parts, slab, share), planes, 0, 0...  13.8 us
    all_to_all x1, starting transfers between devices, per_device(): summaries = lax.all_to_all(summary, line, 0, 0, tiled=True)  13.5 us
    all_to_all x1, waiting for transfers between devices, per_device(): got = lax.all_to_all(sent, plane, 0, 0, tiled=True)  12.4 us
    all_to_all x1, starting transfers between devices, per_device(): got = lax.all_to_all(sent, plane, 0, 0, tiled=True)  10.5 us
    all_to_all x1, starting transfers between devices, per_device(): own = lax.all_to_all(mine, col, 0, 0, tiled=True)  10.2 us
    all_to_all x1, waiting for transfers between devices, per_device(): lax.all_to_all(predicted.reshape(devices, sites, span), plane, 0, 0, tile...  8.35 us
  transfers between devices with their start and end apart: 8, of which 6 were waited for; matrix products, arithmetic and copies ran while one was open for 1% of the time, Pallas kernels for 0%

profile of v3, /device:TPU:1, one launch (start us, length us, event | category | flops | bytes accessed | tf_op | source)
XLA Modules:
  0.0 157.0 jit_solution(2230565424111765125)
XLA Ops:
  0.6 0.0 copy-start
  0.6 2.1 %front.1 = bf16[32,16,1280]{2,1,0:T(8,128)(2,1)} custom-call(s32[16]{0:T(128)} %start_hbm.1, s32[16]{0:T(128)} %count_hbm.1, bf16[16,8192]{1,0:T(8,128)(2,1)} %values_hbm.1, bf16[16,1024]{1,0:T(8,128)(2,1)} %gain_hbm.1), custom_call_target="tpu_custom_call" | custom-call | tf_op jit(solution)/shard_map/front/pallas_call | solution.py:166
  2.8 10.5 %all-to-all-start = ((bf16[32,16,1280]{2,1,0:T(8,128)(2,1)}), bf16[32,16,1280]{2,1,0:T(8,128)(2,1)S(1)}, u32[]{:S(2)}, u32[]{:S(2)}) async-start(bf16[32,16,1280]{2,1,0:T(8,128)(2,1)} %front.1), calls=%async_computation | async-start | bytes 2621440 | tf_op jit(solution)/shard_map/all_to_all | solution.py:203
  13.3 0.0 copy-done
  13.3 3.1 %collective-permute-start = (f32[128,128]{1,0:T(8,128)S(1)}, f32[128,128]{1,0:T(8,128)S(1)}, u32[]{:S(2)}, u32[]{:S(2)}) collective-permute-start(f32[128,128]{1,0:T(8,128)S(1)} %constant_dynamic-slice_fusion), channel_id=1, source_target_pairs={{0,0},{1,16},{2,32},{3,48},{4,64},{5,80},{6,96},{7,112},{8,8},{9,2... | collective-permute-start | bytes 196616 | tf_op jit(solution)/shard_map/ppermute | solution.py:205
  16.5 0.8 dynamic-slice_bitcast_fusion.persist_ref
  17.2 0.0 copy-start.1
  17.2 3.5 %collective-permute-done.decay_ref = f32[128,128]{1,0:T(8,128)S(1)} collective-permute-done((f32[128,128]{1,0:T(8,128)S(1)}, f32[128,128]{1,0:T(8,128)S(1)}, u32[]{:S(2)}, u32[]{:S(2)}) %collective-permute-start) | collective-permute-done | bytes 65568 | tf_op jit(solution)/shard_map/ppermute | solution.py:205
  20.7 12.4 %all-to-all-done.got_ref = bf16[32,16,1280]{2,1,0:T(8,128)(2,1)S(1)} async-done(((bf16[32,16,1280]{2,1,0:T(8,128)(2,1)}), bf16[32,16,1280]{2,1,0:T(8,128)(2,1)S(1)}, u32[]{:S(2)}, u32[]{:S(2)}) %all-to-all-start) | async-done | bytes 1310752 | tf_op jit(solution)/shard_map/all_to_all | solution.py:203
  33.2 1.2 drive.1
  34.4 13.8 %all-to-all-start.1 = ((bf16[16,128,128]{2,1,0:T(8,128)(2,1)}), bf16[16,128,128]{2,1,0:T(8,128)(2,1)S(1)}, u32[]{:S(2)}, u32[]{:S(2)}) async-start(bf16[16,128,128]{2,1,0:T(8,128)(2,1)} %bitcast.2), calls=%async_computation.1 | async-start | bytes 1048576 | tf_op jit(solution)/shard_map/all_to_all | solution.py:212
  48.2 0.0 copy-done.1
  48.2 19.0 %all_gather.9.near_ref = bf16[256,1024]{1,0:T(8,128)(2,1)S(1)} all-gather(bf16[16,1024]{1,0:T(8,128)(2,1)S(1)} %copy-done.1), channel_id=1, replica_groups=mesh['x'=4,'zh'=8,'zl'=2,'y'=4,'core'=2] {'x','y'}, dimensions={0}, use_global_device_ids=true | all-gather | bytes 557056 | tf_op jit(solution)/shard_map/all_gather | solution.py:209
  67.1 3.9 %all-to-all-done.1.parts_ref = bf16[16,128,128]{2,1,0:T(8,128)(2,1)S(1)} async-done(((bf16[16,128,128]{2,1,0:T(8,128)(2,1)}), bf16[16,128,128]{2,1,0:T(8,128)(2,1)S(1)}, u32[]{:S(2)}, u32[]{:S(2)}) %all-to-all-start.1) | async-done | bytes 524320 | tf_op jit(solution)/shard_map/all_to_all | solution.py:212
  71.0 1.0 scan.1
  72.0 13.5 %all-to-all-start.2 = ((f32[64,8,128]{2,1,0:T(8,128)}), f32[64,8,128]{2,1,0:T(8,128)S(1)}, u32[]{:S(2)}, u32[]{:S(2)}) async-start(f32[64,8,128]{2,1,0:T(8,128)} %get-tuple-element.21), calls=%async_computation.2 | async-start | bytes 524288 | tf_op jit(solution)/shard_map/all_to_all | solution.py:220
  85.5 2.4 %collective-permute-start.2 = (bf16[256,1024]{1,0:T(8,128)(2,1)S(1)}, bf16[256,1024]{1,0:T(8,128)(2,1)S(1)}, u32[]{:S(2)}, u32[]{:S(2)}) collective-permute-start(bf16[256,1024]{1,0:T(8,128)(2,1)S(1)} %all_gather.9.near_ref), channel_id=1, source_target_pairs={{0,1},{1,0},{2,3},{3,2},{4,5},{5,4},{6,7},{7,6},{8,9},{9,8},{10,11... | collective-permute-start | bytes 1572872 | tf_op jit(solution)/shard_map/ppermute | solution.py:214
  87.9 7.2 %all-to-all-done.2.slabs_ref = f32[64,8,128]{2,1,0:T(8,128)S(1)} async-done(((f32[64,8,128]{2,1,0:T(8,128)}), f32[64,8,128]{2,1,0:T(8,128)S(1)}, u32[]{:S(2)}, u32[]{:S(2)}) %all-to-all-start.2) | async-done | bytes 262176 | tf_op jit(solution)/shard_map/all_to_all | solution.py:220
  95.2 0.4 finish.1
  95.5 25.2 %all-gather = bf16[1024,128]{1,0:T(8,128)(2,1)} all-gather(bf16[128,128]{1,0:T(8,128)(2,1)S(1)} %finish.1), channel_id=2, replica_groups=mesh['x'=4,'zh'=8,'zl'=2,'y'=4,'core'=2] {'zh'}, dimensions={0}, use_global_device_ids=true | all-gather | bytes 294912 | tf_op jit(solution)/shard_map/all_gather | solution.py:227
  120.7 2.0 %collective-permute-start.1 = (bf16[8,128,128]{2,1,0:T(8,128)(2,1)}, bf16[8,128,128]{2,1,0:T(8,128)(2,1)S(1)}, u32[]{:S(2)}, u32[]{:S(2)}) collective-permute-start(bf16[8,128,128]{2,1,0:T(8,128)(2,1)} %bitcast.3.mine_ref), channel_id=1, source_target_pairs={{0,8},{8,0},{1,9},{9,1},{2,10},{10,2},{3,11},{11,3},{4,12},{12,4},... | collective-permute-start | bytes 786440 | tf_op jit(solution)/shard_map/ppermute | solution.py:228
  122.7 10.2 %all-to-all-start.3 = ((bf16[8,128,128]{2,1,0:T(8,128)(2,1)}), bf16[8,128,128]{2,1,0:T(8,128)(2,1)S(1)}, u32[]{:S(2)}, u32[]{:S(2)}) async-start(bf16[8,128,128]{2,1,0:T(8,128)(2,1)} %bitcast.3.mine_ref), calls=%async_computation.3 | async-start | bytes 524288 | tf_op jit(solution)/shard_map/all_to_all | solution.py:229
  132.9 0.1 pad_add_fusion.where_ref
  133.0 6.4 %all-to-all-done.3 = bf16[8,128,128]{2,1,0:T(8,128)(2,1)S(1)} async-done(((bf16[8,128,128]{2,1,0:T(8,128)(2,1)}), bf16[8,128,128]{2,1,0:T(8,128)(2,1)S(1)}, u32[]{:S(2)}, u32[]{:S(2)}) %all-to-all-start.3) | async-done | bytes 262176 | tf_op jit(solution)/shard_map/all_to_all | solution.py:229
  139.5 0.0 collective-permute-done.1.pair_ref
  139.5 0.0 collective-permute-done.2.far_ref
  139.5 3.1 %predict.1 = bf16[16,2,16,256]{3,2,1,0:T(8,128)(2,1)} custom-call(s32[2]{0:T(128)S(1)} %pad_add_fusion.where_ref, bf16[256,1024]{1,0:T(8,128)(2,1)S(1)} %all_gather.9.near_ref, bf16[256,1024]{1,0:T(8,128)(2,1)S(1)} %collective-permute-done.2.far_ref, bf16[8,128,128]{2,1,0:T(8,128)(2,1)} %bitcast.3.mine_ref, ...), custom_call_target="tpu_custom_call" | custom-call | tf_op jit(solution)/shard_map/predict/pallas_call | solution.py:166
  142.6 4.6 %all-to-all-start.4 = ((bf16[32,16,256]{2,1,0:T(8,128)(2,1)}), bf16[32,16,256]{2,1,0:T(8,128)(2,1)S(1)}, u32[]{:S(2)}, u32[]{:S(2)}) async-start(bf16[32,16,256]{2,1,0:T(8,128)(2,1)} %bitcast.8), calls=%async_computation.4 | async-start | bytes 524288 | tf_op jit(solution)/shard_map/all_to_all | solution.py:243
  147.2 0.7 copy.10
  147.9 8.3 %all-to-all-done.4 = bf16[32,16,256]{2,1,0:T(8,128)(2,1)S(1)} async-done(((bf16[32,16,256]{2,1,0:T(8,128)(2,1)}), bf16[32,16,256]{2,1,0:T(8,128)(2,1)S(1)}, u32[]{:S(2)}, u32[]{:S(2)}) %all-to-all-start.4) | async-done | bytes 262176 | tf_op jit(solution)/shard_map/all_to_all | solution.py:243
  156.3 0.7 copy.11
  (2 shorter events, 0.0 us)
Async XLA Ops:
  0.6 12.7 %copy-start = (f32[128,1024]{1,0:T(8,128)S(1)}, f32[128,1024]{1,0:T(8,128)}, u32[]{:S(2)}) copy-start(f32[128,1024]{1,0:T(8,128)} %param.12) | copy-start | bytes 1572868
  2.8 30.4 %all-to-all-start = ((bf16[32,16,1280]{2,1,0:T(8,128)(2,1)}), bf16[32,16,1280]{2,1,0:T(8,128)(2,1)S(1)}, u32[]{:S(2)}, u32[]{:S(2)}) async-start(bf16[32,16,1280]{2,1,0:T(8,128)(2,1)} %front.1), calls=%async_computation | async-start | bytes 2621440 | tf_op jit(solution)/shard_map/all_to_all | solution.py:203
  13.3 7.4 %collective-permute-start = (f32[128,128]{1,0:T(8,128)S(1)}, f32[128,128]{1,0:T(8,128)S(1)}, u32[]{:S(2)}, u32[]{:S(2)}) collective-permute-start(f32[128,128]{1,0:T(8,128)S(1)} %constant_dynamic-slice_fusion), channel_id=1, source_target_pairs={{0,0},{1,16},{2,32},{3,48},{4,64},{5,80},{6,96},{7,112},{8,8},{9,2... | collective-permute-start | bytes 196616 | tf_op jit(solution)/shard_map/ppermute | solution.py:205
  17.2 30.9 %copy-start.1 = (bf16[16,1024]{1,0:T(8,128)(2,1)S(1)}, bf16[16,1024]{1,0:T(8,128)(2,1)}, u32[]{:S(2)}) copy-start(bf16[16,1024]{1,0:T(8,128)(2,1)} %param.11) | copy-start | bytes 98308
  34.4 36.6 %all-to-all-start.1 = ((bf16[16,128,128]{2,1,0:T(8,128)(2,1)}), bf16[16,128,128]{2,1,0:T(8,128)(2,1)S(1)}, u32[]{:S(2)}, u32[]{:S(2)}) async-start(bf16[16,128,128]{2,1,0:T(8,128)(2,1)} %bitcast.2), calls=%async_computation.1 | async-start | bytes 1048576 | tf_op jit(solution)/shard_map/all_to_all | solution.py:212
  72.0 23.2 %all-to-all-start.2 = ((f32[64,8,128]{2,1,0:T(8,128)}), f32[64,8,128]{2,1,0:T(8,128)S(1)}, u32[]{:S(2)}, u32[]{:S(2)}) async-start(f32[64,8,128]{2,1,0:T(8,128)} %get-tuple-element.21), calls=%async_computation.2 | async-start | bytes 524288 | tf_op jit(solution)/shard_map/all_to_all | solution.py:220
  85.5 53.9 %collective-permute-start.2 = (bf16[256,1024]{1,0:T(8,128)(2,1)S(1)}, bf16[256,1024]{1,0:T(8,128)(2,1)S(1)}, u32[]{:S(2)}, u32[]{:S(2)}) collective-permute-start(bf16[256,1024]{1,0:T(8,128)(2,1)S(1)} %all_gather.9.near_ref), channel_id=1, source_target_pairs={{0,1},{1,0},{2,3},{3,2},{4,5},{5,4},{6,7},{7,6},{8,9},{9,8},{10,11... | collective-permute-start | bytes 1572872 | tf_op jit(solution)/shard_map/ppermute | solution.py:214
  120.7 18.8 %collective-permute-start.1 = (bf16[8,128,128]{2,1,0:T(8,128)(2,1)}, bf16[8,128,128]{2,1,0:T(8,128)(2,1)S(1)}, u32[]{:S(2)}, u32[]{:S(2)}) collective-permute-start(bf16[8,128,128]{2,1,0:T(8,128)(2,1)} %bitcast.3.mine_ref), channel_id=1, source_target_pairs={{0,8},{8,0},{1,9},{9,1},{2,10},{10,2},{3,11},{11,3},{4,12},{12,4},... | collective-permute-start | bytes 786440 | tf_op jit(solution)/shard_map/ppermute | solution.py:228
  122.7 16.8 %all-to-all-start.3 = ((bf16[8,128,128]{2,1,0:T(8,128)(2,1)}), bf16[8,128,128]{2,1,0:T(8,128)(2,1)S(1)}, u32[]{:S(2)}, u32[]{:S(2)}) async-start(bf16[8,128,128]{2,1,0:T(8,128)(2,1)} %bitcast.3.mine_ref), calls=%async_computation.3 | async-start | bytes 524288 | tf_op jit(solution)/shard_map/all_to_all | solution.py:229
  142.6 13.7 %all-to-all-start.4 = ((bf16[32,16,256]{2,1,0:T(8,128)(2,1)}), bf16[32,16,256]{2,1,0:T(8,128)(2,1)S(1)}, u32[]{:S(2)}, u32[]{:S(2)}) async-start(bf16[32,16,256]{2,1,0:T(8,128)(2,1)} %bitcast.8), calls=%async_computation.4 | async-start | bytes 524288 | tf_op jit(solution)/shard_map/all_to_all | solution.py:243

commit v4 on v3

--- a/solution.py
+++ b/solution.py
@@ -48,17 +48,19 @@
         copy.wait()
 
 
-def drive_kernel(got_ref, out_ref):
-    sources, sites, _ = got_ref.shape
-    blocks, parts, slab, share = out_ref.shape
-    span = parts * slab
+def drive_kernel(part_ref, got_ref, keep_ref, give_ref):
+    sources, sites, width = got_ref.shape
+    blocks, slab, share = keep_ref.shape
+    span = width - blocks * share
     rows = got_ref[:, :, :span].reshape(sources * sites, span)
     gains = got_ref[:, :, span:].reshape(sources * sites, blocks * share)
     partial = lax.dot_general(rows, gains, (((0,), (0,)), ((), ())), preferred_element_type=jnp.float32)
-    partial = partial.astype(out_ref.dtype)
+    first = part_ref[0] == 0
+    keep = jnp.where(first, partial[:slab], partial[slab:])
+    give = jnp.where(first, partial[slab:], partial[:slab]).astype(give_ref.dtype)
     for block in range(blocks):
-        for part in range(parts):
-            out_ref[block, part] = partial[part * slab:(part + 1) * slab, block * share:(block + 1) * share]
+        keep_ref[block] = keep[:, block * share:(block + 1) * share]
+        give_ref[block] = give[:, block * share:(block + 1) * share]
 
 
 def shifted(value, by, fill):
@@ -139,23 +141,22 @@
     place = place_ref[0]
     f_in, g_in = fwd[pl.ds(place, 1), :], bwd[pl.ds(place, 1), :]
     smoothed = smooth_ref[...] + entry_ref[...] * f_in + product_ref[...] * g_in
-    rounded_ref[...] = smoothed.T.astype(rounded_ref.dtype)
+    rounded = smoothed.T.astype(rounded_ref.dtype)
+    for to in range(rounded_ref.shape[0]):
+        rounded_ref[to] = rounded
 
 
 def predict_kernel(where_ref, near_ref, far_ref, mine_ref, pair_ref, out_ref):
     blocks, share, slab = mine_ref.shape
-    pairs, _, sites, _ = out_ref.shape
-    part, core = where_ref[0], where_ref[1]
+    pairs, _, sites, span = out_ref.shape
+    first, core = where_ref[0] == 0, where_ref[1]
+    mine, pair = mine_ref[...].reshape(blocks * share, slab), pair_ref[...].reshape(blocks * share, slab)
+    states = jnp.concatenate([jnp.where(first, mine, pair), jnp.where(first, pair, mine)], axis=1)
     loadings = jnp.concatenate([near_ref[...], far_ref[...]], axis=0)
-    predicted = []
-    for ref in (mine_ref, pair_ref):
-        states = ref[...].reshape(blocks * share, slab)
-        predicted.append(jnp.dot(loadings, states, preferred_element_type=jnp.float32))
-    mine, pair = predicted
-    for at in range(2):
-        chosen = jnp.where(part == at, mine, pair).astype(out_ref.dtype).reshape(2, pairs, sites, slab)
-        for other in range(2):
-            out_ref[:, core ^ other, :, at * slab:(at + 1) * slab] = chosen[other]
+    predicted = jnp.dot(loadings, states, preferred_element_type=jnp.float32)
+    predicted = predicted.astype(out_ref.dtype).reshape(2, pairs, sites, span)
+    for other in range(2):
+        out_ref[:, core ^ other] = predicted[other]
 
 
 def call(kernel, name, out_shape, *args, scratch=(), scalars=0, vmem=32, **grid):
@@ -205,41 +206,44 @@
     decays = lax.ppermute(own, planes + col, turn)
     persist = lax.dynamic_slice_in_dim(persistence, lax.axis_index("zh") * share, share, 0)[None]
     got, decays, persist = lax.optimization_barrier((got, decays, persist))
-    loadings, got = lax.optimization_barrier((site_loading, got))
-    near = lax.all_gather(loadings, ("x", "y"), axis=0, tiled=True)
-
-    partial = call(drive_kernel, "drive", shape((blocks, parts, slab, share), bf16), got)
-    summed = lax.all_to_all(partial.reshape(blocks * parts, slab, share), planes, 0, 0, tiled=True)
+
+    part = lax.axis_index("zl").astype(jnp.int32)
+    both = (shape((blocks, slab, share), f32), shape((blocks, slab, share), bf16))
+    keep, give = call(drive_kernel, "drive", both, part[None], got, scalars=1)
+    taken = lax.ppermute(give, "zl", [(0, 1), (1, 0)])
+    taken, near = lax.optimization_barrier((taken, site_loading))
+    halves = (keep + taken.astype(f32)).astype(bf16)
+    summed = lax.all_to_all(halves, "zh", 0, 0, tiled=True)
+    near = lax.all_gather(near, "y", axis=0, tiled=True)
     summed, near = lax.optimization_barrier((summed, near))
-    far = lax.ppermute(near, "core", [(0, 1), (1, 0)])
     square = shape((slab, share), f32)
     smooth, entry, product, summary = call(
         scan_kernel, "scan", (square, square, square, shape((slabs, 8, share), f32)), summed, decays, persist,
         scratch=[pltpu.VMEM((slab, share), f32)],
     )
     summaries = lax.all_to_all(summary, line, 0, 0, tiled=True)
+    summaries, near = lax.optimization_barrier((summaries, near))
     rounded = call(
-        finish_kernel, "finish", shape((share, slab), bf16),
+        finish_kernel, "finish", shape((blocks, share, slab), bf16),
         lax.axis_index(line).astype(jnp.int32)[None], summaries, smooth, entry, product,
         scratch=[pltpu.VMEM((slabs, share), f32)] * 2, scalars=1,
     )
 
-    mine = lax.all_gather(rounded, "zh", axis=0, tiled=False)
+    mine = lax.all_to_all(rounded, "zh", 0, 0, tiled=True)
+    near = lax.all_gather(near, "x", axis=0, tiled=True)
+    mine, near = lax.optimization_barrier((mine, near))
+    far = lax.ppermute(near, "core", [(0, 1), (1, 0)])
     pair = lax.ppermute(mine, "zl", [(0, 1), (1, 0)])
     own = lax.all_to_all(mine, col, 0, 0, tiled=True)
-    pair, own = lax.optimization_barrier((pair, own))
-    out = lax.dynamic_index_in_dim(own, lax.axis_index("zh"), 0, False).T.astype(f32)
 
     cores = lax.axis_size("core")
-    where = jnp.stack([lax.axis_index("zl"), lax.axis_index("core")]).astype(jnp.int32)
-    whole = pl.BlockSpec((blocks, share, slab), lambda i: (0, 0, 0))
-    rows = pl.BlockSpec((near.shape[0] // STEPS, basis), lambda i: (i, 0))
+    where = jnp.stack([part, lax.axis_index("core").astype(jnp.int32)])
     predicted = call(
         predict_kernel, "predict", shape((devices // cores, cores, sites, span), bf16),
-        where, near, far, mine, pair, grid=(STEPS,),
-        in_specs=[pl.BlockSpec(memory_space=smem), rows, rows, whole, whole],
-        out_specs=pl.BlockSpec((devices // cores // STEPS, cores, sites, span), lambda i: (i, 0, 0, 0)),
-    )
+        where, near, far, mine, pair, scalars=1,
+    )
+    predicted, own = lax.optimization_barrier((predicted, own))
+    out = lax.dynamic_index_in_dim(own, lax.axis_index("zh"), 0, False).T.astype(f32)
     back = lax.all_to_all(predicted.reshape(devices, sites, span), plane, 0, 0, tiled=True)
     return (out, back.transpose(1, 0, 2).reshape(sites, epochs))
 

time: 158 us -> 152 us (0.962)
  blocking collectives: 44.1 us -> 19.9 us
  waiting for transfers between devices: 41.9 us -> 60.3 us
    all_gather x2, blocking collectives: 44.1 us -> 19.9 us  [the longest x1 10.5 us: per_device(): near = lax.all_gather(near, 'x', axis=0, tiled=True)]
    all_to_all x1 -> x2, waiting for transfers between devices: 3.89 us -> 14.4 us  [the longest x1 7.28 us: per_device(): mine = lax.all_to_all(rounded, 'zh', 0, 0, tiled=True)]
    ppermute x0 -> x1, waiting for transfers between devices: none -> 7.46 us  [per_device(): taken = lax.ppermute(give, 'zl', [(0, 1), (1, 0)])]
    all_to_all x1, starting transfers between devices: 10.2 us -> 3.4 us  [per_device(): own = lax.all_to_all(mine, col, 0, 0, tiled=True)]
    all_to_all x1, waiting for transfers between devices: 6.45 us -> 0.01 us  [per_device(): own = lax.all_to_all(mine, col, 0, 0, tiled=True)]
    ppermute x1, waiting for transfers between devices: 0.01 us -> 4.62 us  [per_device(): pair = lax.ppermute(mine, 'zl', [(0, 1), (1, 0)])]
    all_to_all x1 -> x2, starting transfers between devices: 13.8 us -> 17.4 us  [the longest x1 13.4 us: per_device(): summed = lax.all_to_all(halves, 'zh', 0, 0, tiled=True)]
    ppermute x1, starting transfers between devices: 2.36 us -> 5.83 us  [per_device(): far = lax.ppermute(near, 'core', [(0, 1), (1, 0)])]
  transfers between devices with their start and end apart: 8 -> 10, of which waited for: 6 -> 8; matrix products, arithmetic and copies ran while one was open for 1% -> 1% of each run, Pallas kernels for 0% -> 1%
where the time goes in v4:
time: 152 us; the launch traced here: 151 us
  starting transfers between devices  60.3 us (40%)
  waiting for transfers between devices  60.3 us (40%)
  blocking collectives  19.9 us (13%)
  Pallas kernels  6.71 us (4%)
  local copies, waits for them, and re-layouts  2.24 us (1%)
    all_to_all x1, starting transfers between devices, per_device(): summed = lax.all_to_all(halves, 'zh', 0, 0, tiled=True)  13.4 us
    all_to_all x1, waiting for transfers between devices, per_device(): got = lax.all_to_all(sent, plane, 0, 0, tiled=True)  12.4 us
    all_to_all x1, starting transfers between devices, per_device(): summaries = lax.all_to_all(summary, line, 0, 0, tiled=True)  11.6 us
    all_gather x1, blocking collectives, per_device(): near = lax.all_gather(near, 'x', axis=0, tiled=True)  10.5 us
    all_to_all x1, starting transfers between devices, per_device(): got = lax.all_to_all(sent, plane, 0, 0, tiled=True)  10.5 us
    all_to_all x1, waiting for transfers between devices, per_device(): summaries = lax.all_to_all(summary, line, 0, 0, tiled=True)  9.6 us
    all_gather x1, blocking collectives, per_device(): near = lax.all_gather(near, 'y', axis=0, tiled=True)  9.4 us
    all_to_all x1, waiting for transfers between devices, per_device(): lax.all_to_all(predicted.reshape(devices, sites, span), plane, 0, 0, tile...  8.23 us
  transfers between devices with their start and end apart: 10, of which 8 were waited for; matrix products, arithmetic and copies ran while one was open for 1% of the time, Pallas kernels for 1%

profile of v4, /device:TPU:1, one launch (start us, length us, event | category | flops | bytes accessed | tf_op | source)
XLA Modules:
  0.0 151.1 jit_solution(17002984792937443011)
XLA Ops:
  0.6 0.0 copy-start
  0.6 2.1 %front.1 = bf16[32,16,1280]{2,1,0:T(8,128)(2,1)} custom-call(s32[16]{0:T(128)} %start_hbm.1, s32[16]{0:T(128)} %count_hbm.1, bf16[16,8192]{1,0:T(8,128)(2,1)} %values_hbm.1, bf16[16,1024]{1,0:T(8,128)(2,1)} %gain_hbm.1), custom_call_target="tpu_custom_call" | custom-call | tf_op jit(solution)/shard_map/front/pallas_call | solution.py:167
  2.8 10.5 %all-to-all-start = ((bf16[32,16,1280]{2,1,0:T(8,128)(2,1)}), bf16[32,16,1280]{2,1,0:T(8,128)(2,1)S(1)}, u32[]{:S(2)}, u32[]{:S(2)}) async-start(bf16[32,16,1280]{2,1,0:T(8,128)(2,1)} %front.1), calls=%async_computation | async-start | bytes 2621440 | tf_op jit(solution)/shard_map/all_to_all | solution.py:204
  13.3 0.0 copy-done
  13.3 3.1 %collective-permute-start = (f32[128,128]{1,0:T(8,128)S(1)}, f32[128,128]{1,0:T(8,128)S(1)}, u32[]{:S(2)}, u32[]{:S(2)}) collective-permute-start(f32[128,128]{1,0:T(8,128)S(1)} %constant_dynamic-slice_fusion), channel_id=1, source_target_pairs={{0,0},{1,16},{2,32},{3,48},{4,64},{5,80},{6,96},{7,112},{8,8},{9,2... | collective-permute-start | bytes 196616 | tf_op jit(solution)/shard_map/ppermute | solution.py:206
  16.5 0.8 dynamic-slice_bitcast_fusion.persist_ref
  17.2 3.5 %collective-permute-done.decay_ref = f32[128,128]{1,0:T(8,128)S(1)} collective-permute-done((f32[128,128]{1,0:T(8,128)S(1)}, f32[128,128]{1,0:T(8,128)S(1)}, u32[]{:S(2)}, u32[]{:S(2)}) %collective-permute-start) | collective-permute-done | bytes 65568 | tf_op jit(solution)/shard_map/ppermute | solution.py:206
  20.8 12.4 %all-to-all-done.got_ref = bf16[32,16,1280]{2,1,0:T(8,128)(2,1)S(1)} async-done(((bf16[32,16,1280]{2,1,0:T(8,128)(2,1)}), bf16[32,16,1280]{2,1,0:T(8,128)(2,1)S(1)}, u32[]{:S(2)}, u32[]{:S(2)}) %all-to-all-start) | async-done | bytes 1310752 | tf_op jit(solution)/shard_map/all_to_all | solution.py:204
  33.2 0.0 copy-start.1
  33.2 0.5 drive.1
  33.6 1.9 %collective-permute-start.1 = (bf16[8,128,128]{2,1,0:T(8,128)(2,1)S(1)}, bf16[8,128,128]{2,1,0:T(8,128)(2,1)S(1)}, u32[]{:S(2)}, u32[]{:S(2)}) collective-permute-start(bf16[8,128,128]{2,1,0:T(8,128)(2,1)S(1)} %get-tuple-element.23), channel_id=1, source_target_pairs={{0,8},{8,0},{1,9},{9,1},{2,10},{10,2},{3,11},{11,3},{4,12},{12,4},... | collective-permute-start | bytes 786440 | tf_op jit(solution)/shard_map/ppermute | solution.py:213
  35.6 7.5 %collective-permute-done.1 = bf16[8,128,128]{2,1,0:T(8,128)(2,1)S(1)} collective-permute-done((bf16[8,128,128]{2,1,0:T(8,128)(2,1)S(1)}, bf16[8,128,128]{2,1,0:T(8,128)(2,1)S(1)}, u32[]{:S(2)}, u32[]{:S(2)}) %collective-permute-start.1) | collective-permute-done | bytes 262176 | tf_op jit(solution)/shard_map/ppermute | solution.py:213
  43.0 0.8 add_convert_fusion
  43.8 13.4 %all-to-all-start.1 = ((bf16[8,128,128]{2,1,0:T(8,128)(2,1)}), bf16[8,128,128]{2,1,0:T(8,128)(2,1)S(1)}, u32[]{:S(2)}, u32[]{:S(2)}) async-start(bf16[8,128,128]{2,1,0:T(8,128)(2,1)} %add_convert_fusion), calls=%async_computation.1 | async-start | bytes 524288 | tf_op jit(solution)/shard_map/all_to_all | solution.py:216
  57.2 0.0 copy-done.1
  57.2 9.4 %all_gather.6 = bf16[64,1024]{1,0:T(8,128)(2,1)S(1)} all-gather(bf16[16,1024]{1,0:T(8,128)(2,1)S(1)} %copy-done.1), channel_id=1, replica_groups=mesh['x'=4,'zh'=8,'zl'=2,'y'=4,'core'=2] {'y'}, dimensions={0}, use_global_device_ids=true | all-gather | bytes 163840 | tf_op jit(solution)/shard_map/all_gather | solution.py:217
  66.6 7.1 %all-to-all-done.1.parts_ref = bf16[8,128,128]{2,1,0:T(8,128)(2,1)S(1)} async-done(((bf16[8,128,128]{2,1,0:T(8,128)(2,1)}), bf16[8,128,128]{2,1,0:T(8,128)(2,1)S(1)}, u32[]{:S(2)}, u32[]{:S(2)}) %all-to-all-start.1) | async-done | bytes 262176 | tf_op jit(solution)/shard_map/all_to_all | solution.py:216
  73.7 0.9 scan.1
  74.6 11.6 %all-to-all-start.2 = ((f32[64,8,128]{2,1,0:T(8,128)}), f32[64,8,128]{2,1,0:T(8,128)S(1)}, u32[]{:S(2)}, u32[]{:S(2)}) async-start(f32[64,8,128]{2,1,0:T(8,128)} %get-tuple-element.29), calls=%async_computation.2 | async-start | bytes 524288 | tf_op jit(solution)/shard_map/all_to_all | solution.py:224
  86.3 9.6 %all-to-all-done.2.slabs_ref = f32[64,8,128]{2,1,0:T(8,128)S(1)} async-done(((f32[64,8,128]{2,1,0:T(8,128)}), f32[64,8,128]{2,1,0:T(8,128)S(1)}, u32[]{:S(2)}, u32[]{:S(2)}) %all-to-all-start.2) | async-done | bytes 262176 | tf_op jit(solution)/shard_map/all_to_all | solution.py:224
  95.9 1.1 finish.1
  97.0 4.1 %all-to-all-start.3 = ((bf16[8,128,128]{2,1,0:T(8,128)(2,1)}), bf16[8,128,128]{2,1,0:T(8,128)(2,1)}, u32[]{:S(2)}, u32[]{:S(2)}) async-start(bf16[8,128,128]{2,1,0:T(8,128)(2,1)} %finish.1), calls=%async_computation.3 | async-start | bytes 524288 | tf_op jit(solution)/shard_map/all_to_all | solution.py:232
  101.0 10.5 %all_gather.7.near_ref = bf16[256,1024]{1,0:T(8,128)(2,1)S(1)} all-gather(bf16[64,1024]{1,0:T(8,128)(2,1)S(1)} %all_gather.6), channel_id=1, replica_groups=mesh['x'=4,'zh'=8,'zl'=2,'y'=4,'core'=2] {'x'}, dimensions={0}, use_global_device_ids=true | all-gather | bytes 655360 | tf_op jit(solution)/shard_map/all_gather | solution.py:233
  111.6 7.3 %all-to-all-done.3.mine_ref = bf16[8,128,128]{2,1,0:T(8,128)(2,1)} async-done(((bf16[8,128,128]{2,1,0:T(8,128)(2,1)}), bf16[8,128,128]{2,1,0:T(8,128)(2,1)}, u32[]{:S(2)}, u32[]{:S(2)}) %all-to-all-start.3) | async-done | bytes 262176 | tf_op jit(solution)/shard_map/all_to_all | solution.py:232
  118.9 5.8 %collective-permute-start.2 = (bf16[256,1024]{1,0:T(8,128)(2,1)S(1)}, bf16[256,1024]{1,0:T(8,128)(2,1)S(1)}, u32[]{:S(2)}, u32[]{:S(2)}) collective-permute-start(bf16[256,1024]{1,0:T(8,128)(2,1)S(1)} %all_gather.7.near_ref), channel_id=1, source_target_pairs={{0,1},{1,0},{2,3},{3,2},{4,5},{5,4},{6,7},{7,6},{8,9},{9,8},{10,11... | collective-permute-start | bytes 1572872 | tf_op jit(solution)/shard_map/ppermute | solution.py:235
  124.7 1.9 %collective-permute-start.3 = (bf16[8,128,128]{2,1,0:T(8,128)(2,1)}, bf16[8,128,128]{2,1,0:T(8,128)(2,1)S(1)}, u32[]{:S(2)}, u32[]{:S(2)}) collective-permute-start(bf16[8,128,128]{2,1,0:T(8,128)(2,1)} %all-to-all-done.3.mine_ref), channel_id=1, source_target_pairs={{0,8},{8,0},{1,9},{9,1},{2,10},{10,2},{3,11},{11,3},{4,12},{12,4},... | collective-permute-start | bytes 786440 | tf_op jit(solution)/shard_map/ppermute | solution.py:236
  126.6 3.4 %all-to-all-start.4 = ((bf16[8,128,128]{2,1,0:T(8,128)(2,1)}), bf16[8,128,128]{2,1,0:T(8,128)(2,1)S(1)}, u32[]{:S(2)}, u32[]{:S(2)}) async-start(bf16[8,128,128]{2,1,0:T(8,128)(2,1)} %all-to-all-done.3.mine_ref), calls=%async_computation.4 | async-start | bytes 524288 | tf_op jit(solution)/shard_map/all_to_all | solution.py:237
  130.0 0.1 pad_add_fusion.where_ref
  130.1 4.6 %collective-permute-done.3.pair_ref = bf16[8,128,128]{2,1,0:T(8,128)(2,1)S(1)} collective-permute-done((bf16[8,128,128]{2,1,0:T(8,128)(2,1)}, bf16[8,128,128]{2,1,0:T(8,128)(2,1)S(1)}, u32[]{:S(2)}, u32[]{:S(2)}) %collective-permute-start.3) | collective-permute-done | bytes 262176 | tf_op jit(solution)/shard_map/ppermute | solution.py:236
  134.7 0.0 collective-permute-done.2.far_ref
  134.7 2.1 %predict.1 = bf16[16,2,16,256]{3,2,1,0:T(8,128)(2,1)} custom-call(s32[2]{0:T(128)S(1)} %pad_add_fusion.where_ref, bf16[256,1024]{1,0:T(8,128)(2,1)S(1)} %all_gather.7.near_ref, bf16[256,1024]{1,0:T(8,128)(2,1)S(1)} %collective-permute-done.2.far_ref, bf16[8,128,128]{2,1,0:T(8,128)(2,1)} %all-to-all-done.3.mine_ref, ...), custom_call_target="tpu_custom_call" | custom-call | tf_op jit(solution)/shard_map/predict/pallas_call | solution.py:167
  136.9 0.0 all-to-all-done.4
  136.9 4.5 %all-to-all-start.5 = ((bf16[32,16,256]{2,1,0:T(8,128)(2,1)}), bf16[32,16,256]{2,1,0:T(8,128)(2,1)S(1)}, u32[]{:S(2)}, u32[]{:S(2)}) async-start(bf16[32,16,256]{2,1,0:T(8,128)(2,1)} %bitcast.6), calls=%async_computation.5 | async-start | bytes 524288 | tf_op jit(solution)/shard_map/all_to_all | solution.py:247
  141.4 0.7 copy.10
  142.2 8.2 %all-to-all-done.5 = bf16[32,16,256]{2,1,0:T(8,128)(2,1)S(1)} async-done(((bf16[32,16,256]{2,1,0:T(8,128)(2,1)}), bf16[32,16,256]{2,1,0:T(8,128)(2,1)S(1)}, u32[]{:S(2)}, u32[]{:S(2)}) %all-to-all-start.5) | async-done | bytes 262176 | tf_op jit(solution)/shard_map/all_to_all | solution.py:247
  150.4 0.7 copy.11
  (2 shorter events, 0.0 us)
Async XLA Ops:
  0.6 12.7 %copy-start = (f32[128,1024]{1,0:T(8,128)S(1)}, f32[128,1024]{1,0:T(8,128)}, u32[]{:S(2)}) copy-start(f32[128,1024]{1,0:T(8,128)} %param.12) | copy-start | bytes 1572868
  2.8 30.4 %all-to-all-start = ((bf16[32,16,1280]{2,1,0:T(8,128)(2,1)}), bf16[32,16,1280]{2,1,0:T(8,128)(2,1)S(1)}, u32[]{:S(2)}, u32[]{:S(2)}) async-start(bf16[32,16,1280]{2,1,0:T(8,128)(2,1)} %front.1), calls=%async_computation | async-start | bytes 2621440 | tf_op jit(solution)/shard_map/all_to_all | solution.py:204
  13.3 7.4 %collective-permute-start = (f32[128,128]{1,0:T(8,128)S(1)}, f32[128,128]{1,0:T(8,128)S(1)}, u32[]{:S(2)}, u32[]{:S(2)}) collective-permute-start(f32[128,128]{1,0:T(8,128)S(1)} %constant_dynamic-slice_fusion), channel_id=1, source_target_pairs={{0,0},{1,16},{2,32},{3,48},{4,64},{5,80},{6,96},{7,112},{8,8},{9,2... | collective-permute-start | bytes 196616 | tf_op jit(solution)/shard_map/ppermute | solution.py:206
  33.2 24.0 %copy-start.1 = (bf16[16,1024]{1,0:T(8,128)(2,1)S(1)}, bf16[16,1024]{1,0:T(8,128)(2,1)}, u32[]{:S(2)}) copy-start(bf16[16,1024]{1,0:T(8,128)(2,1)} %param.11) | copy-start | bytes 98308
  33.6 9.4 %collective-permute-start.1 = (bf16[8,128,128]{2,1,0:T(8,128)(2,1)S(1)}, bf16[8,128,128]{2,1,0:T(8,128)(2,1)S(1)}, u32[]{:S(2)}, u32[]{:S(2)}) collective-permute-start(bf16[8,128,128]{2,1,0:T(8,128)(2,1)S(1)} %get-tuple-element.23), channel_id=1, source_target_pairs={{0,8},{8,0},{1,9},{9,1},{2,10},{10,2},{3,11},{11,3},{4,12},{12,4},... | collective-permute-start | bytes 786440 | tf_op jit(solution)/shard_map/ppermute | solution.py:213
  43.8 29.9 %all-to-all-start.1 = ((bf16[8,128,128]{2,1,0:T(8,128)(2,1)}), bf16[8,128,128]{2,1,0:T(8,128)(2,1)S(1)}, u32[]{:S(2)}, u32[]{:S(2)}) async-start(bf16[8,128,128]{2,1,0:T(8,128)(2,1)} %add_convert_fusion), calls=%async_computation.1 | async-start | bytes 524288 | tf_op jit(solution)/shard_map/all_to_all | solution.py:216
  74.6 21.3 %all-to-all-start.2 = ((f32[64,8,128]{2,1,0:T(8,128)}), f32[64,8,128]{2,1,0:T(8,128)S(1)}, u32[]{:S(2)}, u32[]{:S(2)}) async-start(f32[64,8,128]{2,1,0:T(8,128)} %get-tuple-element.29), calls=%async_computation.2 | async-start | bytes 524288 | tf_op jit(solution)/shard_map/all_to_all | solution.py:224
  97.0 21.9 %all-to-all-start.3 = ((bf16[8,128,128]{2,1,0:T(8,128)(2,1)}), bf16[8,128,128]{2,1,0:T(8,128)(2,1)}, u32[]{:S(2)}, u32[]{:S(2)}) async-start(bf16[8,128,128]{2,1,0:T(8,128)(2,1)} %finish.1), calls=%async_computation.3 | async-start | bytes 524288 | tf_op jit(solution)/shard_map/all_to_all | solution.py:232
  118.9 15.9 %collective-permute-start.2 = (bf16[256,1024]{1,0:T(8,128)(2,1)S(1)}, bf16[256,1024]{1,0:T(8,128)(2,1)S(1)}, u32[]{:S(2)}, u32[]{:S(2)}) collective-permute-start(bf16[256,1024]{1,0:T(8,128)(2,1)S(1)} %all_gather.7.near_ref), channel_id=1, source_target_pairs={{0,1},{1,0},{2,3},{3,2},{4,5},{5,4},{6,7},{7,6},{8,9},{9,8},{10,11... | collective-permute-start | bytes 1572872 | tf_op jit(solution)/shard_map/ppermute | solution.py:235
  124.7 10.0 %collective-permute-start.3 = (bf16[8,128,128]{2,1,0:T(8,128)(2,1)}, bf16[8,128,128]{2,1,0:T(8,128)(2,1)S(1)}, u32[]{:S(2)}, u32[]{:S(2)}) collective-permute-start(bf16[8,128,128]{2,1,0:T(8,128)(2,1)} %all-to-all-done.3.mine_ref), channel_id=1, source_target_pairs={{0,8},{8,0},{1,9},{9,1},{2,10},{10,2},{3,11},{11,3},{4,12},{12,4},... | collective-permute-start | bytes 786440 | tf_op jit(solution)/shard_map/ppermute | solution.py:236
  126.6 10.2 %all-to-all-start.4 = ((bf16[8,128,128]{2,1,0:T(8,128)(2,1)}), bf16[8,128,128]{2,1,0:T(8,128)(2,1)S(1)}, u32[]{:S(2)}, u32[]{:S(2)}) async-start(bf16[8,128,128]{2,1,0:T(8,128)(2,1)} %all-to-all-done.3.mine_ref), calls=%async_computation.4 | async-start | bytes 524288 | tf_op jit(solution)/shard_map/all_to_all | solution.py:237
  136.9 13.5 %all-to-all-start.5 = ((bf16[32,16,256]{2,1,0:T(8,128)(2,1)}), bf16[32,16,256]{2,1,0:T(8,128)(2,1)S(1)}, u32[]{:S(2)}, u32[]{:S(2)}) async-start(bf16[32,16,256]{2,1,0:T(8,128)(2,1)} %bitcast.6), calls=%async_computation.5 | async-start | bytes 524288 | tf_op jit(solution)/shard_map/all_to_all | solution.py:247

commit v5 on v4

--- a/solution.py
+++ b/solution.py
@@ -48,19 +48,17 @@
         copy.wait()
 
 
-def drive_kernel(part_ref, got_ref, keep_ref, give_ref):
+def drive_kernel(got_ref, out_ref):
     sources, sites, width = got_ref.shape
-    blocks, slab, share = keep_ref.shape
-    span = width - blocks * share
+    blocks, parts, slab, share = out_ref.shape
+    span = parts * slab
     rows = got_ref[:, :, :span].reshape(sources * sites, span)
     gains = got_ref[:, :, span:].reshape(sources * sites, blocks * share)
     partial = lax.dot_general(rows, gains, (((0,), (0,)), ((), ())), preferred_element_type=jnp.float32)
-    first = part_ref[0] == 0
-    keep = jnp.where(first, partial[:slab], partial[slab:])
-    give = jnp.where(first, partial[slab:], partial[:slab]).astype(give_ref.dtype)
+    partial = partial.astype(out_ref.dtype)
     for block in range(blocks):
-        keep_ref[block] = keep[:, block * share:(block + 1) * share]
-        give_ref[block] = give[:, block * share:(block + 1) * share]
+        for part in range(parts):
+            out_ref[block, part] = partial[part * slab:(part + 1) * slab, block * share:(block + 1) * share]
 
 
 def shifted(value, by, fill):
@@ -207,14 +205,10 @@
     persist = lax.dynamic_slice_in_dim(persistence, lax.axis_index("zh") * share, share, 0)[None]
     got, decays, persist = lax.optimization_barrier((got, decays, persist))
 
-    part = lax.axis_index("zl").astype(jnp.int32)
-    both = (shape((blocks, slab, share), f32), shape((blocks, slab, share), bf16))
-    keep, give = call(drive_kernel, "drive", both, part[None], got, scalars=1)
-    taken = lax.ppermute(give, "zl", [(0, 1), (1, 0)])
-    taken, near = lax.optimization_barrier((taken, site_loading))
-    halves = (keep + taken.astype(f32)).astype(bf16)
-    summed = lax.all_to_all(halves, "zh", 0, 0, tiled=True)
-    near = lax.all_gather(near, "y", axis=0, tiled=True)
+    partial = call(drive_kernel, "drive", shape((blocks, parts, slab, share), bf16), got)
+    summed = lax.all_to_all(partial.reshape(blocks * parts, slab, share), planes, 0, 0, tiled=True)
+    near, _ = lax.optimization_barrier((site_loading, got))
+    near = lax.all_gather(near, ("x", "y"), axis=0, tiled=True)
     summed, near = lax.optimization_barrier((summed, near))
     square = shape((slab, share), f32)
     smooth, entry, product, summary = call(
@@ -222,7 +216,8 @@
         scratch=[pltpu.VMEM((slab, share), f32)],
     )
     summaries = lax.all_to_all(summary, line, 0, 0, tiled=True)
-    summaries, near = lax.optimization_barrier((summaries, near))
+    far = lax.ppermute(near, "core", [(0, 1), (1, 0)])
+    summaries, near, far = lax.optimization_barrier((summaries, near, far))
     rounded = call(
         finish_kernel, "finish", shape((blocks, share, slab), bf16),
         lax.axis_index(line).astype(jnp.int32)[None], summaries, smooth, entry, product,
@@ -230,14 +225,11 @@
     )
 
     mine = lax.all_to_all(rounded, "zh", 0, 0, tiled=True)
-    near = lax.all_gather(near, "x", axis=0, tiled=True)
-    mine, near = lax.optimization_barrier((mine, near))
-    far = lax.ppermute(near, "core", [(0, 1), (1, 0)])
     pair = lax.ppermute(mine, "zl", [(0, 1), (1, 0)])
     own = lax.all_to_all(mine, col, 0, 0, tiled=True)
 
     cores = lax.axis_size("core")
-    where = jnp.stack([part, lax.axis_index("core").astype(jnp.int32)])
+    where = jnp.stack([lax.axis_index("zl"), lax.axis_index("core")]).astype(jnp.int32)
     predicted = call(
         predict_kernel, "predict", shape((devices // cores, cores, sites, span), bf16),
         where, near, far, mine, pair, scalars=1,

time: 152 us -> 149 us (0.980)
  blocking collectives: 19.9 us -> 41.2 us
  waiting for transfers between devices: 60.3 us -> 39.6 us
  starting transfers between devices: 60.3 us -> 57.8 us
    all_to_all x0 -> x1, blocking collectives: none -> 22.2 us  [per_device(): mine = lax.all_to_all(rounded, 'zh', 0, 0, tiled=True)]
    all_to_all x2 -> x1, waiting for transfers between devices: 14.4 us -> 3.89 us  [per_device(): lax.all_to_all(partial.reshape(blocks * parts, slab, share), planes, 0, 0...]
    ppermute x1 -> x0, waiting for transfers between devices: 7.46 us -> none  [per_device(): taken = lax.ppermute(give, 'zl', [(0, 1), (1, 0)])]
    ppermute x1, waiting for transfers between devices: 4.62 us -> 0.01 us  [per_device(): pair = lax.ppermute(mine, 'zl', [(0, 1), (1, 0)])]
    all_to_all x1, starting transfers between devices: 3.4 us -> 7.84 us  [per_device(): own = lax.all_to_all(mine, col, 0, 0, tiled=True)]
    all_to_all x1, waiting for transfers between devices: 0.01 us -> 4.34 us  [per_device(): own = lax.all_to_all(mine, col, 0, 0, tiled=True)]
    all_to_all x1, waiting for transfers between devices: 9.6 us -> 5.73 us  [per_device(): summaries = lax.all_to_all(summary, line, 0, 0, tiled=True)]
    all_to_all x2 -> x1, starting transfers between devices: 17.4 us -> 13.8 us  [per_device(): lax.all_to_all(partial.reshape(blocks * parts, slab, share), planes, 0, 0...]
  transfers between devices with their start and end apart: 10 -> 8, of which waited for: 8 -> 7; matrix products, arithmetic and copies ran while one was open for 1% -> 1% of each run, Pallas kernels for 1% -> 1%
where the time goes in v5:
time: 149 us
  starting transfers between devices  57.8 us (39%)
  blocking collectives  41.2 us (28%)
  waiting for transfers between devices  39.6 us (27%)
  Pallas kernels  6.81 us (5%)
  local copies, waits for them, and re-layouts  2.24 us (2%)
    all_to_all x1, blocking collectives, per_device(): mine = lax.all_to_all(rounded, 'zh', 0, 0, tiled=True)  22.2 us
    all_gather x1, blocking collectives, per_device(): near = lax.all_gather(near, ('x', 'y'), axis=0, tiled=True)  19 us
    all_to_all x1, starting transfers between devices, per_device(): lax.all_to_all(partial.reshape(blocks * parts, slab, share), planes, 0, 0...  13.8 us
    all_to_all x1, starting transfers between devices, per_device(): summaries = lax.all_to_all(summary, line, 0, 0, tiled=True)  13.5 us
    all_to_all x1, waiting for transfers between devices, per_device(): got = lax.all_to_all(sent, plane, 0, 0, tiled=True)  12.4 us
    all_to_all x1, starting transfers between devices, per_device(): got = lax.all_to_all(sent, plane, 0, 0, tiled=True)  10.5 us
    all_to_all x1, waiting for transfers between devices, per_device(): lax.all_to_all(predicted.reshape(devices, sites, span), plane, 0, 0, tile...  8.23 us
    all_to_all x1, starting transfers between devices, per_device(): own = lax.all_to_all(mine, col, 0, 0, tiled=True)  7.84 us
  transfers between devices with their start and end apart: 8, of which 7 were waited for; matrix products, arithmetic and copies ran while one was open for 1% of the time, Pallas kernels for 1%

profile of v5, /device:TPU:1, one launch (start us, length us, event | category | flops | bytes accessed | tf_op | source)
XLA Modules:
  0.0 148.6 jit_solution(436511038420040983)
XLA Ops:
  0.6 0.0 copy-start
  0.6 2.1 %front.1 = bf16[32,16,1280]{2,1,0:T(8,128)(2,1)} custom-call(s32[16]{0:T(128)} %start_hbm.1, s32[16]{0:T(128)} %count_hbm.1, bf16[16,8192]{1,0:T(8,128)(2,1)} %values_hbm.1, bf16[16,1024]{1,0:T(8,128)(2,1)} %gain_hbm.1), custom_call_target="tpu_custom_call" | custom-call | tf_op jit(solution)/shard_map/front/pallas_call | solution.py:165
  2.8 10.5 %all-to-all-start = ((bf16[32,16,1280]{2,1,0:T(8,128)(2,1)}), bf16[32,16,1280]{2,1,0:T(8,128)(2,1)S(1)}, u32[]{:S(2)}, u32[]{:S(2)}) async-start(bf16[32,16,1280]{2,1,0:T(8,128)(2,1)} %front.1), calls=%async_computation | async-start | bytes 2621440 | tf_op jit(solution)/shard_map/all_to_all | solution.py:202
  13.3 0.0 copy-done
  13.3 3.1 %collective-permute-start = (f32[128,128]{1,0:T(8,128)S(1)}, f32[128,128]{1,0:T(8,128)S(1)}, u32[]{:S(2)}, u32[]{:S(2)}) collective-permute-start(f32[128,128]{1,0:T(8,128)S(1)} %constant_dynamic-slice_fusion), channel_id=1, source_target_pairs={{0,0},{1,16},{2,32},{3,48},{4,64},{5,80},{6,96},{7,112},{8,8},{9,2... | collective-permute-start | bytes 196616 | tf_op jit(solution)/shard_map/ppermute | solution.py:204
  16.5 0.8 dynamic-slice_bitcast_fusion.persist_ref
  17.2 0.0 copy-start.1
  17.2 3.5 %collective-permute-done.decay_ref = f32[128,128]{1,0:T(8,128)S(1)} collective-permute-done((f32[128,128]{1,0:T(8,128)S(1)}, f32[128,128]{1,0:T(8,128)S(1)}, u32[]{:S(2)}, u32[]{:S(2)}) %collective-permute-start) | collective-permute-done | bytes 65568 | tf_op jit(solution)/shard_map/ppermute | solution.py:204
  20.7 12.4 %all-to-all-done.got_ref = bf16[32,16,1280]{2,1,0:T(8,128)(2,1)S(1)} async-done(((bf16[32,16,1280]{2,1,0:T(8,128)(2,1)}), bf16[32,16,1280]{2,1,0:T(8,128)(2,1)S(1)}, u32[]{:S(2)}, u32[]{:S(2)}) %all-to-all-start) | async-done | bytes 1310752 | tf_op jit(solution)/shard_map/all_to_all | solution.py:202
  33.2 1.2 drive.1
  34.4 13.8 %all-to-all-start.1 = ((bf16[16,128,128]{2,1,0:T(8,128)(2,1)}), bf16[16,128,128]{2,1,0:T(8,128)(2,1)S(1)}, u32[]{:S(2)}, u32[]{:S(2)}) async-start(bf16[16,128,128]{2,1,0:T(8,128)(2,1)} %bitcast.3), calls=%async_computation.1 | async-start | bytes 1048576 | tf_op jit(solution)/shard_map/all_to_all | solution.py:209
  48.2 0.0 copy-done.1
  48.2 19.0 %all_gather.3.near_ref = bf16[256,1024]{1,0:T(8,128)(2,1)S(1)} all-gather(bf16[16,1024]{1,0:T(8,128)(2,1)S(1)} %copy-done.1), channel_id=1, replica_groups=mesh['x'=4,'zh'=8,'zl'=2,'y'=4,'core'=2] {'x','y'}, dimensions={0}, use_global_device_ids=true | all-gather | bytes 557056 | tf_op jit(solution)/shard_map/all_gather | solution.py:211
  67.1 3.9 %all-to-all-done.1.parts_ref = bf16[16,128,128]{2,1,0:T(8,128)(2,1)S(1)} async-done(((bf16[16,128,128]{2,1,0:T(8,128)(2,1)}), bf16[16,128,128]{2,1,0:T(8,128)(2,1)S(1)}, u32[]{:S(2)}, u32[]{:S(2)}) %all-to-all-start.1) | async-done | bytes 524320 | tf_op jit(solution)/shard_map/all_to_all | solution.py:209
  71.0 1.0 scan.1
  72.0 13.5 %all-to-all-start.2 = ((f32[64,8,128]{2,1,0:T(8,128)}), f32[64,8,128]{2,1,0:T(8,128)S(1)}, u32[]{:S(2)}, u32[]{:S(2)}) async-start(f32[64,8,128]{2,1,0:T(8,128)} %get-tuple-element.22), calls=%async_computation.2 | async-start | bytes 524288 | tf_op jit(solution)/shard_map/all_to_all | solution.py:218
  85.5 2.4 %collective-permute-start.1 = (bf16[256,1024]{1,0:T(8,128)(2,1)S(1)}, bf16[256,1024]{1,0:T(8,128)(2,1)S(1)}, u32[]{:S(2)}, u32[]{:S(2)}) collective-permute-start(bf16[256,1024]{1,0:T(8,128)(2,1)S(1)} %all_gather.3.near_ref), channel_id=1, source_target_pairs={{0,1},{1,0},{2,3},{3,2},{4,5},{5,4},{6,7},{7,6},{8,9},{9,8},{10,11... | collective-permute-start | bytes 1572872 | tf_op jit(solution)/shard_map/ppermute | solution.py:219
  87.9 1.5 %collective-permute-done.1.far_ref = bf16[256,1024]{1,0:T(8,128)(2,1)S(1)} collective-permute-done((bf16[256,1024]{1,0:T(8,128)(2,1)S(1)}, bf16[256,1024]{1,0:T(8,128)(2,1)S(1)}, u32[]{:S(2)}, u32[]{:S(2)}) %collective-permute-start.1) | collective-permute-done | bytes 524320 | tf_op jit(solution)/shard_map/ppermute | solution.py:219
  89.4 5.7 %all-to-all-done.2.slabs_ref = f32[64,8,128]{2,1,0:T(8,128)S(1)} async-done(((f32[64,8,128]{2,1,0:T(8,128)}), f32[64,8,128]{2,1,0:T(8,128)S(1)}, u32[]{:S(2)}, u32[]{:S(2)}) %all-to-all-start.2) | async-done | bytes 262176 | tf_op jit(solution)/shard_map/all_to_all | solution.py:218
  95.2 0.4 finish.1
  95.6 22.2 %all_to_all.30.mine_ref = bf16[8,128,128]{2,1,0:T(8,128)(2,1)} all-to-all(bf16[8,128,128]{2,1,0:T(8,128)(2,1)S(1)} %finish.1), channel_id=1, replica_groups=mesh['x'=4,'zh'=8,'zl'=2,'y'=4,'core'=2] {'zh'}, dimensions={0} | all-to-all | bytes 524288 | tf_op jit(solution)/shard_map/all_to_all | solution.py:227
  117.8 1.9 %collective-permute-start.2 = (bf16[8,128,128]{2,1,0:T(8,128)(2,1)}, bf16[8,128,128]{2,1,0:T(8,128)(2,1)S(1)}, u32[]{:S(2)}, u32[]{:S(2)}) collective-permute-start(bf16[8,128,128]{2,1,0:T(8,128)(2,1)} %all_to_all.30.mine_ref), channel_id=1, source_target_pairs={{0,8},{8,0},{1,9},{9,1},{2,10},{10,2},{3,11},{11,3},{4,12},{12,4},... | collective-permute-start | bytes 786440 | tf_op jit(solution)/shard_map/ppermute | solution.py:228
  119.7 7.8 %all-to-all-start.4 = ((bf16[8,128,128]{2,1,0:T(8,128)(2,1)}), bf16[8,128,128]{2,1,0:T(8,128)(2,1)S(1)}, u32[]{:S(2)}, u32[]{:S(2)}) async-start(bf16[8,128,128]{2,1,0:T(8,128)(2,1)} %all_to_all.30.mine_ref), calls=%async_computation.4 | async-start | bytes 524288 | tf_op jit(solution)/shard_map/all_to_all | solution.py:229
  127.5 0.1 pad_add_fusion.where_ref
  127.6 0.0 collective-permute-done.2.pair_ref
  127.6 2.1 %predict.1 = bf16[16,2,16,256]{3,2,1,0:T(8,128)(2,1)} custom-call(s32[2]{0:T(128)S(1)} %pad_add_fusion.where_ref, bf16[256,1024]{1,0:T(8,128)(2,1)S(1)} %all_gather.3.near_ref, bf16[256,1024]{1,0:T(8,128)(2,1)S(1)} %collective-permute-done.1.far_ref, bf16[8,128,128]{2,1,0:T(8,128)(2,1)} %all_to_all.30.mine_ref, ...), custom_call_target="tpu_custom_call" | custom-call | tf_op jit(solution)/shard_map/predict/pallas_call | solution.py:165
  129.7 4.3 %all-to-all-done.4 = bf16[8,128,128]{2,1,0:T(8,128)(2,1)S(1)} async-done(((bf16[8,128,128]{2,1,0:T(8,128)(2,1)}), bf16[8,128,128]{2,1,0:T(8,128)(2,1)S(1)}, u32[]{:S(2)}, u32[]{:S(2)}) %all-to-all-start.4) | async-done | bytes 262176 | tf_op jit(solution)/shard_map/all_to_all | solution.py:229
  134.1 4.8 %all-to-all-start.5 = ((bf16[32,16,256]{2,1,0:T(8,128)(2,1)}), bf16[32,16,256]{2,1,0:T(8,128)(2,1)S(1)}, u32[]{:S(2)}, u32[]{:S(2)}) async-start(bf16[32,16,256]{2,1,0:T(8,128)(2,1)} %bitcast.7), calls=%async_computation.5 | async-start | bytes 524288 | tf_op jit(solution)/shard_map/all_to_all | solution.py:239
  138.9 0.7 copy.10
  139.6 8.2 %all-to-all-done.5 = bf16[32,16,256]{2,1,0:T(8,128)(2,1)S(1)} async-done(((bf16[32,16,256]{2,1,0:T(8,128)(2,1)}), bf16[32,16,256]{2,1,0:T(8,128)(2,1)S(1)}, u32[]{:S(2)}, u32[]{:S(2)}) %all-to-all-start.5) | async-done | bytes 262176 | tf_op jit(solution)/shard_map/all_to_all | solution.py:239
  147.8 0.7 copy.11
  (2 shorter events, 0.0 us)
Async XLA Ops:
  0.6 12.7 %copy-start = (f32[128,1024]{1,0:T(8,128)S(1)}, f32[128,1024]{1,0:T(8,128)}, u32[]{:S(2)}) copy-start(f32[128,1024]{1,0:T(8,128)} %param.12) | copy-start | bytes 1572868
  2.8 30.4 %all-to-all-start = ((bf16[32,16,1280]{2,1,0:T(8,128)(2,1)}), bf16[32,16,1280]{2,1,0:T(8,128)(2,1)S(1)}, u32[]{:S(2)}, u32[]{:S(2)}) async-start(bf16[32,16,1280]{2,1,0:T(8,128)(2,1)} %front.1), calls=%async_computation | async-start | bytes 2621440 | tf_op jit(solution)/shard_map/all_to_all | solution.py:202
  13.3 7.4 %collective-permute-start = (f32[128,128]{1,0:T(8,128)S(1)}, f32[128,128]{1,0:T(8,128)S(1)}, u32[]{:S(2)}, u32[]{:S(2)}) collective-permute-start(f32[128,128]{1,0:T(8,128)S(1)} %constant_dynamic-slice_fusion), channel_id=1, source_target_pairs={{0,0},{1,16},{2,32},{3,48},{4,64},{5,80},{6,96},{7,112},{8,8},{9,2... | collective-permute-start | bytes 196616 | tf_op jit(solution)/shard_map/ppermute | solution.py:204
  17.2 30.9 %copy-start.1 = (bf16[16,1024]{1,0:T(8,128)(2,1)S(1)}, bf16[16,1024]{1,0:T(8,128)(2,1)}, u32[]{:S(2)}) copy-start(bf16[16,1024]{1,0:T(8,128)(2,1)} %param.11) | copy-start | bytes 98308
  34.4 36.6 %all-to-all-start.1 = ((bf16[16,128,128]{2,1,0:T(8,128)(2,1)}), bf16[16,128,128]{2,1,0:T(8,128)(2,1)S(1)}, u32[]{:S(2)}, u32[]{:S(2)}) async-start(bf16[16,128,128]{2,1,0:T(8,128)(2,1)} %bitcast.3), calls=%async_computation.1 | async-start | bytes 1048576 | tf_op jit(solution)/shard_map/all_to_all | solution.py:209
  72.0 23.2 %all-to-all-start.2 = ((f32[64,8,128]{2,1,0:T(8,128)}), f32[64,8,128]{2,1,0:T(8,128)S(1)}, u32[]{:S(2)}, u32[]{:S(2)}) async-start(f32[64,8,128]{2,1,0:T(8,128)} %get-tuple-element.22), calls=%async_computation.2 | async-start | bytes 524288 | tf_op jit(solution)/shard_map/all_to_all | solution.py:218
  85.5 3.9 %collective-permute-start.1 = (bf16[256,1024]{1,0:T(8,128)(2,1)S(1)}, bf16[256,1024]{1,0:T(8,128)(2,1)S(1)}, u32[]{:S(2)}, u32[]{:S(2)}) collective-permute-start(bf16[256,1024]{1,0:T(8,128)(2,1)S(1)} %all_gather.3.near_ref), channel_id=1, source_target_pairs={{0,1},{1,0},{2,3},{3,2},{4,5},{5,4},{6,7},{7,6},{8,9},{9,8},{10,11... | collective-permute-start | bytes 1572872 | tf_op jit(solution)/shard_map/ppermute | solution.py:219
  117.8 9.8 %collective-permute-start.2 = (bf16[8,128,128]{2,1,0:T(8,128)(2,1)}, bf16[8,128,128]{2,1,0:T(8,128)(2,1)S(1)}, u32[]{:S(2)}, u32[]{:S(2)}) collective-permute-start(bf16[8,128,128]{2,1,0:T(8,128)(2,1)} %all_to_all.30.mine_ref), channel_id=1, source_target_pairs={{0,8},{8,0},{1,9},{9,1},{2,10},{10,2},{3,11},{11,3},{4,12},{12,4},... | collective-permute-start | bytes 786440 | tf_op jit(solution)/shard_map/ppermute | solution.py:228
  119.7 14.4 %all-to-all-start.4 = ((bf16[8,128,128]{2,1,0:T(8,128)(2,1)}), bf16[8,128,128]{2,1,0:T(8,128)(2,1)S(1)}, u32[]{:S(2)}, u32[]{:S(2)}) async-start(bf16[8,128,128]{2,1,0:T(8,128)(2,1)} %all_to_all.30.mine_ref), calls=%async_computation.4 | async-start | bytes 524288 | tf_op jit(solution)/shard_map/all_to_all | solution.py:229
  134.1 13.8 %all-to-all-start.5 = ((bf16[32,16,256]{2,1,0:T(8,128)(2,1)}), bf16[32,16,256]{2,1,0:T(8,128)(2,1)S(1)}, u32[]{:S(2)}, u32[]{:S(2)}) async-start(bf16[32,16,256]{2,1,0:T(8,128)(2,1)} %bitcast.7), calls=%async_computation.5 | async-start | bytes 524288 | tf_op jit(solution)/shard_map/all_to_all | solution.py:239

commit v6 on v5

--- a/solution.py
+++ b/solution.py
@@ -122,7 +122,7 @@
         summary_ref[to] = summary
 
 
-def finish_kernel(place_ref, slabs_ref, smooth_ref, entry_ref, product_ref, rounded_ref, fwd, bwd):
+def finish_kernel(place_ref, slabs_ref, smooth_ref, entry_ref, product_ref, rounded_ref, own_ref, fwd, bwd):
     count, _, width = slabs_ref.shape
 
     def of(at, what):
@@ -139,22 +139,23 @@
     place = place_ref[0]
     f_in, g_in = fwd[pl.ds(place, 1), :], bwd[pl.ds(place, 1), :]
     smoothed = smooth_ref[...] + entry_ref[...] * f_in + product_ref[...] * g_in
+    own_ref[...] = smoothed.astype(own_ref.dtype)
     rounded = smoothed.T.astype(rounded_ref.dtype)
     for to in range(rounded_ref.shape[0]):
         rounded_ref[to] = rounded
 
 
-def predict_kernel(where_ref, near_ref, far_ref, mine_ref, pair_ref, out_ref):
-    blocks, share, slab = mine_ref.shape
-    pairs, _, sites, span = out_ref.shape
-    first, core = where_ref[0] == 0, where_ref[1]
-    mine, pair = mine_ref[...].reshape(blocks * share, slab), pair_ref[...].reshape(blocks * share, slab)
-    states = jnp.concatenate([jnp.where(first, mine, pair), jnp.where(first, pair, mine)], axis=1)
-    loadings = jnp.concatenate([near_ref[...], far_ref[...]], axis=0)
-    predicted = jnp.dot(loadings, states, preferred_element_type=jnp.float32)
-    predicted = predicted.astype(out_ref.dtype).reshape(2, pairs, sites, span)
-    for other in range(2):
-        out_ref[:, core ^ other] = predicted[other]
+def predict_kernel(where_ref, near_ref, far_ref, pair_near_ref, pair_far_ref, states_ref, out_ref):
+    blocks, share, slab = states_ref.shape
+    chips, _, _, sites, _ = out_ref.shape
+    core, part = where_ref[0], where_ref[1]
+    states = states_ref[...].reshape(blocks * share, slab)
+    for plane, refs in enumerate(((near_ref, far_ref), (pair_near_ref, pair_far_ref))):
+        loadings = jnp.concatenate([ref[...] for ref in refs], axis=0)
+        predicted = jnp.dot(loadings, states, preferred_element_type=jnp.float32)
+        predicted = predicted.astype(out_ref.dtype).reshape(2, chips, sites, slab)
+        for other in range(2):
+            out_ref[:, core ^ other, part ^ plane] = predicted[other]
 
 
 def call(kernel, name, out_shape, *args, scratch=(), scalars=0, vmem=32, **grid):
@@ -209,6 +210,8 @@
     summed = lax.all_to_all(partial.reshape(blocks * parts, slab, share), planes, 0, 0, tiled=True)
     near, _ = lax.optimization_barrier((site_loading, got))
     near = lax.all_gather(near, ("x", "y"), axis=0, tiled=True)
+    swap = [(0, 1), (1, 0)]
+    pair_near, far = lax.ppermute(near, "zl", swap), lax.ppermute(near, "core", swap)
     summed, near = lax.optimization_barrier((summed, near))
     square = shape((slab, share), f32)
     smooth, entry, product, summary = call(
@@ -216,28 +219,26 @@
         scratch=[pltpu.VMEM((slab, share), f32)],
     )
     summaries = lax.all_to_all(summary, line, 0, 0, tiled=True)
-    far = lax.ppermute(near, "core", [(0, 1), (1, 0)])
-    summaries, near, far = lax.optimization_barrier((summaries, near, far))
-    rounded = call(
-        finish_kernel, "finish", shape((blocks, share, slab), bf16),
+    summaries, near, far, pair_near = lax.optimization_barrier((summaries, near, far, pair_near))
+    rounded, own = call(
+        finish_kernel, "finish", (shape((blocks, share, slab), bf16), shape((slab, share), bf16)),
         lax.axis_index(line).astype(jnp.int32)[None], summaries, smooth, entry, product,
         scratch=[pltpu.VMEM((slabs, share), f32)] * 2, scalars=1,
     )
 
-    mine = lax.all_to_all(rounded, "zh", 0, 0, tiled=True)
-    pair = lax.ppermute(mine, "zl", [(0, 1), (1, 0)])
-    own = lax.all_to_all(mine, col, 0, 0, tiled=True)
+    states = lax.all_to_all(rounded, "zh", 0, 0, tiled=True)
+    pair_far = lax.ppermute(pair_near, "core", swap)
+    out = lax.ppermute(own, planes + col, turn)
+    states, pair_far, out = lax.optimization_barrier((states, pair_far, out))
 
     cores = lax.axis_size("core")
-    where = jnp.stack([lax.axis_index("zl"), lax.axis_index("core")]).astype(jnp.int32)
+    where = jnp.stack([lax.axis_index("core"), lax.axis_index("zl")]).astype(jnp.int32)
     predicted = call(
-        predict_kernel, "predict", shape((devices // cores, cores, sites, span), bf16),
-        where, near, far, mine, pair, scalars=1,
-    )
-    predicted, own = lax.optimization_barrier((predicted, own))
-    out = lax.dynamic_index_in_dim(own, lax.axis_index("zh"), 0, False).T.astype(f32)
-    back = lax.all_to_all(predicted.reshape(devices, sites, span), plane, 0, 0, tiled=True)
-    return (out, back.transpose(1, 0, 2).reshape(sites, epochs))
+        predict_kernel, "predict", shape((devices // cores, cores, parts, sites, slab), bf16),
+        where, near, far, pair_near, pair_far, states, scalars=1,
+    )
+    back = lax.all_to_all(predicted.reshape(slabs, sites, slab), line, 0, 0, tiled=True)
+    return (out.astype(f32), back.transpose(1, 0, 2).reshape(sites, epochs))
 
 
 def solution(mesh):

time: 149 us -> 155 us (1.040)
  blocking collectives: 41.2 us -> 19 us
  starting transfers between devices: 57.8 us -> 74.5 us
  waiting for transfers between devices: 39.6 us -> 49.9 us
    all_to_all x1 -> x0, blocking collectives: 22.2 us -> none  [per_device(): mine = lax.all_to_all(rounded, 'zh', 0, 0, tiled=True)]
    ppermute x2 -> x4, waiting for transfers between devices: 1.5 us -> 16.8 us  [the longest x1 12.2 us: per_device(): lax.ppermute(near, 'zl', swap)]
    ppermute x2 -> x4, starting transfers between devices: 4.27 us -> 13 us  [the longest x1 4.45 us: per_device(): out = lax.ppermute(own, planes + col, turn)]
    all_to_all x2, starting transfers between devices: 12.6 us -> 20.6 us  [the longest x1 15.6 us: per_device(): lax.all_to_all(predicted.reshape(slabs, sites, slab), line, 0, 0, tiled=T...]
    all_to_all x1, waiting for transfers between devices: 5.73 us -> 0.01 us  [per_device(): summaries = lax.all_to_all(summary, line, 0, 0, tiled=True)]
  transfers between devices with their start and end apart: 8 -> 10, of which waited for: 7 -> 7; matrix products, arithmetic and copies ran while one was open for 1% -> 1% of each run, Pallas kernels for 1% -> 0%
where the time goes in v6:
time: 155 us; the launch traced here: 154 us
  starting transfers between devices  74.5 us (48%)
  waiting for transfers between devices  49.9 us (32%)
  blocking collectives  19 us (12%)
  Pallas kernels  7.42 us (5%)
    all_gather x1, blocking collectives, per_device(): near = lax.all_gather(near, ('x', 'y'), axis=0, tiled=True)  19 us
    all_to_all x1, starting transfers between devices, per_device(): lax.all_to_all(predicted.reshape(slabs, sites, slab), line, 0, 0, tiled=T...  15.6 us
    all_to_all x1, starting transfers between devices, per_device(): lax.all_to_all(partial.reshape(blocks * parts, slab, share), planes, 0, 0...  13.8 us
    all_to_all x1, starting transfers between devices, per_device(): summaries = lax.all_to_all(summary, line, 0, 0, tiled=True)  13.6 us
    all_to_all x1, waiting for transfers between devices, per_device(): got = lax.all_to_all(sent, plane, 0, 0, tiled=True)  12.4 us
    ppermute x1, waiting for transfers between devices, per_device(): lax.ppermute(near, 'zl', swap)  12.2 us
    all_to_all x1, starting transfers between devices, per_device(): got = lax.all_to_all(sent, plane, 0, 0, tiled=True)  10.5 us
    all_to_all x1, waiting for transfers between devices, per_device(): lax.all_to_all(predicted.reshape(slabs, sites, slab), line, 0, 0, tiled=T...  8.98 us
  transfers between devices with their start and end apart: 10, of which 7 were waited for; matrix products, arithmetic and copies ran while one was open for 1% of the time, Pallas kernels for 0%

profile of v6, /device:TPU:1, one launch (start us, length us, event | category | flops | bytes accessed | tf_op | source)
XLA Modules:
  0.0 153.8 jit_solution(4574827433596829895)
XLA Ops:
  0.6 0.0 copy-start
  0.6 2.1 %front.1 = bf16[32,16,1280]{2,1,0:T(8,128)(2,1)} custom-call(s32[16]{0:T(128)} %start_hbm.1, s32[16]{0:T(128)} %count_hbm.1, bf16[16,8192]{1,0:T(8,128)(2,1)} %values_hbm.1, bf16[16,1024]{1,0:T(8,128)(2,1)} %gain_hbm.1), custom_call_target="tpu_custom_call" | custom-call | tf_op jit(solution)/shard_map/front/pallas_call | solution.py:166
  2.8 10.5 %all-to-all-start = ((bf16[32,16,1280]{2,1,0:T(8,128)(2,1)}), bf16[32,16,1280]{2,1,0:T(8,128)(2,1)S(1)}, u32[]{:S(2)}, u32[]{:S(2)}) async-start(bf16[32,16,1280]{2,1,0:T(8,128)(2,1)} %front.1), calls=%async_computation | async-start | bytes 2621440 | tf_op jit(solution)/shard_map/all_to_all | solution.py:203
  13.3 0.0 copy-done
  13.3 3.1 %collective-permute-start = (f32[128,128]{1,0:T(8,128)S(1)}, f32[128,128]{1,0:T(8,128)S(1)}, u32[]{:S(2)}, u32[]{:S(2)}) collective-permute-start(f32[128,128]{1,0:T(8,128)S(1)} %constant_dynamic-slice_fusion), channel_id=1, source_target_pairs={{0,0},{1,16},{2,32},{3,48},{4,64},{5,80},{6,96},{7,112},{8,8},{9,2... | collective-permute-start | bytes 196616 | tf_op jit(solution)/shard_map/ppermute | solution.py:205
  16.5 0.8 dynamic-slice_bitcast_fusion.persist_ref
  17.2 0.0 copy-start.1
  17.2 3.5 %collective-permute-done.decay_ref = f32[128,128]{1,0:T(8,128)S(1)} collective-permute-done((f32[128,128]{1,0:T(8,128)S(1)}, f32[128,128]{1,0:T(8,128)S(1)}, u32[]{:S(2)}, u32[]{:S(2)}) %collective-permute-start) | collective-permute-done | bytes 65568 | tf_op jit(solution)/shard_map/ppermute | solution.py:205
  20.8 12.4 %all-to-all-done.got_ref = bf16[32,16,1280]{2,1,0:T(8,128)(2,1)S(1)} async-done(((bf16[32,16,1280]{2,1,0:T(8,128)(2,1)}), bf16[32,16,1280]{2,1,0:T(8,128)(2,1)S(1)}, u32[]{:S(2)}, u32[]{:S(2)}) %all-to-all-start) | async-done | bytes 1310752 | tf_op jit(solution)/shard_map/all_to_all | solution.py:203
  33.2 1.3 drive.1
  34.4 13.8 %all-to-all-start.1 = ((bf16[16,128,128]{2,1,0:T(8,128)(2,1)}), bf16[16,128,128]{2,1,0:T(8,128)(2,1)S(1)}, u32[]{:S(2)}, u32[]{:S(2)}) async-start(bf16[16,128,128]{2,1,0:T(8,128)(2,1)} %bitcast.2), calls=%async_computation.1 | async-start | bytes 1048576 | tf_op jit(solution)/shard_map/all_to_all | solution.py:210
  48.2 0.0 copy-done.1
  48.2 19.0 %all_gather.3.near_ref = bf16[256,1024]{1,0:T(8,128)(2,1)S(1)} all-gather(bf16[16,1024]{1,0:T(8,128)(2,1)S(1)} %copy-done.1), channel_id=1, replica_groups=mesh['x'=4,'zh'=8,'zl'=2,'y'=4,'core'=2] {'x','y'}, dimensions={0}, use_global_device_ids=true | all-gather | bytes 557056 | tf_op jit(solution)/shard_map/all_gather | solution.py:212
  67.2 3.9 %all-to-all-done.1.parts_ref = bf16[16,128,128]{2,1,0:T(8,128)(2,1)S(1)} async-done(((bf16[16,128,128]{2,1,0:T(8,128)(2,1)}), bf16[16,128,128]{2,1,0:T(8,128)(2,1)S(1)}, u32[]{:S(2)}, u32[]{:S(2)}) %all-to-all-start.1) | async-done | bytes 524320 | tf_op jit(solution)/shard_map/all_to_all | solution.py:210
  71.1 1.0 scan.1
  72.0 13.6 %all-to-all-start.2 = ((f32[64,8,128]{2,1,0:T(8,128)}), f32[64,8,128]{2,1,0:T(8,128)S(1)}, u32[]{:S(2)}, u32[]{:S(2)}) async-start(f32[64,8,128]{2,1,0:T(8,128)} %get-tuple-element.26), calls=%async_computation.2 | async-start | bytes 524288 | tf_op jit(solution)/shard_map/all_to_all | solution.py:221
  85.6 2.4 %collective-permute-start.1 = (bf16[256,1024]{1,0:T(8,128)(2,1)S(1)}, bf16[256,1024]{1,0:T(8,128)(2,1)S(1)}, u32[]{:S(2)}, u32[]{:S(2)}) collective-permute-start(bf16[256,1024]{1,0:T(8,128)(2,1)S(1)} %all_gather.3.near_ref), channel_id=1, source_target_pairs={{0,1},{1,0},{2,3},{3,2},{4,5},{5,4},{6,7},{7,6},{8,9},{9,8},{10,11... | collective-permute-start | bytes 1572872 | tf_op jit(solution)/shard_map/ppermute | solution.py:214
  88.0 3.2 %collective-permute-start.2 = (bf16[256,1024]{1,0:T(8,128)(2,1)S(1)}, bf16[256,1024]{1,0:T(8,128)(2,1)S(1)}, u32[]{:S(2)}, u32[]{:S(2)}) collective-permute-start(bf16[256,1024]{1,0:T(8,128)(2,1)S(1)} %all_gather.3.near_ref), channel_id=1, source_target_pairs={{0,8},{8,0},{1,9},{9,1},{2,10},{10,2},{3,11},{11,3},{4,12},{12,4},... | collective-permute-start | bytes 1572872 | tf_op jit(solution)/shard_map/ppermute | solution.py:214
  91.2 0.0 collective-permute-done.1.far_ref
  91.2 12.2 %collective-permute-done.2.pair_near_ref = bf16[256,1024]{1,0:T(8,128)(2,1)S(1)} collective-permute-done((bf16[256,1024]{1,0:T(8,128)(2,1)S(1)}, bf16[256,1024]{1,0:T(8,128)(2,1)S(1)}, u32[]{:S(2)}, u32[]{:S(2)}) %collective-permute-start.2) | collective-permute-done | bytes 524320 | tf_op jit(solution)/shard_map/ppermute | solution.py:214
  103.4 0.0 all-to-all-done.2.slabs_ref
  103.4 1.1 finish.1
  104.4 5.0 %all-to-all-start.3 = ((bf16[8,128,128]{2,1,0:T(8,128)(2,1)}), bf16[8,128,128]{2,1,0:T(8,128)(2,1)S(1)}, u32[]{:S(2)}, u32[]{:S(2)}) async-start(bf16[8,128,128]{2,1,0:T(8,128)(2,1)} %get-tuple-element.32), calls=%async_computation.3 | async-start | bytes 524288 | tf_op jit(solution)/shard_map/all_to_all | solution.py:229
  109.4 3.0 %collective-permute-start.3 = (bf16[256,1024]{1,0:T(8,128)(2,1)S(1)}, bf16[256,1024]{1,0:T(8,128)(2,1)S(1)}, u32[]{:S(2)}, u32[]{:S(2)}) collective-permute-start(bf16[256,1024]{1,0:T(8,128)(2,1)S(1)} %collective-permute-done.2.pair_near_ref), channel_id=1, source_target_pairs={{0,1},{1,0},{2,3},{3,2},{4,5},{5,4},{6,7},{7,6},{8,9},{9,8},{10,11... | collective-permute-start | bytes 1572872 | tf_op jit(solution)/shard_map/ppermute | solution.py:230
  112.5 4.4 %collective-permute-start.4 = (bf16[128,128]{1,0:T(8,128)(2,1)S(1)}, bf16[128,128]{1,0:T(8,128)(2,1)S(1)}, u32[]{:S(2)}, u32[]{:S(2)}) collective-permute-start(bf16[128,128]{1,0:T(8,128)(2,1)S(1)} %get-tuple-element.34), channel_id=1, source_target_pairs={{0,0},{1,16},{2,32},{3,48},{4,64},{5,80},{6,96},{7,112},{8,8},{9,2... | collective-permute-start | bytes 98312 | tf_op jit(solution)/shard_map/ppermute | solution.py:231
  116.9 0.1 pad_add_fusion.where_ref
  117.0 4.7 %collective-permute-done.4 = bf16[128,128]{1,0:T(8,128)(2,1)S(1)} collective-permute-done((bf16[128,128]{1,0:T(8,128)(2,1)S(1)}, bf16[128,128]{1,0:T(8,128)(2,1)S(1)}, u32[]{:S(2)}, u32[]{:S(2)}) %collective-permute-start.4) | collective-permute-done | bytes 32800 | tf_op jit(solution)/shard_map/ppermute | solution.py:231
  121.7 0.0 collective-permute-done.3.pair_far_ref
  121.7 4.3 %all-to-all-done.3.states_ref = bf16[8,128,128]{2,1,0:T(8,128)(2,1)S(1)} async-done(((bf16[8,128,128]{2,1,0:T(8,128)(2,1)}), bf16[8,128,128]{2,1,0:T(8,128)(2,1)S(1)}, u32[]{:S(2)}, u32[]{:S(2)}) %all-to-all-start.3) | async-done | bytes 262176 | tf_op jit(solution)/shard_map/all_to_all | solution.py:229
  125.9 2.0 %predict.1 = bf16[16,2,2,16,128]{4,3,2,1,0:T(8,128)(2,1)} custom-call(s32[2]{0:T(128)S(1)} %pad_add_fusion.where_ref, bf16[256,1024]{1,0:T(8,128)(2,1)S(1)} %all_gather.3.near_ref, bf16[256,1024]{1,0:T(8,128)(2,1)S(1)} %collective-permute-done.1.far_ref, bf16[256,1024]{1,0:T(8,128)(2,1)S(1)} %collective-permute-done.2.pair_near_ref, ...), custom_call_target="tpu_custom_call" | custom-call | tf_op jit(solution)/shard_map/predict/pallas_call | solution.py:166
  127.9 15.6 %all-to-all-start.4 = ((bf16[64,16,128]{2,1,0:T(8,128)(2,1)}), bf16[64,16,128]{2,1,0:T(8,128)(2,1)S(1)}, u32[]{:S(2)}, u32[]{:S(2)}) async-start(bf16[64,16,128]{2,1,0:T(8,128)(2,1)} %bitcast.5), calls=%async_computation.4 | async-start | bytes 524288 | tf_op jit(solution)/shard_map/all_to_all | solution.py:240
  143.5 0.6 convert_element_type.3
  144.1 9.0 %all-to-all-done.4 = bf16[64,16,128]{2,1,0:T(8,128)(2,1)S(1)} async-done(((bf16[64,16,128]{2,1,0:T(8,128)(2,1)}), bf16[64,16,128]{2,1,0:T(8,128)(2,1)S(1)}, u32[]{:S(2)}, u32[]{:S(2)}) %all-to-all-start.4) | async-done | bytes 262176 | tf_op jit(solution)/shard_map/all_to_all | solution.py:240
  153.1 0.7 copy_bitcast_fusion
  (1 shorter events, 0.0 us)
Async XLA Ops:
  0.6 12.7 %copy-start = (f32[128,1024]{1,0:T(8,128)S(1)}, f32[128,1024]{1,0:T(8,128)}, u32[]{:S(2)}) copy-start(f32[128,1024]{1,0:T(8,128)} %param.12) | copy-start | bytes 1572868
  2.8 30.4 %all-to-all-start = ((bf16[32,16,1280]{2,1,0:T(8,128)(2,1)}), bf16[32,16,1280]{2,1,0:T(8,128)(2,1)S(1)}, u32[]{:S(2)}, u32[]{:S(2)}) async-start(bf16[32,16,1280]{2,1,0:T(8,128)(2,1)} %front.1), calls=%async_computation | async-start | bytes 2621440 | tf_op jit(solution)/shard_map/all_to_all | solution.py:203
  13.3 7.4 %collective-permute-start = (f32[128,128]{1,0:T(8,128)S(1)}, f32[128,128]{1,0:T(8,128)S(1)}, u32[]{:S(2)}, u32[]{:S(2)}) collective-permute-start(f32[128,128]{1,0:T(8,128)S(1)} %constant_dynamic-slice_fusion), channel_id=1, source_target_pairs={{0,0},{1,16},{2,32},{3,48},{4,64},{5,80},{6,96},{7,112},{8,8},{9,2... | collective-permute-start | bytes 196616 | tf_op jit(solution)/shard_map/ppermute | solution.py:205
  17.2 31.0 %copy-start.1 = (bf16[16,1024]{1,0:T(8,128)(2,1)S(1)}, bf16[16,1024]{1,0:T(8,128)(2,1)}, u32[]{:S(2)}) copy-start(bf16[16,1024]{1,0:T(8,128)(2,1)} %param.11) | copy-start | bytes 98308
  34.4 36.6 %all-to-all-start.1 = ((bf16[16,128,128]{2,1,0:T(8,128)(2,1)}), bf16[16,128,128]{2,1,0:T(8,128)(2,1)S(1)}, u32[]{:S(2)}, u32[]{:S(2)}) async-start(bf16[16,128,128]{2,1,0:T(8,128)(2,1)} %bitcast.2), calls=%async_computation.1 | async-start | bytes 1048576 | tf_op jit(solution)/shard_map/all_to_all | solution.py:210
  72.0 31.3 %all-to-all-start.2 = ((f32[64,8,128]{2,1,0:T(8,128)}), f32[64,8,128]{2,1,0:T(8,128)S(1)}, u32[]{:S(2)}, u32[]{:S(2)}) async-start(f32[64,8,128]{2,1,0:T(8,128)} %get-tuple-element.26), calls=%async_computation.2 | async-start | bytes 524288 | tf_op jit(solution)/shard_map/all_to_all | solution.py:221
  85.6 5.6 %collective-permute-start.1 = (bf16[256,1024]{1,0:T(8,128)(2,1)S(1)}, bf16[256,1024]{1,0:T(8,128)(2,1)S(1)}, u32[]{:S(2)}, u32[]{:S(2)}) collective-permute-start(bf16[256,1024]{1,0:T(8,128)(2,1)S(1)} %all_gather.3.near_ref), channel_id=1, source_target_pairs={{0,1},{1,0},{2,3},{3,2},{4,5},{5,4},{6,7},{7,6},{8,9},{9,8},{10,11... | collective-permute-start | bytes 1572872 | tf_op jit(solution)/shard_map/ppermute | solution.py:214
  88.0 15.4 %collective-permute-start.2 = (bf16[256,1024]{1,0:T(8,128)(2,1)S(1)}, bf16[256,1024]{1,0:T(8,128)(2,1)S(1)}, u32[]{:S(2)}, u32[]{:S(2)}) collective-permute-start(bf16[256,1024]{1,0:T(8,128)(2,1)S(1)} %all_gather.3.near_ref), channel_id=1, source_target_pairs={{0,8},{8,0},{1,9},{9,1},{2,10},{10,2},{3,11},{11,3},{4,12},{12,4},... | collective-permute-start | bytes 1572872 | tf_op jit(solution)/shard_map/ppermute | solution.py:214
  104.4 21.5 %all-to-all-start.3 = ((bf16[8,128,128]{2,1,0:T(8,128)(2,1)}), bf16[8,128,128]{2,1,0:T(8,128)(2,1)S(1)}, u32[]{:S(2)}, u32[]{:S(2)}) async-start(bf16[8,128,128]{2,1,0:T(8,128)(2,1)} %get-tuple-element.32), calls=%async_computation.3 | async-start | bytes 524288 | tf_op jit(solution)/shard_map/all_to_all | solution.py:229
  109.4 12.2 %collective-permute-start.3 = (bf16[256,1024]{1,0:T(8,128)(2,1)S(1)}, bf16[256,1024]{1,0:T(8,128)(2,1)S(1)}, u32[]{:S(2)}, u32[]{:S(2)}) collective-permute-start(bf16[256,1024]{1,0:T(8,128)(2,1)S(1)} %collective-permute-done.2.pair_near_ref), channel_id=1, source_target_pairs={{0,1},{1,0},{2,3},{3,2},{4,5},{5,4},{6,7},{7,6},{8,9},{9,8},{10,11... | collective-permute-start | bytes 1572872 | tf_op jit(solution)/shard_map/ppermute | solution.py:230
  112.5 9.2 %collective-permute-start.4 = (bf16[128,128]{1,0:T(8,128)(2,1)S(1)}, bf16[128,128]{1,0:T(8,128)(2,1)S(1)}, u32[]{:S(2)}, u32[]{:S(2)}) collective-permute-start(bf16[128,128]{1,0:T(8,128)(2,1)S(1)} %get-tuple-element.34), channel_id=1, source_target_pairs={{0,0},{1,16},{2,32},{3,48},{4,64},{5,80},{6,96},{7,112},{8,8},{9,2... | collective-permute-start | bytes 98312 | tf_op jit(solution)/shard_map/ppermute | solution.py:231
  127.9 25.2 %all-to-all-start.4 = ((bf16[64,16,128]{2,1,0:T(8,128)(2,1)}), bf16[64,16,128]{2,1,0:T(8,128)(2,1)S(1)}, u32[]{:S(2)}, u32[]{:S(2)}) async-start(bf16[64,16,128]{2,1,0:T(8,128)(2,1)} %bitcast.5), calls=%async_computation.4 | async-start | bytes 524288 | tf_op jit(solution)/shard_map/all_to_all | solution.py:240

commit v7 on v4

--- a/solution.py
+++ b/solution.py
@@ -148,15 +148,16 @@
 
 def predict_kernel(where_ref, near_ref, far_ref, mine_ref, pair_ref, out_ref):
     blocks, share, slab = mine_ref.shape
-    pairs, _, sites, span = out_ref.shape
-    first, core = where_ref[0] == 0, where_ref[1]
+    nx, ny, cores, sites, span = out_ref.shape
+    first, core, y = where_ref[0] == 0, where_ref[1], where_ref[2]
     mine, pair = mine_ref[...].reshape(blocks * share, slab), pair_ref[...].reshape(blocks * share, slab)
     states = jnp.concatenate([jnp.where(first, mine, pair), jnp.where(first, pair, mine)], axis=1)
     loadings = jnp.concatenate([near_ref[...], far_ref[...]], axis=0)
     predicted = jnp.dot(loadings, states, preferred_element_type=jnp.float32)
-    predicted = predicted.astype(out_ref.dtype).reshape(2, pairs, sites, span)
-    for other in range(2):
-        out_ref[:, core ^ other] = predicted[other]
+    predicted = predicted.astype(out_ref.dtype).reshape(cores, nx, ny, sites, span)
+    for other in range(cores):
+        for step in range(ny):
+            out_ref[:, y ^ step, core ^ other] = predicted[other, :, step]
 
 
 def call(kernel, name, out_shape, *args, scratch=(), scalars=0, vmem=32, **grid):
@@ -205,16 +206,19 @@
     own = lax.dynamic_slice_in_dim(decay, lax.axis_index(col) * share, share, 1)
     decays = lax.ppermute(own, planes + col, turn)
     persist = lax.dynamic_slice_in_dim(persistence, lax.axis_index("zh") * share, share, 0)[None]
-    got, decays, persist = lax.optimization_barrier((got, decays, persist))
+    ny, cores = lax.axis_size("y"), lax.axis_size("core")
+    near = [site_loading]
+    near += [lax.ppermute(site_loading, "y", [(i, i ^ step) for i in range(ny)]) for step in range(1, ny)]
+    got, decays, persist, *near = lax.optimization_barrier((got, decays, persist, *near))
 
     part = lax.axis_index("zl").astype(jnp.int32)
+    swap = [(0, 1), (1, 0)]
     both = (shape((blocks, slab, share), f32), shape((blocks, slab, share), bf16))
     keep, give = call(drive_kernel, "drive", both, part[None], got, scalars=1)
-    taken = lax.ppermute(give, "zl", [(0, 1), (1, 0)])
-    taken, near = lax.optimization_barrier((taken, site_loading))
+    taken, near = lax.optimization_barrier((lax.ppermute(give, "zl", swap), jnp.concatenate(near)))
     halves = (keep + taken.astype(f32)).astype(bf16)
     summed = lax.all_to_all(halves, "zh", 0, 0, tiled=True)
-    near = lax.all_gather(near, "y", axis=0, tiled=True)
+    near = lax.all_gather(near, "x", axis=0, tiled=True)
     summed, near = lax.optimization_barrier((summed, near))
     square = shape((slab, share), f32)
     smooth, entry, product, summary = call(
@@ -222,7 +226,8 @@
         scratch=[pltpu.VMEM((slab, share), f32)],
     )
     summaries = lax.all_to_all(summary, line, 0, 0, tiled=True)
-    summaries, near = lax.optimization_barrier((summaries, near))
+    far = lax.ppermute(near, "core", swap)
+    summaries, near, far = lax.optimization_barrier((summaries, near, far))
     rounded = call(
         finish_kernel, "finish", shape((blocks, share, slab), bf16),
         lax.axis_index(line).astype(jnp.int32)[None], summaries, smooth, entry, product,
@@ -230,16 +235,12 @@
     )
 
     mine = lax.all_to_all(rounded, "zh", 0, 0, tiled=True)
-    near = lax.all_gather(near, "x", axis=0, tiled=True)
-    mine, near = lax.optimization_barrier((mine, near))
-    far = lax.ppermute(near, "core", [(0, 1), (1, 0)])
-    pair = lax.ppermute(mine, "zl", [(0, 1), (1, 0)])
+    pair = lax.ppermute(mine, "zl", swap)
     own = lax.all_to_all(mine, col, 0, 0, tiled=True)
 
-    cores = lax.axis_size("core")
-    where = jnp.stack([part, lax.axis_index("core").astype(jnp.int32)])
+    where = jnp.stack([part, lax.axis_index("core").astype(jnp.int32), lax.axis_index("y").astype(jnp.int32)])
     predicted = call(
-        predict_kernel, "predict", shape((devices // cores, cores, sites, span), bf16),
+        predict_kernel, "predict", shape((devices // cores // ny, ny, cores, sites, span), bf16),
         where, near, far, mine, pair, scalars=1,
     )
     predicted, own = lax.optimization_barrier((predicted, own))

time: 152 us -> 156 us (1.026)
  waiting for transfers between devices: 60.3 us -> 40.8 us
  blocking collectives: 19.9 us -> 33.9 us
  starting transfers between devices: 60.3 us -> 69.9 us
    all_to_all x0 -> x1, blocking collectives: none -> 23.9 us  [per_device(): mine = lax.all_to_all(rounded, 'zh', 0, 0, tiled=True)]
    all_to_all x1, waiting for transfers between devices: 12.4 us -> 0.01 us  [per_device(): got = lax.all_to_all(sent, plane, 0, 0, tiled=True)]
    all_gather x1 -> x0, blocking collectives: 9.4 us -> none  [per_device(): near = lax.all_gather(near, 'y', axis=0, tiled=True)]
    all_to_all x1 -> x0, waiting for transfers between devices: 7.28 us -> none  [per_device(): mine = lax.all_to_all(rounded, 'zh', 0, 0, tiled=True)]
    ppermute x3 -> x6, starting transfers between devices: 9.67 us -> 15.8 us  [the longest x3 9.58 us: per_device(): lax.ppermute(site_loading, 'y', [(i, i ^ step) for i in range(ny)])]
    all_to_all x1, starting transfers between devices: 3.4 us -> 7.84 us  [per_device(): own = lax.all_to_all(mine, col, 0, 0, tiled=True)]
    all_to_all x1, waiting for transfers between devices: 0.01 us -> 4.33 us  [per_device(): own = lax.all_to_all(mine, col, 0, 0, tiled=True)]
    all_to_all x1 -> x0, starting transfers between devices: 4.05 us -> none  [per_device(): mine = lax.all_to_all(rounded, 'zh', 0, 0, tiled=True)]
  transfers between devices with their start and end apart: 10 -> 12, of which waited for: 8 -> 8; matrix products, arithmetic and copies ran while one was open for 1% -> 1% of each run, Pallas kernels for 1% -> 1%
where the time goes in v7:
time: 156 us; the launch traced here: 155 us
  starting transfers between devices  69.9 us (45%)
  waiting for transfers between devices  40.8 us (26%)
  blocking collectives  33.9 us (22%)
  Pallas kernels  6 us (4%)
  local copies, waits for them, and re-layouts  2.25 us (1%)
    all_to_all x1, blocking collectives, per_device(): mine = lax.all_to_all(rounded, 'zh', 0, 0, tiled=True)  23.9 us
    all_to_all x1, starting transfers between devices, per_device(): summed = lax.all_to_all(halves, 'zh', 0, 0, tiled=True)  15.6 us
    all_to_all x1, starting transfers between devices, per_device(): summaries = lax.all_to_all(summary, line, 0, 0, tiled=True)  11.4 us
    all_to_all x1, starting transfers between devices, per_device(): got = lax.all_to_all(sent, plane, 0, 0, tiled=True)  10.5 us
    all_gather x1, blocking collectives, per_device(): near = lax.all_gather(near, 'x', axis=0, tiled=True)  10 us
    ppermute x3, starting transfers between devices, per_device(): lax.ppermute(site_loading, 'y', [(i, i ^ step) for i in range(ny)])  9.58 us
    ppermute x1, waiting for transfers between devices, per_device(): lax.ppermute(give, 'zl', swap)  8.73 us
    all_to_all x1, waiting for transfers between devices, per_device(): lax.all_to_all(predicted.reshape(devices, sites, span), plane, 0, 0, tile...  8.23 us
  transfers between devices with their start and end apart: 12, of which 8 were waited for; matrix products, arithmetic and copies ran while one was open for 1% of the time, Pallas kernels for 1%

profile of v7, /device:TPU:1, one launch (start us, length us, event | category | flops | bytes accessed | tf_op | source)
XLA Modules:
  0.0 154.6 jit_solution(6073801419482102462)
XLA Ops:
  0.6 0.0 copy-start
  0.6 2.1 %front.1 = bf16[32,16,1280]{2,1,0:T(8,128)(2,1)} custom-call(s32[16]{0:T(128)} %start_hbm.1, s32[16]{0:T(128)} %count_hbm.1, bf16[16,8192]{1,0:T(8,128)(2,1)} %values_hbm.1, bf16[16,1024]{1,0:T(8,128)(2,1)} %gain_hbm.1), custom_call_target="tpu_custom_call" | custom-call | tf_op jit(solution)/shard_map/front/pallas_call | solution.py:168
  2.8 0.0 copy-start.1
  2.8 10.5 %all-to-all-start = ((bf16[32,16,1280]{2,1,0:T(8,128)(2,1)}), bf16[32,16,1280]{2,1,0:T(8,128)(2,1)S(1)}, u32[]{:S(2)}, u32[]{:S(2)}) async-start(bf16[32,16,1280]{2,1,0:T(8,128)(2,1)} %front.1), calls=%async_computation | async-start | bytes 2621440 | tf_op jit(solution)/shard_map/all_to_all | solution.py:205
  13.3 0.0 copy-done.1
  13.3 3.3 %collective-permute-start.1 = (bf16[16,1024]{1,0:T(8,128)(2,1)S(1)}, bf16[16,1024]{1,0:T(8,128)(2,1)S(1)}, u32[]{:S(2)}, u32[]{:S(2)}) collective-permute-start(bf16[16,1024]{1,0:T(8,128)(2,1)S(1)} %copy-done.1), channel_id=1, source_target_pairs={{0,2},{2,0},{4,6},{6,4},{1,3},{3,1},{5,7},{7,5},{8,10},{10,8},{12,... | collective-permute-start | bytes 98312 | tf_op jit(solution)/shard_map/ppermute | solution.py:211
  16.6 4.3 %collective-permute-start.2 = (bf16[16,1024]{1,0:T(8,128)(2,1)S(1)}, bf16[16,1024]{1,0:T(8,128)(2,1)S(1)}, u32[]{:S(2)}, u32[]{:S(2)}) collective-permute-start(bf16[16,1024]{1,0:T(8,128)(2,1)S(1)} %copy-done.1), channel_id=1, source_target_pairs={{0,4},{2,6},{4,0},{6,2},{1,5},{3,7},{5,1},{7,3},{8,12},{10,14},{12... | collective-permute-start | bytes 98312 | tf_op jit(solution)/shard_map/ppermute | solution.py:211
  21.0 2.0 %collective-permute-start.3 = (bf16[16,1024]{1,0:T(8,128)(2,1)S(1)}, bf16[16,1024]{1,0:T(8,128)(2,1)S(1)}, u32[]{:S(2)}, u32[]{:S(2)}) collective-permute-start(bf16[16,1024]{1,0:T(8,128)(2,1)S(1)} %copy-done.1), channel_id=1, source_target_pairs={{0,6},{2,4},{4,2},{6,0},{1,7},{3,5},{5,3},{7,1},{8,14},{10,12},{12... | collective-permute-start | bytes 98312 | tf_op jit(solution)/shard_map/ppermute | solution.py:211
  22.9 0.0 copy-done
  23.0 4.0 %collective-permute-start = (f32[128,128]{1,0:T(8,128)S(1)}, f32[128,128]{1,0:T(8,128)S(1)}, u32[]{:S(2)}, u32[]{:S(2)}) collective-permute-start(f32[128,128]{1,0:T(8,128)S(1)} %constant_dynamic-slice_fusion), channel_id=1, source_target_pairs={{0,0},{1,16},{2,32},{3,48},{4,64},{5,80},{6,96},{7,112},{8,8},{9,2... | collective-permute-start | bytes 196616 | tf_op jit(solution)/shard_map/ppermute | solution.py:207
  26.9 0.8 dynamic-slice_bitcast_fusion.persist_ref
  27.7 0.9 collective-permute-done.1
  28.6 0.0 collective-permute-done.2
  28.6 4.9 %collective-permute-done.3 = bf16[16,1024]{1,0:T(8,128)(2,1)S(1)} collective-permute-done((bf16[16,1024]{1,0:T(8,128)(2,1)S(1)}, bf16[16,1024]{1,0:T(8,128)(2,1)S(1)}, u32[]{:S(2)}, u32[]{:S(2)}) %collective-permute-start.3) | collective-permute-done | bytes 32800 | tf_op jit(solution)/shard_map/ppermute | solution.py:211
  33.5 0.0 collective-permute-done.decay_ref
  33.5 0.0 all-to-all-done.got_ref
  33.5 0.5 drive.1
  34.0 1.9 %collective-permute-start.4 = (bf16[8,128,128]{2,1,0:T(8,128)(2,1)S(1)}, bf16[8,128,128]{2,1,0:T(8,128)(2,1)S(1)}, u32[]{:S(2)}, u32[]{:S(2)}) collective-permute-start(bf16[8,128,128]{2,1,0:T(8,128)(2,1)S(1)} %get-tuple-element.26), channel_id=1, source_target_pairs={{0,8},{8,0},{1,9},{9,1},{2,10},{10,2},{3,11},{11,3},{4,12},{12,4},... | collective-permute-start | bytes 786440 | tf_op jit(solution)/shard_map/ppermute | solution.py:218
  35.9 8.7 %collective-permute-done.4 = bf16[8,128,128]{2,1,0:T(8,128)(2,1)S(1)} collective-permute-done((bf16[8,128,128]{2,1,0:T(8,128)(2,1)S(1)}, bf16[8,128,128]{2,1,0:T(8,128)(2,1)S(1)}, u32[]{:S(2)}, u32[]{:S(2)}) %collective-permute-start.4) | collective-permute-done | bytes 262176 | tf_op jit(solution)/shard_map/ppermute | solution.py:218
  44.7 0.8 add_convert_fusion
  45.4 15.6 %all-to-all-start.1 = ((bf16[8,128,128]{2,1,0:T(8,128)(2,1)}), bf16[8,128,128]{2,1,0:T(8,128)(2,1)S(1)}, u32[]{:S(2)}, u32[]{:S(2)}) async-start(bf16[8,128,128]{2,1,0:T(8,128)(2,1)} %add_convert_fusion), calls=%async_computation.1 | async-start | bytes 524288 | tf_op jit(solution)/shard_map/all_to_all | solution.py:220
  61.1 10.0 %all_gather.3.near_ref = bf16[256,1024]{1,0:T(8,128)(2,1)S(1)} all-gather(bf16[64,1024]{1,0:T(8,128)(2,1)S(1)} %pad_maximum_fusion), channel_id=1, replica_groups=mesh['x'=4,'zh'=8,'zl'=2,'y'=4,'core'=2] {'x'}, dimensions={0}, use_global_device_ids=true | all-gather | bytes 655360 | tf_op jit(solution)/shard_map/all_gather | solution.py:221
  71.1 6.5 %all-to-all-done.1.parts_ref = bf16[8,128,128]{2,1,0:T(8,128)(2,1)S(1)} async-done(((bf16[8,128,128]{2,1,0:T(8,128)(2,1)}), bf16[8,128,128]{2,1,0:T(8,128)(2,1)S(1)}, u32[]{:S(2)}, u32[]{:S(2)}) %all-to-all-start.1) | async-done | bytes 262176 | tf_op jit(solution)/shard_map/all_to_all | solution.py:220
  77.6 0.9 scan.1
  78.5 11.4 %all-to-all-start.2 = ((f32[64,8,128]{2,1,0:T(8,128)}), f32[64,8,128]{2,1,0:T(8,128)S(1)}, u32[]{:S(2)}, u32[]{:S(2)}) async-start(f32[64,8,128]{2,1,0:T(8,128)} %get-tuple-element.36), calls=%async_computation.2 | async-start | bytes 524288 | tf_op jit(solution)/shard_map/all_to_all | solution.py:228
  90.0 2.4 %collective-permute-start.5 = (bf16[256,1024]{1,0:T(8,128)(2,1)S(1)}, bf16[256,1024]{1,0:T(8,128)(2,1)S(1)}, u32[]{:S(2)}, u32[]{:S(2)}) collective-permute-start(bf16[256,1024]{1,0:T(8,128)(2,1)S(1)} %all_gather.3.near_ref), channel_id=1, source_target_pairs={{0,1},{1,0},{2,3},{3,2},{4,5},{5,4},{6,7},{7,6},{8,9},{9,8},{10,11... | collective-permute-start | bytes 1572872 | tf_op jit(solution)/shard_map/ppermute | solution.py:229
  92.3 1.5 collective-permute-done.5.far_ref
  93.8 5.7 %all-to-all-done.2.slabs_ref = f32[64,8,128]{2,1,0:T(8,128)S(1)} async-done(((f32[64,8,128]{2,1,0:T(8,128)}), f32[64,8,128]{2,1,0:T(8,128)S(1)}, u32[]{:S(2)}, u32[]{:S(2)}) %all-to-all-start.2) | async-done | bytes 262176 | tf_op jit(solution)/shard_map/all_to_all | solution.py:228
  99.6 0.4 finish.1
  100.0 23.9 %all_to_all.30.mine_ref = bf16[8,128,128]{2,1,0:T(8,128)(2,1)} all-to-all(bf16[8,128,128]{2,1,0:T(8,128)(2,1)S(1)} %finish.1), channel_id=1, replica_groups=mesh['x'=4,'zh'=8,'zl'=2,'y'=4,'core'=2] {'zh'}, dimensions={0} | all-to-all | bytes 524288 | tf_op jit(solution)/shard_map/all_to_all | solution.py:237
  123.9 1.9 %collective-permute-start.6 = (bf16[8,128,128]{2,1,0:T(8,128)(2,1)}, bf16[8,128,128]{2,1,0:T(8,128)(2,1)S(1)}, u32[]{:S(2)}, u32[]{:S(2)}) collective-permute-start(bf16[8,128,128]{2,1,0:T(8,128)(2,1)} %all_to_all.30.mine_ref), channel_id=1, source_target_pairs={{0,8},{8,0},{1,9},{9,1},{2,10},{10,2},{3,11},{11,3},{4,12},{12,4},... | collective-permute-start | bytes 786440 | tf_op jit(solution)/shard_map/ppermute | solution.py:238
  125.8 7.8 %all-to-all-start.4 = ((bf16[8,128,128]{2,1,0:T(8,128)(2,1)}), bf16[8,128,128]{2,1,0:T(8,128)(2,1)S(1)}, u32[]{:S(2)}, u32[]{:S(2)}) async-start(bf16[8,128,128]{2,1,0:T(8,128)(2,1)} %all_to_all.30.mine_ref), calls=%async_computation.4 | async-start | bytes 524288 | tf_op jit(solution)/shard_map/all_to_all | solution.py:239
  133.6 0.1 pad_add_fusion.where_ref
  133.7 0.0 collective-permute-done.6.pair_ref
  133.7 2.1 %predict.1 = bf16[4,4,2,16,256]{4,3,2,1,0:T(8,128)(2,1)} custom-call(s32[3]{0:T(128)S(1)} %pad_add_fusion.where_ref, bf16[256,1024]{1,0:T(8,128)(2,1)S(1)} %all_gather.3.near_ref, bf16[256,1024]{1,0:T(8,128)(2,1)S(1)} %collective-permute-done.5.far_ref, bf16[8,128,128]{2,1,0:T(8,128)(2,1)} %all_to_all.30.mine_ref, ...), custom_call_target="tpu_custom_call" | custom-call | tf_op jit(solution)/shard_map/predict/pallas_call | solution.py:168
  135.8 4.3 %all-to-all-done.4 = bf16[8,128,128]{2,1,0:T(8,128)(2,1)S(1)} async-done(((bf16[8,128,128]{2,1,0:T(8,128)(2,1)}), bf16[8,128,128]{2,1,0:T(8,128)(2,1)S(1)}, u32[]{:S(2)}, u32[]{:S(2)}) %all-to-all-start.4) | async-done | bytes 262176 | tf_op jit(solution)/shard_map/all_to_all | solution.py:239
  140.1 4.8 %all-to-all-start.5 = ((bf16[32,16,256]{2,1,0:T(8,128)(2,1)}), bf16[32,16,256]{2,1,0:T(8,128)(2,1)S(1)}, u32[]{:S(2)}, u32[]{:S(2)}) async-start(bf16[32,16,256]{2,1,0:T(8,128)(2,1)} %bitcast.7), calls=%async_computation.5 | async-start | bytes 524288 | tf_op jit(solution)/shard_map/all_to_all | solution.py:248
  145.0 0.7 copy.10
  145.7 8.2 %all-to-all-done.5 = bf16[32,16,256]{2,1,0:T(8,128)(2,1)S(1)} async-done(((bf16[32,16,256]{2,1,0:T(8,128)(2,1)}), bf16[32,16,256]{2,1,0:T(8,128)(2,1)S(1)}, u32[]{:S(2)}, u32[]{:S(2)}) %all-to-all-start.5) | async-done | bytes 262176 | tf_op jit(solution)/shard_map/all_to_all | solution.py:248
  153.9 0.7 copy.11
  (3 shorter events, 0.0 us)
Async XLA Ops:
  0.6 22.3 %copy-start = (f32[128,1024]{1,0:T(8,128)S(1)}, f32[128,1024]{1,0:T(8,128)}, u32[]{:S(2)}) copy-start(f32[128,1024]{1,0:T(8,128)} %param.12) | copy-start | bytes 1572868
  2.8 10.5 %copy-start.1 = (bf16[16,1024]{1,0:T(8,128)(2,1)S(1)}, bf16[16,1024]{1,0:T(8,128)(2,1)}, u32[]{:S(2)}) copy-start(bf16[16,1024]{1,0:T(8,128)(2,1)} %param.11) | copy-start | bytes 98308
  2.8 30.7 %all-to-all-start = ((bf16[32,16,1280]{2,1,0:T(8,128)(2,1)}), bf16[32,16,1280]{2,1,0:T(8,128)(2,1)S(1)}, u32[]{:S(2)}, u32[]{:S(2)}) async-start(bf16[32,16,1280]{2,1,0:T(8,128)(2,1)} %front.1), calls=%async_computation | async-start | bytes 2621440 | tf_op jit(solution)/shard_map/all_to_all | solution.py:205
  13.3 15.3 %collective-permute-start.1 = (bf16[16,1024]{1,0:T(8,128)(2,1)S(1)}, bf16[16,1024]{1,0:T(8,128)(2,1)S(1)}, u32[]{:S(2)}, u32[]{:S(2)}) collective-permute-start(bf16[16,1024]{1,0:T(8,128)(2,1)S(1)} %copy-done.1), channel_id=1, source_target_pairs={{0,2},{2,0},{4,6},{6,4},{1,3},{3,1},{5,7},{7,5},{8,10},{10,8},{12,... | collective-permute-start | bytes 98312 | tf_op jit(solution)/shard_map/ppermute | solution.py:211
  16.6 12.0 %collective-permute-start.2 = (bf16[16,1024]{1,0:T(8,128)(2,1)S(1)}, bf16[16,1024]{1,0:T(8,128)(2,1)S(1)}, u32[]{:S(2)}, u32[]{:S(2)}) collective-permute-start(bf16[16,1024]{1,0:T(8,128)(2,1)S(1)} %copy-done.1), channel_id=1, source_target_pairs={{0,4},{2,6},{4,0},{6,2},{1,5},{3,7},{5,1},{7,3},{8,12},{10,14},{12... | collective-permute-start | bytes 98312 | tf_op jit(solution)/shard_map/ppermute | solution.py:211
  21.0 12.6 %collective-permute-start.3 = (bf16[16,1024]{1,0:T(8,128)(2,1)S(1)}, bf16[16,1024]{1,0:T(8,128)(2,1)S(1)}, u32[]{:S(2)}, u32[]{:S(2)}) collective-permute-start(bf16[16,1024]{1,0:T(8,128)(2,1)S(1)} %copy-done.1), channel_id=1, source_target_pairs={{0,6},{2,4},{4,2},{6,0},{1,7},{3,5},{5,3},{7,1},{8,14},{10,12},{12... | collective-permute-start | bytes 98312 | tf_op jit(solution)/shard_map/ppermute | solution.py:211
  23.0 10.6 %collective-permute-start = (f32[128,128]{1,0:T(8,128)S(1)}, f32[128,128]{1,0:T(8,128)S(1)}, u32[]{:S(2)}, u32[]{:S(2)}) collective-permute-start(f32[128,128]{1,0:T(8,128)S(1)} %constant_dynamic-slice_fusion), channel_id=1, source_target_pairs={{0,0},{1,16},{2,32},{3,48},{4,64},{5,80},{6,96},{7,112},{8,8},{9,2... | collective-permute-start | bytes 196616 | tf_op jit(solution)/shard_map/ppermute | solution.py:207
  34.0 10.7 %collective-permute-start.4 = (bf16[8,128,128]{2,1,0:T(8,128)(2,1)S(1)}, bf16[8,128,128]{2,1,0:T(8,128)(2,1)S(1)}, u32[]{:S(2)}, u32[]{:S(2)}) collective-permute-start(bf16[8,128,128]{2,1,0:T(8,128)(2,1)S(1)} %get-tuple-element.26), channel_id=1, source_target_pairs={{0,8},{8,0},{1,9},{9,1},{2,10},{10,2},{3,11},{11,3},{4,12},{12,4},... | collective-permute-start | bytes 786440 | tf_op jit(solution)/shard_map/ppermute | solution.py:218
  45.4 32.2 %all-to-all-start.1 = ((bf16[8,128,128]{2,1,0:T(8,128)(2,1)}), bf16[8,128,128]{2,1,0:T(8,128)(2,1)S(1)}, u32[]{:S(2)}, u32[]{:S(2)}) async-start(bf16[8,128,128]{2,1,0:T(8,128)(2,1)} %add_convert_fusion), calls=%async_computation.1 | async-start | bytes 524288 | tf_op jit(solution)/shard_map/all_to_all | solution.py:220
  78.5 21.1 %all-to-all-start.2 = ((f32[64,8,128]{2,1,0:T(8,128)}), f32[64,8,128]{2,1,0:T(8,128)S(1)}, u32[]{:S(2)}, u32[]{:S(2)}) async-start(f32[64,8,128]{2,1,0:T(8,128)} %get-tuple-element.36), calls=%async_computation.2 | async-start | bytes 524288 | tf_op jit(solution)/shard_map/all_to_all | solution.py:228
  90.0 3.9 %collective-permute-start.5 = (bf16[256,1024]{1,0:T(8,128)(2,1)S(1)}, bf16[256,1024]{1,0:T(8,128)(2,1)S(1)}, u32[]{:S(2)}, u32[]{:S(2)}) collective-permute-start(bf16[256,1024]{1,0:T(8,128)(2,1)S(1)} %all_gather.3.near_ref), channel_id=1, source_target_pairs={{0,1},{1,0},{2,3},{3,2},{4,5},{5,4},{6,7},{7,6},{8,9},{9,8},{10,11... | collective-permute-start | bytes 1572872 | tf_op jit(solution)/shard_map/ppermute | solution.py:229
  123.9 9.8 %collective-permute-start.6 = (bf16[8,128,128]{2,1,0:T(8,128)(2,1)}, bf16[8,128,128]{2,1,0:T(8,128)(2,1)S(1)}, u32[]{:S(2)}, u32[]{:S(2)}) collective-permute-start(bf16[8,128,128]{2,1,0:T(8,128)(2,1)} %all_to_all.30.mine_ref), channel_id=1, source_target_pairs={{0,8},{8,0},{1,9},{9,1},{2,10},{10,2},{3,11},{11,3},{4,12},{12,4},... | collective-permute-start | bytes 786440 | tf_op jit(solution)/shard_map/ppermute | solution.py:238
  125.8 14.4 %all-to-all-start.4 = ((bf16[8,128,128]{2,1,0:T(8,128)(2,1)}), bf16[8,128,128]{2,1,0:T(8,128)(2,1)S(1)}, u32[]{:S(2)}, u32[]{:S(2)}) async-start(bf16[8,128,128]{2,1,0:T(8,128)(2,1)} %all_to_all.30.mine_ref), calls=%async_computation.4 | async-start | bytes 524288 | tf_op jit(solution)/shard_map/all_to_all | solution.py:239
  140.1 13.8 %all-to-all-start.5 = ((bf16[32,16,256]{2,1,0:T(8,128)(2,1)}), bf16[32,16,256]{2,1,0:T(8,128)(2,1)S(1)}, u32[]{:S(2)}, u32[]{:S(2)}) async-start(bf16[32,16,256]{2,1,0:T(8,128)(2,1)} %bitcast.7), calls=%async_computation.5 | async-start | bytes 524288 | tf_op jit(solution)/shard_map/all_to_all | solution.py:248

commit v8 on v7

--- a/solution.py
+++ b/solution.py
@@ -152,12 +152,11 @@
     first, core, y = where_ref[0] == 0, where_ref[1], where_ref[2]
     mine, pair = mine_ref[...].reshape(blocks * share, slab), pair_ref[...].reshape(blocks * share, slab)
     states = jnp.concatenate([jnp.where(first, mine, pair), jnp.where(first, pair, mine)], axis=1)
-    loadings = jnp.concatenate([near_ref[...], far_ref[...]], axis=0)
-    predicted = jnp.dot(loadings, states, preferred_element_type=jnp.float32)
-    predicted = predicted.astype(out_ref.dtype).reshape(cores, nx, ny, sites, span)
-    for other in range(cores):
+    for other, ref in enumerate((near_ref, far_ref)):
+        predicted = jnp.dot(ref[...], states, preferred_element_type=jnp.float32)
+        predicted = predicted.astype(out_ref.dtype).reshape(ny, nx, sites, span)
         for step in range(ny):
-            out_ref[:, y ^ step, core ^ other] = predicted[other, :, step]
+            out_ref[:, y ^ step, core ^ other] = predicted[step]
 
 
 def call(kernel, name, out_shape, *args, scratch=(), scalars=0, vmem=32, **grid):
@@ -206,16 +205,13 @@
     own = lax.dynamic_slice_in_dim(decay, lax.axis_index(col) * share, share, 1)
     decays = lax.ppermute(own, planes + col, turn)
     persist = lax.dynamic_slice_in_dim(persistence, lax.axis_index("zh") * share, share, 0)[None]
-    ny, cores = lax.axis_size("y"), lax.axis_size("core")
-    near = [site_loading]
-    near += [lax.ppermute(site_loading, "y", [(i, i ^ step) for i in range(ny)]) for step in range(1, ny)]
-    got, decays, persist, *near = lax.optimization_barrier((got, decays, persist, *near))
+    got, decays, persist = lax.optimization_barrier((got, decays, persist))
 
     part = lax.axis_index("zl").astype(jnp.int32)
     swap = [(0, 1), (1, 0)]
     both = (shape((blocks, slab, share), f32), shape((blocks, slab, share), bf16))
     keep, give = call(drive_kernel, "drive", both, part[None], got, scalars=1)
-    taken, near = lax.optimization_barrier((lax.ppermute(give, "zl", swap), jnp.concatenate(near)))
+    taken, near = lax.optimization_barrier((lax.ppermute(give, "zl", swap), site_loading))
     halves = (keep + taken.astype(f32)).astype(bf16)
     summed = lax.all_to_all(halves, "zh", 0, 0, tiled=True)
     near = lax.all_gather(near, "x", axis=0, tiled=True)
@@ -226,8 +222,9 @@
         scratch=[pltpu.VMEM((slab, share), f32)],
     )
     summaries = lax.all_to_all(summary, line, 0, 0, tiled=True)
-    far = lax.ppermute(near, "core", swap)
-    summaries, near, far = lax.optimization_barrier((summaries, near, far))
+    ny, cores = lax.axis_size("y"), lax.axis_size("core")
+    near = [near] + [lax.ppermute(near, "y", [(i, i ^ step) for i in range(ny)]) for step in range(1, ny)]
+    summaries, *near = lax.optimization_barrier((summaries, *near))
     rounded = call(
         finish_kernel, "finish", shape((blocks, share, slab), bf16),
         lax.axis_index(line).astype(jnp.int32)[None], summaries, smooth, entry, product,
@@ -235,6 +232,8 @@
     )
 
     mine = lax.all_to_all(rounded, "zh", 0, 0, tiled=True)
+    near = jnp.concatenate(near)
+    mine, near, far = lax.optimization_barrier((mine, near, lax.ppermute(near, "core", swap)))
     pair = lax.ppermute(mine, "zl", swap)
     own = lax.all_to_all(mine, col, 0, 0, tiled=True)
 

time: 156 us -> 158 us (1.013)
  blocking collectives: 33.9 us -> 10.4 us
  waiting for transfers between devices: 40.8 us -> 61.8 us
  starting transfers between devices: 69.9 us -> 74.3 us
    all_to_all x1 -> x0, blocking collectives: 23.9 us -> none  [per_device(): mine = lax.all_to_all(rounded, 'zh', 0, 0, tiled=True)]
    all_to_all x1, waiting for transfers between devices: 0.01 us -> 12.4 us  [per_device(): got = lax.all_to_all(sent, plane, 0, 0, tiled=True)]
    all_to_all x0 -> x1, waiting for transfers between devices: none -> 11.7 us  [per_device(): mine = lax.all_to_all(rounded, 'zh', 0, 0, tiled=True)]
    all_to_all x1, waiting for transfers between devices: 5.73 us -> 0.01 us  [per_device(): summaries = lax.all_to_all(summary, line, 0, 0, tiled=True)]
    all_to_all x0 -> x1, starting transfers between devices: none -> 4.05 us  [per_device(): mine = lax.all_to_all(rounded, 'zh', 0, 0, tiled=True)]
    ppermute x1, waiting for transfers between devices: 0.01 us -> 3.51 us  [per_device(): decays = lax.ppermute(own, planes + col, turn)]
    all_to_all x1, starting transfers between devices: 15.6 us -> 13.4 us  [per_device(): summed = lax.all_to_all(halves, 'zh', 0, 0, tiled=True)]
  transfers between devices with their start and end apart: 12 -> 13, of which waited for: 8 -> 10; matrix products, arithmetic and copies ran while one was open for 1% -> 1% of each run, Pallas kernels for 1% -> 1%
where the time goes in v8:
time: 158 us; the launch traced here: 157 us
  starting transfers between devices  74.3 us (47%)
  waiting for transfers between devices  61.8 us (39%)
  blocking collectives  10.4 us (7%)
  Pallas kernels  6.71 us (4%)
  local copies, waits for them, and re-layouts  2.29 us (1%)
    all_to_all x1, starting transfers between devices, per_device(): summed = lax.all_to_all(halves, 'zh', 0, 0, tiled=True)  13.4 us
    all_to_all x1, waiting for transfers between devices, per_device(): got = lax.all_to_all(sent, plane, 0, 0, tiled=True)  12.4 us
    all_to_all x1, waiting for transfers between devices, per_device(): mine = lax.all_to_all(rounded, 'zh', 0, 0, tiled=True)  11.7 us
    all_to_all x1, starting transfers between devices, per_device(): summaries = lax.all_to_all(summary, line, 0, 0, tiled=True)  11.6 us
    all_to_all x1, starting transfers between devices, per_device(): got = lax.all_to_all(sent, plane, 0, 0, tiled=True)  10.5 us
    all_gather x1, blocking collectives, per_device(): near = lax.all_gather(near, 'x', axis=0, tiled=True)  10.4 us
    ppermute x3, starting transfers between devices, per_device(): lax.ppermute(near, 'y', [(i, i ^ step) for i in range(ny)])  9.58 us
    all_to_all x1, starting transfers between devices, per_device(): own = lax.all_to_all(mine, col, 0, 0, tiled=True)  8.44 us
  transfers between devices with their start and end apart: 13, of which 10 were waited for; matrix products, arithmetic and copies ran while one was open for 1% of the time, Pallas kernels for 1%

profile of v8, /device:TPU:1, one launch (start us, length us, event | category | flops | bytes accessed | tf_op | source)
XLA Modules:
  0.0 157.2 jit_solution(62752991554836971)
XLA Ops:
  0.6 0.0 copy-start
  0.6 2.1 %front.1 = bf16[32,16,1280]{2,1,0:T(8,128)(2,1)} custom-call(s32[16]{0:T(128)} %start_hbm.1, s32[16]{0:T(128)} %count_hbm.1, bf16[16,8192]{1,0:T(8,128)(2,1)} %values_hbm.1, bf16[16,1024]{1,0:T(8,128)(2,1)} %gain_hbm.1), custom_call_target="tpu_custom_call" | custom-call | tf_op jit(solution)/shard_map/front/pallas_call | solution.py:167
  2.8 10.5 %all-to-all-start = ((bf16[32,16,1280]{2,1,0:T(8,128)(2,1)}), bf16[32,16,1280]{2,1,0:T(8,128)(2,1)S(1)}, u32[]{:S(2)}, u32[]{:S(2)}) async-start(bf16[32,16,1280]{2,1,0:T(8,128)(2,1)} %front.1), calls=%async_computation | async-start | bytes 2621440 | tf_op jit(solution)/shard_map/all_to_all | solution.py:204
  13.3 0.0 copy-done
  13.3 3.1 %collective-permute-start = (f32[128,128]{1,0:T(8,128)S(1)}, f32[128,128]{1,0:T(8,128)S(1)}, u32[]{:S(2)}, u32[]{:S(2)}) collective-permute-start(f32[128,128]{1,0:T(8,128)S(1)} %constant_dynamic-slice_fusion), channel_id=1, source_target_pairs={{0,0},{1,16},{2,32},{3,48},{4,64},{5,80},{6,96},{7,112},{8,8},{9,2... | collective-permute-start | bytes 196616 | tf_op jit(solution)/shard_map/ppermute | solution.py:206
  16.5 0.8 dynamic-slice_bitcast_fusion.persist_ref
  17.2 3.5 %collective-permute-done.decay_ref = f32[128,128]{1,0:T(8,128)S(1)} collective-permute-done((f32[128,128]{1,0:T(8,128)S(1)}, f32[128,128]{1,0:T(8,128)S(1)}, u32[]{:S(2)}, u32[]{:S(2)}) %collective-permute-start) | collective-permute-done | bytes 65568 | tf_op jit(solution)/shard_map/ppermute | solution.py:206
  20.7 12.4 %all-to-all-done.got_ref = bf16[32,16,1280]{2,1,0:T(8,128)(2,1)S(1)} async-done(((bf16[32,16,1280]{2,1,0:T(8,128)(2,1)}), bf16[32,16,1280]{2,1,0:T(8,128)(2,1)S(1)}, u32[]{:S(2)}, u32[]{:S(2)}) %all-to-all-start) | async-done | bytes 1310752 | tf_op jit(solution)/shard_map/all_to_all | solution.py:204
  33.2 0.0 copy-start.1
  33.2 0.5 drive.1
  33.6 1.9 %collective-permute-start.1 = (bf16[8,128,128]{2,1,0:T(8,128)(2,1)S(1)}, bf16[8,128,128]{2,1,0:T(8,128)(2,1)S(1)}, u32[]{:S(2)}, u32[]{:S(2)}) collective-permute-start(bf16[8,128,128]{2,1,0:T(8,128)(2,1)S(1)} %get-tuple-element.27), channel_id=1, source_target_pairs={{0,8},{8,0},{1,9},{9,1},{2,10},{10,2},{3,11},{11,3},{4,12},{12,4},... | collective-permute-start | bytes 786440 | tf_op jit(solution)/shard_map/ppermute | solution.py:214
  35.6 7.5 %collective-permute-done.1 = bf16[8,128,128]{2,1,0:T(8,128)(2,1)S(1)} collective-permute-done((bf16[8,128,128]{2,1,0:T(8,128)(2,1)S(1)}, bf16[8,128,128]{2,1,0:T(8,128)(2,1)S(1)}, u32[]{:S(2)}, u32[]{:S(2)}) %collective-permute-start.1) | collective-permute-done | bytes 262176 | tf_op jit(solution)/shard_map/ppermute | solution.py:214
  43.0 0.8 add_convert_fusion
  43.8 13.4 %all-to-all-start.1 = ((bf16[8,128,128]{2,1,0:T(8,128)(2,1)}), bf16[8,128,128]{2,1,0:T(8,128)(2,1)S(1)}, u32[]{:S(2)}, u32[]{:S(2)}) async-start(bf16[8,128,128]{2,1,0:T(8,128)(2,1)} %add_convert_fusion), calls=%async_computation.1 | async-start | bytes 524288 | tf_op jit(solution)/shard_map/all_to_all | solution.py:216
  57.2 0.0 copy-done.1
  57.2 10.4 %all_gather.3 = bf16[64,1024]{1,0:T(8,128)(2,1)S(1)} all-gather(bf16[16,1024]{1,0:T(8,128)(2,1)S(1)} %copy-done.1), channel_id=1, replica_groups=mesh['x'=4,'zh'=8,'zl'=2,'y'=4,'core'=2] {'x'}, dimensions={0}, use_global_device_ids=true | all-gather | bytes 163840 | tf_op jit(solution)/shard_map/all_gather | solution.py:217
  67.6 6.1 %all-to-all-done.1.parts_ref = bf16[8,128,128]{2,1,0:T(8,128)(2,1)S(1)} async-done(((bf16[8,128,128]{2,1,0:T(8,128)(2,1)}), bf16[8,128,128]{2,1,0:T(8,128)(2,1)S(1)}, u32[]{:S(2)}, u32[]{:S(2)}) %all-to-all-start.1) | async-done | bytes 262176 | tf_op jit(solution)/shard_map/all_to_all | solution.py:216
  73.7 0.9 scan.1
  74.6 11.6 %all-to-all-start.2 = ((f32[64,8,128]{2,1,0:T(8,128)}), f32[64,8,128]{2,1,0:T(8,128)S(1)}, u32[]{:S(2)}, u32[]{:S(2)}) async-start(f32[64,8,128]{2,1,0:T(8,128)} %get-tuple-element.33), calls=%async_computation.2 | async-start | bytes 524288 | tf_op jit(solution)/shard_map/all_to_all | solution.py:224
  86.3 3.3 %collective-permute-start.2 = (bf16[64,1024]{1,0:T(8,128)(2,1)S(1)}, bf16[64,1024]{1,0:T(8,128)(2,1)S(1)}, u32[]{:S(2)}, u32[]{:S(2)}) collective-permute-start(bf16[64,1024]{1,0:T(8,128)(2,1)S(1)} %all_gather.3), channel_id=1, source_target_pairs={{0,2},{2,0},{4,6},{6,4},{1,3},{3,1},{5,7},{7,5},{8,10},{10,8},{12,... | collective-permute-start | bytes 393224 | tf_op jit(solution)/shard_map/ppermute | solution.py:226
  89.6 4.3 %collective-permute-start.3 = (bf16[64,1024]{1,0:T(8,128)(2,1)S(1)}, bf16[64,1024]{1,0:T(8,128)(2,1)S(1)}, u32[]{:S(2)}, u32[]{:S(2)}) collective-permute-start(bf16[64,1024]{1,0:T(8,128)(2,1)S(1)} %all_gather.3), channel_id=1, source_target_pairs={{0,4},{2,6},{4,0},{6,2},{1,5},{3,7},{5,1},{7,3},{8,12},{10,14},{12... | collective-permute-start | bytes 393224 | tf_op jit(solution)/shard_map/ppermute | solution.py:226
  93.9 2.0 %collective-permute-start.4 = (bf16[64,1024]{1,0:T(8,128)(2,1)S(1)}, bf16[64,1024]{1,0:T(8,128)(2,1)S(1)}, u32[]{:S(2)}, u32[]{:S(2)}) collective-permute-start(bf16[64,1024]{1,0:T(8,128)(2,1)S(1)} %all_gather.3), channel_id=1, source_target_pairs={{0,6},{2,4},{4,2},{6,0},{1,7},{3,5},{5,3},{7,1},{8,14},{10,12},{12... | collective-permute-start | bytes 393224 | tf_op jit(solution)/shard_map/ppermute | solution.py:226
  95.9 0.0 collective-permute-done.2
  95.9 4.3 %collective-permute-done.3 = bf16[64,1024]{1,0:T(8,128)(2,1)S(1)} collective-permute-done((bf16[64,1024]{1,0:T(8,128)(2,1)S(1)}, bf16[64,1024]{1,0:T(8,128)(2,1)S(1)}, u32[]{:S(2)}, u32[]{:S(2)}) %collective-permute-start.3) | collective-permute-done | bytes 131104 | tf_op jit(solution)/shard_map/ppermute | solution.py:226
  100.2 2.2 %collective-permute-done.4 = bf16[64,1024]{1,0:T(8,128)(2,1)S(1)} collective-permute-done((bf16[64,1024]{1,0:T(8,128)(2,1)S(1)}, bf16[64,1024]{1,0:T(8,128)(2,1)S(1)}, u32[]{:S(2)}, u32[]{:S(2)}) %collective-permute-start.4) | collective-permute-done | bytes 131104 | tf_op jit(solution)/shard_map/ppermute | solution.py:226
  102.4 0.0 all-to-all-done.2.slabs_ref
  102.4 1.1 finish.1
  103.5 4.0 %all-to-all-start.3 = ((bf16[8,128,128]{2,1,0:T(8,128)(2,1)}), bf16[8,128,128]{2,1,0:T(8,128)(2,1)}, u32[]{:S(2)}, u32[]{:S(2)}) async-start(bf16[8,128,128]{2,1,0:T(8,128)(2,1)} %finish.1), calls=%async_computation.3 | async-start | bytes 524288 | tf_op jit(solution)/shard_map/all_to_all | solution.py:234
  107.6 3.1 %collective-permute-start.5 = (bf16[256,1024]{1,0:T(8,128)(2,1)S(1)}, bf16[256,1024]{1,0:T(8,128)(2,1)S(1)}, u32[]{:S(2)}, u32[]{:S(2)}) collective-permute-start(bf16[256,1024]{1,0:T(8,128)(2,1)S(1)} %constant_dynamic-update-slice_fusion.near_ref), channel_id=1, source_target_pairs={{0,1},{1,0},{2,3},{3,2},{4,5},{5,4},{6,7},{7,6},{8,9},{9,8},{10,11... | collective-permute-start | bytes 1572872 | tf_op jit(solution)/shard_map/ppermute | solution.py:236
  110.7 1.5 collective-permute-done.5.far_ref
  112.2 11.7 %all-to-all-done.3.mine_ref = bf16[8,128,128]{2,1,0:T(8,128)(2,1)} async-done(((bf16[8,128,128]{2,1,0:T(8,128)(2,1)}), bf16[8,128,128]{2,1,0:T(8,128)(2,1)}, u32[]{:S(2)}, u32[]{:S(2)}) %all-to-all-start.3) | async-done | bytes 262176 | tf_op jit(solution)/shard_map/all_to_all | solution.py:234
  123.9 3.0 %collective-permute-start.6 = (bf16[8,128,128]{2,1,0:T(8,128)(2,1)}, bf16[8,128,128]{2,1,0:T(8,128)(2,1)S(1)}, u32[]{:S(2)}, u32[]{:S(2)}) collective-permute-start(bf16[8,128,128]{2,1,0:T(8,128)(2,1)} %all-to-all-done.3.mine_ref), channel_id=1, source_target_pairs={{0,8},{8,0},{1,9},{9,1},{2,10},{10,2},{3,11},{11,3},{4,12},{12,4},... | collective-permute-start | bytes 786440 | tf_op jit(solution)/shard_map/ppermute | solution.py:237
  127.0 8.4 %all-to-all-start.4 = ((bf16[8,128,128]{2,1,0:T(8,128)(2,1)}), bf16[8,128,128]{2,1,0:T(8,128)(2,1)S(1)}, u32[]{:S(2)}, u32[]{:S(2)}) async-start(bf16[8,128,128]{2,1,0:T(8,128)(2,1)} %all-to-all-done.3.mine_ref), calls=%async_computation.4 | async-start | bytes 524288 | tf_op jit(solution)/shard_map/all_to_all | solution.py:238
  135.4 0.1 pad_add_fusion.where_ref
  135.5 0.0 collective-permute-done.6.pair_ref
  135.5 2.1 %predict.1 = bf16[4,4,2,16,256]{4,3,2,1,0:T(8,128)(2,1)} custom-call(s32[3]{0:T(128)S(1)} %pad_add_fusion.where_ref, bf16[256,1024]{1,0:T(8,128)(2,1)S(1)} %constant_dynamic-update-slice_fusion.near_ref, bf16[256,1024]{1,0:T(8,128)(2,1)S(1)} %collective-permute-done.5.far_ref, bf16[8,128,128]{2,1,0:T(8,128)(2,1)} %all-to-all-done.3.mine_ref, ...), custom_call_target="tpu_custom_call" | custom-call | tf_op jit(solution)/shard_map/predict/pallas_call | solution.py:167
  137.6 4.3 %all-to-all-done.4 = bf16[8,128,128]{2,1,0:T(8,128)(2,1)S(1)} async-done(((bf16[8,128,128]{2,1,0:T(8,128)(2,1)}), bf16[8,128,128]{2,1,0:T(8,128)(2,1)S(1)}, u32[]{:S(2)}, u32[]{:S(2)}) %all-to-all-start.4) | async-done | bytes 262176 | tf_op jit(solution)/shard_map/all_to_all | solution.py:238
  141.9 5.6 %all-to-all-start.5 = ((bf16[32,16,256]{2,1,0:T(8,128)(2,1)}), bf16[32,16,256]{2,1,0:T(8,128)(2,1)S(1)}, u32[]{:S(2)}, u32[]{:S(2)}) async-start(bf16[32,16,256]{2,1,0:T(8,128)(2,1)} %bitcast.7), calls=%async_computation.5 | async-start | bytes 524288 | tf_op jit(solution)/shard_map/all_to_all | solution.py:247
  147.5 0.7 copy.10
  148.2 8.2 %all-to-all-done.5 = bf16[32,16,256]{2,1,0:T(8,128)(2,1)S(1)} async-done(((bf16[32,16,256]{2,1,0:T(8,128)(2,1)}), bf16[32,16,256]{2,1,0:T(8,128)(2,1)S(1)}, u32[]{:S(2)}, u32[]{:S(2)}) %all-to-all-start.5) | async-done | bytes 262176 | tf_op jit(solution)/shard_map/all_to_all | solution.py:247
  156.5 0.7 copy.11
  (6 shorter events, 0.1 us)
Async XLA Ops:
  0.6 12.7 %copy-start = (f32[128,1024]{1,0:T(8,128)S(1)}, f32[128,1024]{1,0:T(8,128)}, u32[]{:S(2)}) copy-start(f32[128,1024]{1,0:T(8,128)} %param.12) | copy-start | bytes 1572868
  2.8 30.4 %all-to-all-start = ((bf16[32,16,1280]{2,1,0:T(8,128)(2,1)}), bf16[32,16,1280]{2,1,0:T(8,128)(2,1)S(1)}, u32[]{:S(2)}, u32[]{:S(2)}) async-start(bf16[32,16,1280]{2,1,0:T(8,128)(2,1)} %front.1), calls=%async_computation | async-start | bytes 2621440 | tf_op jit(solution)/shard_map/all_to_all | solution.py:204
  13.3 7.4 %collective-permute-start = (f32[128,128]{1,0:T(8,128)S(1)}, f32[128,128]{1,0:T(8,128)S(1)}, u32[]{:S(2)}, u32[]{:S(2)}) collective-permute-start(f32[128,128]{1,0:T(8,128)S(1)} %constant_dynamic-slice_fusion), channel_id=1, source_target_pairs={{0,0},{1,16},{2,32},{3,48},{4,64},{5,80},{6,96},{7,112},{8,8},{9,2... | collective-permute-start | bytes 196616 | tf_op jit(solution)/shard_map/ppermute | solution.py:206
  33.2 24.0 %copy-start.1 = (bf16[16,1024]{1,0:T(8,128)(2,1)S(1)}, bf16[16,1024]{1,0:T(8,128)(2,1)}, u32[]{:S(2)}) copy-start(bf16[16,1024]{1,0:T(8,128)(2,1)} %param.11) | copy-start | bytes 98308
  33.6 9.4 %collective-permute-start.1 = (bf16[8,128,128]{2,1,0:T(8,128)(2,1)S(1)}, bf16[8,128,128]{2,1,0:T(8,128)(2,1)S(1)}, u32[]{:S(2)}, u32[]{:S(2)}) collective-permute-start(bf16[8,128,128]{2,1,0:T(8,128)(2,1)S(1)} %get-tuple-element.27), channel_id=1, source_target_pairs={{0,8},{8,0},{1,9},{9,1},{2,10},{10,2},{3,11},{11,3},{4,12},{12,4},... | collective-permute-start | bytes 786440 | tf_op jit(solution)/shard_map/ppermute | solution.py:214
  43.8 29.9 %all-to-all-start.1 = ((bf16[8,128,128]{2,1,0:T(8,128)(2,1)}), bf16[8,128,128]{2,1,0:T(8,128)(2,1)S(1)}, u32[]{:S(2)}, u32[]{:S(2)}) async-start(bf16[8,128,128]{2,1,0:T(8,128)(2,1)} %add_convert_fusion), calls=%async_computation.1 | async-start | bytes 524288 | tf_op jit(solution)/shard_map/all_to_all | solution.py:216
  74.6 27.8 %all-to-all-start.2 = ((f32[64,8,128]{2,1,0:T(8,128)}), f32[64,8,128]{2,1,0:T(8,128)S(1)}, u32[]{:S(2)}, u32[]{:S(2)}) async-start(f32[64,8,128]{2,1,0:T(8,128)} %get-tuple-element.33), calls=%async_computation.2 | async-start | bytes 524288 | tf_op jit(solution)/shard_map/all_to_all | solution.py:224
  86.3 9.6 %collective-permute-start.2 = (bf16[64,1024]{1,0:T(8,128)(2,1)S(1)}, bf16[64,1024]{1,0:T(8,128)(2,1)S(1)}, u32[]{:S(2)}, u32[]{:S(2)}) collective-permute-start(bf16[64,1024]{1,0:T(8,128)(2,1)S(1)} %all_gather.3), channel_id=1, source_target_pairs={{0,2},{2,0},{4,6},{6,4},{1,3},{3,1},{5,7},{7,5},{8,10},{10,8},{12,... | collective-permute-start | bytes 393224 | tf_op jit(solution)/shard_map/ppermute | solution.py:226
  89.6 10.7 %collective-permute-start.3 = (bf16[64,1024]{1,0:T(8,128)(2,1)S(1)}, bf16[64,1024]{1,0:T(8,128)(2,1)S(1)}, u32[]{:S(2)}, u32[]{:S(2)}) collective-permute-start(bf16[64,1024]{1,0:T(8,128)(2,1)S(1)} %all_gather.3), channel_id=1, source_target_pairs={{0,4},{2,6},{4,0},{6,2},{1,5},{3,7},{5,1},{7,3},{8,12},{10,14},{12... | collective-permute-start | bytes 393224 | tf_op jit(solution)/shard_map/ppermute | solution.py:226
  93.9 8.5 %collective-permute-start.4 = (bf16[64,1024]{1,0:T(8,128)(2,1)S(1)}, bf16[64,1024]{1,0:T(8,128)(2,1)S(1)}, u32[]{:S(2)}, u32[]{:S(2)}) collective-permute-start(bf16[64,1024]{1,0:T(8,128)(2,1)S(1)} %all_gather.3), channel_id=1, source_target_pairs={{0,6},{2,4},{4,2},{6,0},{1,7},{3,5},{5,3},{7,1},{8,14},{10,12},{12... | collective-permute-start | bytes 393224 | tf_op jit(solution)/shard_map/ppermute | solution.py:226
  103.5 20.4 %all-to-all-start.3 = ((bf16[8,128,128]{2,1,0:T(8,128)(2,1)}), bf16[8,128,128]{2,1,0:T(8,128)(2,1)}, u32[]{:S(2)}, u32[]{:S(2)}) async-start(bf16[8,128,128]{2,1,0:T(8,128)(2,1)} %finish.1), calls=%async_computation.3 | async-start | bytes 524288 | tf_op jit(solution)/shard_map/all_to_all | solution.py:234
  107.6 4.6 %collective-permute-start.5 = (bf16[256,1024]{1,0:T(8,128)(2,1)S(1)}, bf16[256,1024]{1,0:T(8,128)(2,1)S(1)}, u32[]{:S(2)}, u32[]{:S(2)}) collective-permute-start(bf16[256,1024]{1,0:T(8,128)(2,1)S(1)} %constant_dynamic-update-slice_fusion.near_ref), channel_id=1, source_target_pairs={{0,1},{1,0},{2,3},{3,2},{4,5},{5,4},{6,7},{7,6},{8,9},{9,8},{10,11... | collective-permute-start | bytes 1572872 | tf_op jit(solution)/shard_map/ppermute | solution.py:236
  123.9 11.6 %collective-permute-start.6 = (bf16[8,128,128]{2,1,0:T(8,128)(2,1)}, bf16[8,128,128]{2,1,0:T(8,128)(2,1)S(1)}, u32[]{:S(2)}, u32[]{:S(2)}) collective-permute-start(bf16[8,128,128]{2,1,0:T(8,128)(2,1)} %all-to-all-done.3.mine_ref), channel_id=1, source_target_pairs={{0,8},{8,0},{1,9},{9,1},{2,10},{10,2},{3,11},{11,3},{4,12},{12,4},... | collective-permute-start | bytes 786440 | tf_op jit(solution)/shard_map/ppermute | solution.py:237
  127.0 15.0 %all-to-all-start.4 = ((bf16[8,128,128]{2,1,0:T(8,128)(2,1)}), bf16[8,128,128]{2,1,0:T(8,128)(2,1)S(1)}, u32[]{:S(2)}, u32[]{:S(2)}) async-start(bf16[8,128,128]{2,1,0:T(8,128)(2,1)} %all-to-all-done.3.mine_ref), calls=%async_computation.4 | async-start | bytes 524288 | tf_op jit(solution)/shard_map/all_to_all | solution.py:238
  141.9 14.6 %all-to-all-start.5 = ((bf16[32,16,256]{2,1,0:T(8,128)(2,1)}), bf16[32,16,256]{2,1,0:T(8,128)(2,1)S(1)}, u32[]{:S(2)}, u32[]{:S(2)}) async-start(bf16[32,16,256]{2,1,0:T(8,128)(2,1)} %bitcast.7), calls=%async_computation.5 | async-start | bytes 524288 | tf_op jit(solution)/shard_map/all_to_all | solution.py:247

commit v9 on v5

--- a/solution.py
+++ b/solution.py
@@ -11,7 +11,8 @@
 
 def front_kernel(start_hbm, count_hbm, values_hbm, gain_hbm, out_hbm, start, count, values, gain, out, small, large, sent):
     devices, sites, width = out.shape
-    span = width - gain.shape[1]
+    half = gain.shape[1] // 2
+    span = width - half
     wide, each = values.shape[1] // STEPS, devices // STEPS
     arriving = [
         pltpu.make_async_copy(start_hbm, start, small.at[0]),
@@ -40,7 +41,7 @@
             own = values[:, to * span:(to + 1) * span].astype(jnp.float32)
             inside = (epoch + to * span >= first) & (epoch + to * span < end)
             out[to, :, :span] = jnp.where(inside, own, 0.0).astype(out.dtype)
-            out[to, :, span:] = gains
+            out[to, :, span:] = gains[:, to % 2 * half:(to % 2 + 1) * half]
         part = pl.ds(step * each, each)
         leaving.append(pltpu.make_async_copy(out.at[part], out_hbm.at[part], sent.at[step]))
         leaving[-1].start()
@@ -48,17 +49,19 @@
         copy.wait()
 
 
-def drive_kernel(got_ref, out_ref):
-    sources, sites, width = got_ref.shape
+def drive_kernel(core_ref, got_ref, other_ref, out_ref):
+    sources, sites, half = other_ref.shape
     blocks, parts, slab, share = out_ref.shape
     span = parts * slab
     rows = got_ref[:, :, :span].reshape(sources * sites, span)
-    gains = got_ref[:, :, span:].reshape(sources * sites, blocks * share)
-    partial = lax.dot_general(rows, gains, (((0,), (0,)), ((), ())), preferred_element_type=jnp.float32)
-    partial = partial.astype(out_ref.dtype)
-    for block in range(blocks):
-        for part in range(parts):
-            out_ref[block, part] = partial[part * slab:(part + 1) * slab, block * share:(block + 1) * share]
+    for turn in range(2):
+        gains = (got_ref[:, :, span:] if turn == 0 else other_ref[...]).reshape(sources * sites, half)
+        partial = lax.dot_general(rows, gains, (((0,), (0,)), ((), ())), preferred_element_type=jnp.float32)
+        partial = partial.astype(out_ref.dtype)
+        first = (core_ref[0] ^ turn) * (blocks // 2)
+        for block in range(blocks // 2):
+            for part in range(parts):
+                out_ref[first + block, part] = partial[part * slab:(part + 1) * slab, block * share:(block + 1) * share]
 
 
 def shifted(value, by, fill):
@@ -190,12 +193,12 @@
 
     hbm, smem = pl.BlockSpec(memory_space=pl.ANY), pltpu.SMEM
     sent = call(
-        front_kernel, "front", shape((devices, sites, span + basis), bf16),
+        front_kernel, "front", shape((devices, sites, span + basis // 2), bf16),
         site_start, site_count, observations, site_gain, in_specs=[hbm] * 4, out_specs=hbm, vmem=60,
         scratch=[
             smem((sites,), jnp.int32), smem((sites,), jnp.int32),
             pltpu.VMEM((sites, epochs), bf16), pltpu.VMEM((sites, basis), bf16),
-            pltpu.VMEM((devices, sites, span + basis), bf16),
+            pltpu.VMEM((devices, sites, span + basis // 2), bf16),
             pltpu.SemaphoreType.DMA((3,)), pltpu.SemaphoreType.DMA((STEPS,)), pltpu.SemaphoreType.DMA((STEPS,)),
         ],
     )
@@ -205,9 +208,12 @@
     persist = lax.dynamic_slice_in_dim(persistence, lax.axis_index("zh") * share, share, 0)[None]
     got, decays, persist = lax.optimization_barrier((got, decays, persist))
 
-    partial = call(drive_kernel, "drive", shape((blocks, parts, slab, share), bf16), got)
+    swap = [(0, 1), (1, 0)]
+    other = lax.ppermute(got[:, :, span:], "core", swap)
+    core = lax.axis_index("core").astype(jnp.int32)
+    partial = call(drive_kernel, "drive", shape((blocks, parts, slab, share), bf16), core[None], got, other, scalars=1)
     summed = lax.all_to_all(partial.reshape(blocks * parts, slab, share), planes, 0, 0, tiled=True)
-    near, _ = lax.optimization_barrier((site_loading, got))
+    near, _ = lax.optimization_barrier((site_loading, other))
     near = lax.all_gather(near, ("x", "y"), axis=0, tiled=True)
     summed, near = lax.optimization_barrier((summed, near))
     square = shape((slab, share), f32)

time: 149 us -> 152 us (1.020)
  starting transfers between devices: 57.8 us -> 64.2 us
  waiting for transfers between devices: 39.6 us -> 34.9 us
    all_to_all x1, waiting for transfers between devices: 12.4 us -> 6.83 us  [per_device(): got = lax.all_to_all(sent, plane, 0, 0, tiled=True)]
    all_to_all x1, starting transfers between devices: 13.8 us -> 16.3 us  [per_device(): lax.all_to_all(partial.reshape(blocks * parts, slab, share), planes, 0, 0...]
    ppermute x0 -> x1, starting transfers between devices: none -> 1.92 us  [per_device(): other = lax.ppermute(got[:, :, span:], 'core', swap)]
    all_to_all x1, starting transfers between devices: 13.5 us -> 15.4 us  [per_device(): summaries = lax.all_to_all(summary, line, 0, 0, tiled=True)]
    ppermute x0 -> x1, waiting for transfers between devices: none -> 1.88 us  [per_device(): other = lax.ppermute(got[:, :, span:], 'core', swap)]
  transfers between devices with their start and end apart: 8 -> 9, of which waited for: 7 -> 8; matrix products, arithmetic and copies ran while one was open for 1% -> 1% of each run, Pallas kernels for 1% -> 1%
where the time goes in v9:
time: 152 us; the launch traced here: 151 us
  starting transfers between devices  64.2 us (42%)
  blocking collectives  42.4 us (28%)
  waiting for transfers between devices  34.9 us (23%)
  Pallas kernels  6.65 us (4%)
  local copies, waits for them, and re-layouts  2.3 us (2%)
    all_to_all x1, blocking collectives, per_device(): mine = lax.all_to_all(rounded, 'zh', 0, 0, tiled=True)  22.5 us
    all_gather x1, blocking collectives, per_device(): near = lax.all_gather(near, ('x', 'y'), axis=0, tiled=True)  19.9 us
    all_to_all x1, starting transfers between devices, per_device(): lax.all_to_all(partial.reshape(blocks * parts, slab, share), planes, 0, 0...  16.3 us
    all_to_all x1, starting transfers between devices, per_device(): summaries = lax.all_to_all(summary, line, 0, 0, tiled=True)  15.4 us
    all_to_all x1, starting transfers between devices, per_device(): got = lax.all_to_all(sent, plane, 0, 0, tiled=True)  10.4 us
    all_to_all x1, waiting for transfers between devices, per_device(): lax.all_to_all(predicted.reshape(devices, sites, span), plane, 0, 0, tile...  8.23 us
    all_to_all x1, starting transfers between devices, per_device(): own = lax.all_to_all(mine, col, 0, 0, tiled=True)  7.84 us
    all_to_all x1, waiting for transfers between devices, per_device(): got = lax.all_to_all(sent, plane, 0, 0, tiled=True)  6.83 us
  transfers between devices with their start and end apart: 9, of which 8 were waited for; matrix products, arithmetic and copies ran while one was open for 1% of the time, Pallas kernels for 1%

profile of v9, /device:TPU:1, one launch (start us, length us, event | category | flops | bytes accessed | tf_op | source)
XLA Modules:
  0.0 151.3 jit_solution(7177903320144537029)
XLA Ops:
  0.6 0.0 copy-start
  0.6 2.0 %front.1 = bf16[32,16,768]{2,1,0:T(8,128)(2,1)} custom-call(s32[16]{0:T(128)} %start_hbm.1, s32[16]{0:T(128)} %count_hbm.1, bf16[16,8192]{1,0:T(8,128)(2,1)} %values_hbm.1, bf16[16,1024]{1,0:T(8,128)(2,1)} %gain_hbm.1), custom_call_target="tpu_custom_call" | custom-call | tf_op jit(solution)/shard_map/front/pallas_call | solution.py:168
  2.6 10.4 %all-to-all-start = ((bf16[32,16,768]{2,1,0:T(8,128)(2,1)}), bf16[32,16,768]{2,1,0:T(8,128)(2,1)S(1)}, u32[]{:S(2)}, u32[]{:S(2)}) async-start(bf16[32,16,768]{2,1,0:T(8,128)(2,1)} %front.1), calls=%async_computation | async-start | bytes 1572864 | tf_op jit(solution)/shard_map/all_to_all | solution.py:205
  13.1 0.0 copy-done
  13.1 3.2 %collective-permute-start = (f32[128,128]{1,0:T(8,128)S(1)}, f32[128,128]{1,0:T(8,128)S(1)}, u32[]{:S(2)}, u32[]{:S(2)}) collective-permute-start(f32[128,128]{1,0:T(8,128)S(1)} %constant_dynamic-slice_fusion), channel_id=1, source_target_pairs={{0,0},{1,16},{2,32},{3,48},{4,64},{5,80},{6,96},{7,112},{8,8},{9,2... | collective-permute-start | bytes 196616 | tf_op jit(solution)/shard_map/ppermute | solution.py:207
  16.3 0.8 dynamic-slice_bitcast_fusion.persist_ref
  17.1 3.5 %collective-permute-done.decay_ref = f32[128,128]{1,0:T(8,128)S(1)} collective-permute-done((f32[128,128]{1,0:T(8,128)S(1)}, f32[128,128]{1,0:T(8,128)S(1)}, u32[]{:S(2)}, u32[]{:S(2)}) %collective-permute-start) | collective-permute-done | bytes 65568 | tf_op jit(solution)/shard_map/ppermute | solution.py:207
  20.6 6.8 %all-to-all-done.got_ref = bf16[32,16,768]{2,1,0:T(8,128)(2,1)S(1)} async-done(((bf16[32,16,768]{2,1,0:T(8,128)(2,1)}), bf16[32,16,768]{2,1,0:T(8,128)(2,1)S(1)}, u32[]{:S(2)}, u32[]{:S(2)}) %all-to-all-start) | async-done | bytes 786464 | tf_op jit(solution)/shard_map/all_to_all | solution.py:205
  27.4 0.1 slice.3
  27.5 1.9 %collective-permute-start.1 = (bf16[32,16,512]{2,1,0:T(8,128)(2,1)S(1)}, bf16[32,16,512]{2,1,0:T(8,128)(2,1)S(1)}, u32[]{:S(2)}, u32[]{:S(2)}) collective-permute-start(bf16[32,16,512]{2,1,0:T(8,128)(2,1)S(1)} %slice.3), channel_id=1, source_target_pairs={{0,1},{1,0},{2,3},{3,2},{4,5},{5,4},{6,7},{7,6},{8,9},{9,8},{10,11... | collective-permute-start | bytes 1572872 | tf_op jit(solution)/shard_map/ppermute | solution.py:212
  29.4 1.9 %collective-permute-done.1.other_ref = bf16[32,16,512]{2,1,0:T(8,128)(2,1)S(1)} collective-permute-done((bf16[32,16,512]{2,1,0:T(8,128)(2,1)S(1)}, bf16[32,16,512]{2,1,0:T(8,128)(2,1)S(1)}, u32[]{:S(2)}, u32[]{:S(2)}) %collective-permute-start.1) | collective-permute-done | bytes 524320 | tf_op jit(solution)/shard_map/ppermute | solution.py:212
  31.3 1.3 drive.1
  32.5 0.0 copy-start.1
  32.5 16.3 %all-to-all-start.1 = ((bf16[16,128,128]{2,1,0:T(8,128)(2,1)}), bf16[16,128,128]{2,1,0:T(8,128)(2,1)S(1)}, u32[]{:S(2)}, u32[]{:S(2)}) async-start(bf16[16,128,128]{2,1,0:T(8,128)(2,1)} %bitcast.3), calls=%async_computation.1 | async-start | bytes 1048576 | tf_op jit(solution)/shard_map/all_to_all | solution.py:215
  48.9 0.0 copy-done.1
  48.9 19.9 %all_gather.3.near_ref = bf16[256,1024]{1,0:T(8,128)(2,1)S(1)} all-gather(bf16[16,1024]{1,0:T(8,128)(2,1)S(1)} %copy-done.1), channel_id=1, replica_groups=mesh['x'=4,'zh'=8,'zl'=2,'y'=4,'core'=2] {'x','y'}, dimensions={0}, use_global_device_ids=true | all-gather | bytes 557056 | tf_op jit(solution)/shard_map/all_gather | solution.py:217
  68.8 2.8 %all-to-all-done.1.parts_ref = bf16[16,128,128]{2,1,0:T(8,128)(2,1)S(1)} async-done(((bf16[16,128,128]{2,1,0:T(8,128)(2,1)}), bf16[16,128,128]{2,1,0:T(8,128)(2,1)S(1)}, u32[]{:S(2)}, u32[]{:S(2)}) %all-to-all-start.1) | async-done | bytes 524320 | tf_op jit(solution)/shard_map/all_to_all | solution.py:215
  71.6 1.0 scan.1
  72.6 15.4 %all-to-all-start.2 = ((f32[64,8,128]{2,1,0:T(8,128)}), f32[64,8,128]{2,1,0:T(8,128)S(1)}, u32[]{:S(2)}, u32[]{:S(2)}) async-start(f32[64,8,128]{2,1,0:T(8,128)} %get-tuple-element.22), calls=%async_computation.2 | async-start | bytes 524288 | tf_op jit(solution)/shard_map/all_to_all | solution.py:224
  88.0 2.4 %collective-permute-start.2 = (bf16[256,1024]{1,0:T(8,128)(2,1)S(1)}, bf16[256,1024]{1,0:T(8,128)(2,1)S(1)}, u32[]{:S(2)}, u32[]{:S(2)}) collective-permute-start(bf16[256,1024]{1,0:T(8,128)(2,1)S(1)} %all_gather.3.near_ref), channel_id=1, source_target_pairs={{0,1},{1,0},{2,3},{3,2},{4,5},{5,4},{6,7},{7,6},{8,9},{9,8},{10,11... | collective-permute-start | bytes 1572872 | tf_op jit(solution)/shard_map/ppermute | solution.py:225
  90.4 1.5 collective-permute-done.2.far_ref
  91.9 5.7 %all-to-all-done.2.slabs_ref = f32[64,8,128]{2,1,0:T(8,128)S(1)} async-done(((f32[64,8,128]{2,1,0:T(8,128)}), f32[64,8,128]{2,1,0:T(8,128)S(1)}, u32[]{:S(2)}, u32[]{:S(2)}) %all-to-all-start.2) | async-done | bytes 262176 | tf_op jit(solution)/shard_map/all_to_all | solution.py:224
  97.7 0.4 finish.1
  98.0 22.5 %all_to_all.30.mine_ref = bf16[8,128,128]{2,1,0:T(8,128)(2,1)} all-to-all(bf16[8,128,128]{2,1,0:T(8,128)(2,1)S(1)} %finish.1), channel_id=1, replica_groups=mesh['x'=4,'zh'=8,'zl'=2,'y'=4,'core'=2] {'zh'}, dimensions={0} | all-to-all | bytes 524288 | tf_op jit(solution)/shard_map/all_to_all | solution.py:233
  120.6 1.9 %collective-permute-start.3 = (bf16[8,128,128]{2,1,0:T(8,128)(2,1)}, bf16[8,128,128]{2,1,0:T(8,128)(2,1)S(1)}, u32[]{:S(2)}, u32[]{:S(2)}) collective-permute-start(bf16[8,128,128]{2,1,0:T(8,128)(2,1)} %all_to_all.30.mine_ref), channel_id=1, source_target_pairs={{0,8},{8,0},{1,9},{9,1},{2,10},{10,2},{3,11},{11,3},{4,12},{12,4},... | collective-permute-start | bytes 786440 | tf_op jit(solution)/shard_map/ppermute | solution.py:234
  122.5 7.8 %all-to-all-start.4 = ((bf16[8,128,128]{2,1,0:T(8,128)(2,1)}), bf16[8,128,128]{2,1,0:T(8,128)(2,1)S(1)}, u32[]{:S(2)}, u32[]{:S(2)}) async-start(bf16[8,128,128]{2,1,0:T(8,128)(2,1)} %all_to_all.30.mine_ref), calls=%async_computation.4 | async-start | bytes 524288 | tf_op jit(solution)/shard_map/all_to_all | solution.py:235
  130.3 0.1 pad_add_fusion.where_ref
  130.4 0.0 collective-permute-done.3.pair_ref
  130.4 2.1 %predict.1 = bf16[16,2,16,256]{3,2,1,0:T(8,128)(2,1)} custom-call(s32[2]{0:T(128)S(1)} %pad_add_fusion.where_ref, bf16[256,1024]{1,0:T(8,128)(2,1)S(1)} %all_gather.3.near_ref, bf16[256,1024]{1,0:T(8,128)(2,1)S(1)} %collective-permute-done.2.far_ref, bf16[8,128,128]{2,1,0:T(8,128)(2,1)} %all_to_all.30.mine_ref, ...), custom_call_target="tpu_custom_call" | custom-call | tf_op jit(solution)/shard_map/predict/pallas_call | solution.py:168
  132.5 4.3 %all-to-all-done.4 = bf16[8,128,128]{2,1,0:T(8,128)(2,1)S(1)} async-done(((bf16[8,128,128]{2,1,0:T(8,128)(2,1)}), bf16[8,128,128]{2,1,0:T(8,128)(2,1)S(1)}, u32[]{:S(2)}, u32[]{:S(2)}) %all-to-all-start.4) | async-done | bytes 262176 | tf_op jit(solution)/shard_map/all_to_all | solution.py:235
  136.8 4.8 %all-to-all-start.5 = ((bf16[32,16,256]{2,1,0:T(8,128)(2,1)}), bf16[32,16,256]{2,1,0:T(8,128)(2,1)S(1)}, u32[]{:S(2)}, u32[]{:S(2)}) async-start(bf16[32,16,256]{2,1,0:T(8,128)(2,1)} %bitcast.7), calls=%async_computation.5 | async-start | bytes 524288 | tf_op jit(solution)/shard_map/all_to_all | solution.py:245
  141.7 0.7 copy.10
  142.4 8.2 %all-to-all-done.5 = bf16[32,16,256]{2,1,0:T(8,128)(2,1)S(1)} async-done(((bf16[32,16,256]{2,1,0:T(8,128)(2,1)}), bf16[32,16,256]{2,1,0:T(8,128)(2,1)S(1)}, u32[]{:S(2)}, u32[]{:S(2)}) %all-to-all-start.5) | async-done | bytes 262176 | tf_op jit(solution)/shard_map/all_to_all | solution.py:245
  150.6 0.7 copy.11
  (2 shorter events, 0.0 us)
Async XLA Ops:
  0.6 12.4 %copy-start = (f32[128,1024]{1,0:T(8,128)S(1)}, f32[128,1024]{1,0:T(8,128)}, u32[]{:S(2)}) copy-start(f32[128,1024]{1,0:T(8,128)} %param.12) | copy-start | bytes 1572868
  2.6 24.8 %all-to-all-start = ((bf16[32,16,768]{2,1,0:T(8,128)(2,1)}), bf16[32,16,768]{2,1,0:T(8,128)(2,1)S(1)}, u32[]{:S(2)}, u32[]{:S(2)}) async-start(bf16[32,16,768]{2,1,0:T(8,128)(2,1)} %front.1), calls=%async_computation | async-start | bytes 1572864 | tf_op jit(solution)/shard_map/all_to_all | solution.py:205
  13.1 7.5 %collective-permute-start = (f32[128,128]{1,0:T(8,128)S(1)}, f32[128,128]{1,0:T(8,128)S(1)}, u32[]{:S(2)}, u32[]{:S(2)}) collective-permute-start(f32[128,128]{1,0:T(8,128)S(1)} %constant_dynamic-slice_fusion), channel_id=1, source_target_pairs={{0,0},{1,16},{2,32},{3,48},{4,64},{5,80},{6,96},{7,112},{8,8},{9,2... | collective-permute-start | bytes 196616 | tf_op jit(solution)/shard_map/ppermute | solution.py:207
  27.5 3.8 %collective-permute-start.1 = (bf16[32,16,512]{2,1,0:T(8,128)(2,1)S(1)}, bf16[32,16,512]{2,1,0:T(8,128)(2,1)S(1)}, u32[]{:S(2)}, u32[]{:S(2)}) collective-permute-start(bf16[32,16,512]{2,1,0:T(8,128)(2,1)S(1)} %slice.3), channel_id=1, source_target_pairs={{0,1},{1,0},{2,3},{3,2},{4,5},{5,4},{6,7},{7,6},{8,9},{9,8},{10,11... | collective-permute-start | bytes 1572872 | tf_op jit(solution)/shard_map/ppermute | solution.py:212
  32.5 16.4 %copy-start.1 = (bf16[16,1024]{1,0:T(8,128)(2,1)S(1)}, bf16[16,1024]{1,0:T(8,128)(2,1)}, u32[]{:S(2)}) copy-start(bf16[16,1024]{1,0:T(8,128)(2,1)} %param.11) | copy-start | bytes 98308
  32.5 39.1 %all-to-all-start.1 = ((bf16[16,128,128]{2,1,0:T(8,128)(2,1)}), bf16[16,128,128]{2,1,0:T(8,128)(2,1)S(1)}, u32[]{:S(2)}, u32[]{:S(2)}) async-start(bf16[16,128,128]{2,1,0:T(8,128)(2,1)} %bitcast.3), calls=%async_computation.1 | async-start | bytes 1048576 | tf_op jit(solution)/shard_map/all_to_all | solution.py:215
  72.6 25.1 %all-to-all-start.2 = ((f32[64,8,128]{2,1,0:T(8,128)}), f32[64,8,128]{2,1,0:T(8,128)S(1)}, u32[]{:S(2)}, u32[]{:S(2)}) async-start(f32[64,8,128]{2,1,0:T(8,128)} %get-tuple-element.22), calls=%async_computation.2 | async-start | bytes 524288 | tf_op jit(solution)/shard_map/all_to_all | solution.py:224
  88.0 3.9 %collective-permute-start.2 = (bf16[256,1024]{1,0:T(8,128)(2,1)S(1)}, bf16[256,1024]{1,0:T(8,128)(2,1)S(1)}, u32[]{:S(2)}, u32[]{:S(2)}) collective-permute-start(bf16[256,1024]{1,0:T(8,128)(2,1)S(1)} %all_gather.3.near_ref), channel_id=1, source_target_pairs={{0,1},{1,0},{2,3},{3,2},{4,5},{5,4},{6,7},{7,6},{8,9},{9,8},{10,11... | collective-permute-start | bytes 1572872 | tf_op jit(solution)/shard_map/ppermute | solution.py:225
  120.6 9.8 %collective-permute-start.3 = (bf16[8,128,128]{2,1,0:T(8,128)(2,1)}, bf16[8,128,128]{2,1,0:T(8,128)(2,1)S(1)}, u32[]{:S(2)}, u32[]{:S(2)}) collective-permute-start(bf16[8,128,128]{2,1,0:T(8,128)(2,1)} %all_to_all.30.mine_ref), channel_id=1, source_target_pairs={{0,8},{8,0},{1,9},{9,1},{2,10},{10,2},{3,11},{11,3},{4,12},{12,4},... | collective-permute-start | bytes 786440 | tf_op jit(solution)/shard_map/ppermute | solution.py:234
  122.5 14.4 %all-to-all-start.4 = ((bf16[8,128,128]{2,1,0:T(8,128)(2,1)}), bf16[8,128,128]{2,1,0:T(8,128)(2,1)S(1)}, u32[]{:S(2)}, u32[]{:S(2)}) async-start(bf16[8,128,128]{2,1,0:T(8,128)(2,1)} %all_to_all.30.mine_ref), calls=%async_computation.4 | async-start | bytes 524288 | tf_op jit(solution)/shard_map/all_to_all | solution.py:235
  136.8 13.8 %all-to-all-start.5 = ((bf16[32,16,256]{2,1,0:T(8,128)(2,1)}), bf16[32,16,256]{2,1,0:T(8,128)(2,1)S(1)}, u32[]{:S(2)}, u32[]{:S(2)}) async-start(bf16[32,16,256]{2,1,0:T(8,128)(2,1)} %bitcast.7), calls=%async_computation.5 | async-start | bytes 524288 | tf_op jit(solution)/shard_map/all_to_all | solution.py:245

commit v10 on v9

--- a/solution.py
+++ b/solution.py
@@ -203,6 +203,159 @@
         ],
     )
     got = lax.all_to_all(sent, plane, 0, 0, tiled=True)
+    sources, sites, half = other_ref.shape
+    blocks, parts, slab, share = out_ref.shape
+    span = parts * slab
+    rows = got_ref[:, :, :span].reshape(sources * sites, span)
+    for turn in range(2):
+        gains = (got_ref[:, :, span:] if turn == 0 else other_ref[...]).reshape(sources * sites, half)
+        partial = lax.dot_general(rows, gains, (((0,), (0,)), ((), ())), preferred_element_type=jnp.float32)
+        partial = partial.astype(out_ref.dtype)
+        first = (core_ref[0] ^ turn) * (blocks // 2)
+        for block in range(blocks // 2):
+            for part in range(parts):
+                out_ref[first + block, part] = partial[part * slab:(part + 1) * slab, block * share:(block + 1) * share]
+
+
+def shifted(value, by, fill):
+    count = value.shape[0]
+    row = lax.broadcasted_iota(jnp.int32, value.shape, 0)
+    moved = pltpu.roll(value, by % count, 0)
+    inside = row >= by if by > 0 else row < count + by
+    return jnp.where(inside, moved, fill)
+
+
+def across(rate, states, sign):
+    step = 1
+    while step < ROWS:
+        states = [s + rate * shifted(s, sign * step, 0.0) for s in states]
+        rate = rate * shifted(rate, sign * step, 1.0)
+        step *= 2
+    return shifted(rate, sign, 1.0), [shifted(s, sign, 0.0) for s in states]
+
+
+def scan_kernel(parts_ref, decay_ref, persist_ref, smooth_ref, entry_ref, product_ref, summary_ref, inj):
+    sources, slab, width = parts_ref.shape
+    total = parts_ref[0].astype(jnp.float32)
+    for source in range(1, sources):
+        total = total + parts_ref[source].astype(jnp.float32)
+    inj[...] = jnp.sqrt(1.0 - decay_ref[...] * decay_ref[...]) * total
+    depth = slab // ROWS
+    persist = persist_ref[...]
+
+    def rows(ref, j):
+        return ref[pl.ds(j, ROWS, stride=depth), :]
+
+    decays = [rows(decay_ref, j) for j in range(depth)]
+    decayed, local = [decays[0]], [rows(inj, 0)]
+    for j in range(1, depth):
+        decayed.append(decays[j] * decayed[-1])
+        local.append(decays[j] * local[-1] + rows(inj, j))
+    enter_rate, (enter,) = across(decayed[-1], [local[-1]], 1)
+    local = [h + a * enter for h, a in zip(local, decayed)]
+    decayed = [a * enter_rate for a in decayed]
+    products, smooth, entry = [None] * depth, [None] * depth, [None] * depth
+    for j in reversed(range(depth)):
+        rate = persist * decays[j]
+        keep = 1.0 - rate * decays[j]
+        if j == depth - 1:
+            products[j], smooth[j], entry[j] = rate, keep * local[j], keep * decayed[j]
+        else:
+            products[j] = rate * products[j + 1]
+            smooth[j] = rate * smooth[j + 1] + keep * local[j]
+            entry[j] = rate * entry[j + 1] + keep * decayed[j]
+    leave_rate, (leave_smooth, leave_entry) = across(products[0], [smooth[0], entry[0]], -1)
+    for j in range(depth):
+        smooth[j] = smooth[j] + products[j] * leave_smooth
+        entry[j] = entry[j] + products[j] * leave_entry
+        products[j] = products[j] * leave_rate
+        smooth_ref[pl.ds(j, ROWS, stride=depth), :] = smooth[j]
+        entry_ref[pl.ds(j, ROWS, stride=depth), :] = entry[j]
+        product_ref[pl.ds(j, ROWS, stride=depth), :] = products[j]
+    summary = [decayed[-1][ROWS - 1:], local[-1][ROWS - 1:], products[0][:1], smooth[0][:1], entry[0][:1]]
+    summary = jnp.concatenate(summary + [jnp.zeros((3, width), jnp.float32)], axis=0)
+    for to in range(summary_ref.shape[0]):
+        summary_ref[to] = summary
+
+
+def finish_kernel(place_ref, slabs_ref, smooth_ref, entry_ref, product_ref, rounded_ref, fwd, bwd):
+    count, _, width = slabs_ref.shape
+
+    def of(at, what):
+        return slabs_ref[at, what:what + 1, :]
+
+    state = jnp.zeros((1, width), jnp.float32)
+    for at in range(count):
+        fwd[at:at + 1, :] = state
+        state = of(at, 0) * state + of(at, 1)
+    state = jnp.zeros((1, width), jnp.float32)
+    for at in reversed(range(count)):
+        bwd[at:at + 1, :] = state
+        state = of(at, 2) * state + (of(at, 3) + of(at, 4) * fwd[at:at + 1, :])
+    place = place_ref[0]
+    f_in, g_in = fwd[pl.ds(place, 1), :], bwd[pl.ds(place, 1), :]
+    smoothed = smooth_ref[...] + entry_ref[...] * f_in + product_ref[...] * g_in
+    rounded = smoothed.T.astype(rounded_ref.dtype)
+    for to in range(rounded_ref.shape[0]):
+        rounded_ref[to] = rounded
+
+
+def predict_kernel(where_ref, near_ref, far_ref, mine_ref, pair_ref, out_ref):
+    blocks, share, slab = mine_ref.shape
+    pairs, _, sites, span = out_ref.shape
+    first, core = where_ref[0] == 0, where_ref[1]
+    mine, pair = mine_ref[...].reshape(blocks * share, slab), pair_ref[...].reshape(blocks * share, slab)
+    states = jnp.concatenate([jnp.where(first, mine, pair), jnp.where(first, pair, mine)], axis=1)
+    loadings = jnp.concatenate([near_ref[...], far_ref[...]], axis=0)
+    predicted = jnp.dot(loadings, states, preferred_element_type=jnp.float32)
+    predicted = predicted.astype(out_ref.dtype).reshape(2, pairs, sites, span)
+    for other in range(2):
+        out_ref[:, core ^ other] = predicted[other]
+
+
+def call(kernel, name, out_shape, *args, scratch=(), scalars=0, vmem=32, **grid):
+    if "in_specs" not in grid:
+        specs = [pl.BlockSpec(memory_space=pltpu.SMEM)] * scalars
+        specs += [pl.BlockSpec(memory_space=pltpu.VMEM)] * (len(args) - scalars)
+        grid = dict(in_specs=specs)
+    return pl.pallas_call(
+        kernel,
+        out_shape=out_shape,
+        scratch_shapes=list(scratch),
+        compiler_params=pltpu.CompilerParams(vmem_limit_bytes=vmem << 20),
+        name=name,
+        **grid,
+    )(*args)
+
+
+def per_device(observations, site_start, site_count, site_gain, site_loading, decay, persistence):
+    planes, col, plane = ("zh", "zl"), ("y", "core"), ("x", "y", "core")
+    line = plane + ("zl",)
+    blocks, parts, nc = lax.axis_size("zh"), lax.axis_size("zl"), lax.axis_size(col)
+    devices, slabs = lax.axis_size(plane), lax.axis_size(line)
+    sites, epochs = observations.shape
+    slab, span = epochs // slabs, epochs // devices
+    basis = site_gain.shape[1]
+    share = basis // blocks
+    f32, bf16 = jnp.float32, jnp.bfloat16
+    shape = jax.ShapeDtypeStruct
+    turn = [
+        ((h * parts + l) * nc + c, (c * parts + l) * nc + h)
+        for h in range(blocks) for l in range(parts) for c in range(nc)
+    ]
+
+    hbm, smem = pl.BlockSpec(memory_space=pl.ANY), pltpu.SMEM
+    sent = call(
+        front_kernel, "front", shape((devices, sites, span + basis // 2), bf16),
+        site_start, site_count, observations, site_gain, in_specs=[hbm] * 4, out_specs=hbm, vmem=60,
+        scratch=[
+            smem((sites,), jnp.int32), smem((sites,), jnp.int32),
+            pltpu.VMEM((sites, epochs), bf16), pltpu.VMEM((sites, basis), bf16),
+            pltpu.VMEM((devices, sites, span + basis // 2), bf16),
+            pltpu.SemaphoreType.DMA((3,)), pltpu.SemaphoreType.DMA((STEPS,)), pltpu.SemaphoreType.DMA((STEPS,)),
+        ],
+    )
+    got = lax.all_to_all(sent, plane, 0, 0, tiled=True)
     own = lax.dynamic_slice_in_dim(decay, lax.axis_index(col) * share, share, 1)
     decays = lax.ppermute(own, planes + col, turn)
     persist = lax.dynamic_slice_in_dim(persistence, lax.axis_index("zh") * share, share, 0)[None]
@@ -210,6 +363,10 @@
 
     swap = [(0, 1), (1, 0)]
     other = lax.ppermute(got[:, :, span:], "core", swap)
+    own = lax.dynamic_slice_in_dim(decay, lax.axis_index(col) * share, share, 1)
+    decays = lax.ppermute(own, planes + col, turn)
+    persist = lax.dynamic_slice_in_dim(persistence, lax.axis_index("zh") * share, share, 0)[None]
+    other, decays, persist = lax.optimization_barrier((other, decays, persist))
     core = lax.axis_index("core").astype(jnp.int32)
     partial = call(drive_kernel, "drive", shape((blocks, parts, slab, share), bf16), core[None], got, other, scalars=1)
     summed = lax.all_to_all(partial.reshape(blocks * parts, slab, share), planes, 0, 0, tiled=True)

time: 152 us -> 152 us (level)
  no operation moved by 1% of the time
where the time goes in v10:
time: 152 us; the launch traced here: 151 us
  starting transfers between devices  64.2 us (42%)
  blocking collectives  42.4 us (28%)
  waiting for transfers between devices  34.9 us (23%)
  Pallas kernels  6.65 us (4%)
  local copies, waits for them, and re-layouts  2.3 us (2%)
    all_to_all x1, blocking collectives, per_device(): mine = lax.all_to_all(rounded, 'zh', 0, 0, tiled=True)  22.5 us
    all_gather x1, blocking collectives, per_device(): near = lax.all_gather(near, ('x', 'y'), axis=0, tiled=True)  19.9 us
    all_to_all x1, starting transfers between devices, per_device(): lax.all_to_all(partial.reshape(blocks * parts, slab, share), planes, 0, 0...  16.3 us
    all_to_all x1, starting transfers between devices, per_device(): summaries = lax.all_to_all(summary, line, 0, 0, tiled=True)  15.4 us
    all_to_all x1, starting transfers between devices, per_device(): got = lax.all_to_all(sent, plane, 0, 0, tiled=True)  10.4 us
    all_to_all x1, waiting for transfers between devices, per_device(): lax.all_to_all(predicted.reshape(devices, sites, span), plane, 0, 0, tile...  8.23 us
    all_to_all x1, starting transfers between devices, per_device(): own = lax.all_to_all(mine, col, 0, 0, tiled=True)  7.84 us
    all_to_all x1, waiting for transfers between devices, per_device(): got = lax.all_to_all(sent, plane, 0, 0, tiled=True)  6.83 us
  transfers between devices with their start and end apart: 9, of which 8 were waited for; matrix products, arithmetic and copies ran while one was open for 1% of the time, Pallas kernels for 1%

profile of v10, /device:TPU:1, one launch (start us, length us, event | category | flops | bytes accessed | tf_op | source)
XLA Modules:
  0.0 151.3 jit_solution(7177903320144537029)
XLA Ops:
  0.6 0.0 copy-start
  0.6 2.0 %front.1 = bf16[32,16,768]{2,1,0:T(8,128)(2,1)} custom-call(s32[16]{0:T(128)} %start_hbm.1, s32[16]{0:T(128)} %count_hbm.1, bf16[16,8192]{1,0:T(8,128)(2,1)} %values_hbm.1, bf16[16,1024]{1,0:T(8,128)(2,1)} %gain_hbm.1), custom_call_target="tpu_custom_call" | custom-call | tf_op jit(solution)/shard_map/front/pallas_call | solution.py:321
  2.6 10.4 %all-to-all-start = ((bf16[32,16,768]{2,1,0:T(8,128)(2,1)}), bf16[32,16,768]{2,1,0:T(8,128)(2,1)S(1)}, u32[]{:S(2)}, u32[]{:S(2)}) async-start(bf16[32,16,768]{2,1,0:T(8,128)(2,1)} %front.1), calls=%async_computation | async-start | bytes 1572864 | tf_op jit(solution)/shard_map/all_to_all | solution.py:358
  13.1 0.0 copy-done
  13.1 3.2 %collective-permute-start = (f32[128,128]{1,0:T(8,128)S(1)}, f32[128,128]{1,0:T(8,128)S(1)}, u32[]{:S(2)}, u32[]{:S(2)}) collective-permute-start(f32[128,128]{1,0:T(8,128)S(1)} %constant_dynamic-slice_fusion), channel_id=1, source_target_pairs={{0,0},{1,16},{2,32},{3,48},{4,64},{5,80},{6,96},{7,112},{8,8},{9,2... | collective-permute-start | bytes 196616 | tf_op jit(solution)/shard_map/ppermute | solution.py:360
  16.3 0.8 dynamic-slice_bitcast_fusion.persist_ref
  17.1 3.5 %collective-permute-done.decay_ref = f32[128,128]{1,0:T(8,128)S(1)} collective-permute-done((f32[128,128]{1,0:T(8,128)S(1)}, f32[128,128]{1,0:T(8,128)S(1)}, u32[]{:S(2)}, u32[]{:S(2)}) %collective-permute-start) | collective-permute-done | bytes 65568 | tf_op jit(solution)/shard_map/ppermute | solution.py:360
  20.6 6.8 %all-to-all-done.got_ref = bf16[32,16,768]{2,1,0:T(8,128)(2,1)S(1)} async-done(((bf16[32,16,768]{2,1,0:T(8,128)(2,1)}), bf16[32,16,768]{2,1,0:T(8,128)(2,1)S(1)}, u32[]{:S(2)}, u32[]{:S(2)}) %all-to-all-start) | async-done | bytes 786464 | tf_op jit(solution)/shard_map/all_to_all | solution.py:358
  27.4 0.1 slice.3
  27.5 1.9 %collective-permute-start.1 = (bf16[32,16,512]{2,1,0:T(8,128)(2,1)S(1)}, bf16[32,16,512]{2,1,0:T(8,128)(2,1)S(1)}, u32[]{:S(2)}, u32[]{:S(2)}) collective-permute-start(bf16[32,16,512]{2,1,0:T(8,128)(2,1)S(1)} %slice.3), channel_id=1, source_target_pairs={{0,1},{1,0},{2,3},{3,2},{4,5},{5,4},{6,7},{7,6},{8,9},{9,8},{10,11... | collective-permute-start | bytes 1572872 | tf_op jit(solution)/shard_map/ppermute | solution.py:365
  29.4 1.9 %collective-permute-done.1.other_ref = bf16[32,16,512]{2,1,0:T(8,128)(2,1)S(1)} collective-permute-done((bf16[32,16,512]{2,1,0:T(8,128)(2,1)S(1)}, bf16[32,16,512]{2,1,0:T(8,128)(2,1)S(1)}, u32[]{:S(2)}, u32[]{:S(2)}) %collective-permute-start.1) | collective-permute-done | bytes 524320 | tf_op jit(solution)/shard_map/ppermute | solution.py:365
  31.3 1.3 drive.1
  32.5 0.0 copy-start.1
  32.5 16.3 %all-to-all-start.1 = ((bf16[16,128,128]{2,1,0:T(8,128)(2,1)}), bf16[16,128,128]{2,1,0:T(8,128)(2,1)S(1)}, u32[]{:S(2)}, u32[]{:S(2)}) async-start(bf16[16,128,128]{2,1,0:T(8,128)(2,1)} %bitcast.3), calls=%async_computation.1 | async-start | bytes 1048576 | tf_op jit(solution)/shard_map/all_to_all | solution.py:372
  48.9 0.0 copy-done.1
  48.9 19.9 %all_gather.3.near_ref = bf16[256,1024]{1,0:T(8,128)(2,1)S(1)} all-gather(bf16[16,1024]{1,0:T(8,128)(2,1)S(1)} %copy-done.1), channel_id=1, replica_groups=mesh['x'=4,'zh'=8,'zl'=2,'y'=4,'core'=2] {'x','y'}, dimensions={0}, use_global_device_ids=true | all-gather | bytes 557056 | tf_op jit(solution)/shard_map/all_gather | solution.py:374
  68.8 2.8 %all-to-all-done.1.parts_ref = bf16[16,128,128]{2,1,0:T(8,128)(2,1)S(1)} async-done(((bf16[16,128,128]{2,1,0:T(8,128)(2,1)}), bf16[16,128,128]{2,1,0:T(8,128)(2,1)S(1)}, u32[]{:S(2)}, u32[]{:S(2)}) %all-to-all-start.1) | async-done | bytes 524320 | tf_op jit(solution)/shard_map/all_to_all | solution.py:372
  71.6 1.0 scan.1
  72.6 15.4 %all-to-all-start.2 = ((f32[64,8,128]{2,1,0:T(8,128)}), f32[64,8,128]{2,1,0:T(8,128)S(1)}, u32[]{:S(2)}, u32[]{:S(2)}) async-start(f32[64,8,128]{2,1,0:T(8,128)} %get-tuple-element.24), calls=%async_computation.2 | async-start | bytes 524288 | tf_op jit(solution)/shard_map/all_to_all | solution.py:381
  88.0 2.4 %collective-permute-start.2 = (bf16[256,1024]{1,0:T(8,128)(2,1)S(1)}, bf16[256,1024]{1,0:T(8,128)(2,1)S(1)}, u32[]{:S(2)}, u32[]{:S(2)}) collective-permute-start(bf16[256,1024]{1,0:T(8,128)(2,1)S(1)} %all_gather.3.near_ref), channel_id=1, source_target_pairs={{0,1},{1,0},{2,3},{3,2},{4,5},{5,4},{6,7},{7,6},{8,9},{9,8},{10,11... | collective-permute-start | bytes 1572872 | tf_op jit(solution)/shard_map/ppermute | solution.py:382
  90.4 1.5 collective-permute-done.2.far_ref
  91.9 5.7 %all-to-all-done.2.slabs_ref = f32[64,8,128]{2,1,0:T(8,128)S(1)} async-done(((f32[64,8,128]{2,1,0:T(8,128)}), f32[64,8,128]{2,1,0:T(8,128)S(1)}, u32[]{:S(2)}, u32[]{:S(2)}) %all-to-all-start.2) | async-done | bytes 262176 | tf_op jit(solution)/shard_map/all_to_all | solution.py:381
  97.7 0.4 finish.1
  98.0 22.5 %all_to_all.30.mine_ref = bf16[8,128,128]{2,1,0:T(8,128)(2,1)} all-to-all(bf16[8,128,128]{2,1,0:T(8,128)(2,1)S(1)} %finish.1), channel_id=1, replica_groups=mesh['x'=4,'zh'=8,'zl'=2,'y'=4,'core'=2] {'zh'}, dimensions={0} | all-to-all | bytes 524288 | tf_op jit(solution)/shard_map/all_to_all | solution.py:390
  120.6 1.9 %collective-permute-start.3 = (bf16[8,128,128]{2,1,0:T(8,128)(2,1)}, bf16[8,128,128]{2,1,0:T(8,128)(2,1)S(1)}, u32[]{:S(2)}, u32[]{:S(2)}) collective-permute-start(bf16[8,128,128]{2,1,0:T(8,128)(2,1)} %all_to_all.30.mine_ref), channel_id=1, source_target_pairs={{0,8},{8,0},{1,9},{9,1},{2,10},{10,2},{3,11},{11,3},{4,12},{12,4},... | collective-permute-start | bytes 786440 | tf_op jit(solution)/shard_map/ppermute | solution.py:391
  122.5 7.8 %all-to-all-start.4 = ((bf16[8,128,128]{2,1,0:T(8,128)(2,1)}), bf16[8,128,128]{2,1,0:T(8,128)(2,1)S(1)}, u32[]{:S(2)}, u32[]{:S(2)}) async-start(bf16[8,128,128]{2,1,0:T(8,128)(2,1)} %all_to_all.30.mine_ref), calls=%async_computation.4 | async-start | bytes 524288 | tf_op jit(solution)/shard_map/all_to_all | solution.py:392
  130.3 0.1 pad_add_fusion.where_ref
  130.4 0.0 collective-permute-done.3.pair_ref
  130.4 2.1 %predict.1 = bf16[16,2,16,256]{3,2,1,0:T(8,128)(2,1)} custom-call(s32[2]{0:T(128)S(1)} %pad_add_fusion.where_ref, bf16[256,1024]{1,0:T(8,128)(2,1)S(1)} %all_gather.3.near_ref, bf16[256,1024]{1,0:T(8,128)(2,1)S(1)} %collective-permute-done.2.far_ref, bf16[8,128,128]{2,1,0:T(8,128)(2,1)} %all_to_all.30.mine_ref, ...), custom_call_target="tpu_custom_call" | custom-call | tf_op jit(solution)/shard_map/predict/pallas_call | solution.py:321
  132.5 4.3 %all-to-all-done.4 = bf16[8,128,128]{2,1,0:T(8,128)(2,1)S(1)} async-done(((bf16[8,128,128]{2,1,0:T(8,128)(2,1)}), bf16[8,128,128]{2,1,0:T(8,128)(2,1)S(1)}, u32[]{:S(2)}, u32[]{:S(2)}) %all-to-all-start.4) | async-done | bytes 262176 | tf_op jit(solution)/shard_map/all_to_all | solution.py:392
  136.8 4.8 %all-to-all-start.5 = ((bf16[32,16,256]{2,1,0:T(8,128)(2,1)}), bf16[32,16,256]{2,1,0:T(8,128)(2,1)S(1)}, u32[]{:S(2)}, u32[]{:S(2)}) async-start(bf16[32,16,256]{2,1,0:T(8,128)(2,1)} %bitcast.7), calls=%async_computation.5 | async-start | bytes 524288 | tf_op jit(solution)/shard_map/all_to_all | solution.py:402
  141.7 0.7 copy.10
  142.4 8.2 %all-to-all-done.5 = bf16[32,16,256]{2,1,0:T(8,128)(2,1)S(1)} async-done(((bf16[32,16,256]{2,1,0:T(8,128)(2,1)}), bf16[32,16,256]{2,1,0:T(8,128)(2,1)S(1)}, u32[]{:S(2)}, u32[]{:S(2)}) %all-to-all-start.5) | async-done | bytes 262176 | tf_op jit(solution)/shard_map/all_to_all | solution.py:402
  150.6 0.7 copy.11
  (2 shorter events, 0.0 us)
Async XLA Ops:
  0.6 12.4 %copy-start = (f32[128,1024]{1,0:T(8,128)S(1)}, f32[128,1024]{1,0:T(8,128)}, u32[]{:S(2)}) copy-start(f32[128,1024]{1,0:T(8,128)} %param.12) | copy-start | bytes 1572868
  2.6 24.8 %all-to-all-start = ((bf16[32,16,768]{2,1,0:T(8,128)(2,1)}), bf16[32,16,768]{2,1,0:T(8,128)(2,1)S(1)}, u32[]{:S(2)}, u32[]{:S(2)}) async-start(bf16[32,16,768]{2,1,0:T(8,128)(2,1)} %front.1), calls=%async_computation | async-start | bytes 1572864 | tf_op jit(solution)/shard_map/all_to_all | solution.py:358
  13.1 7.5 %collective-permute-start = (f32[128,128]{1,0:T(8,128)S(1)}, f32[128,128]{1,0:T(8,128)S(1)}, u32[]{:S(2)}, u32[]{:S(2)}) collective-permute-start(f32[128,128]{1,0:T(8,128)S(1)} %constant_dynamic-slice_fusion), channel_id=1, source_target_pairs={{0,0},{1,16},{2,32},{3,48},{4,64},{5,80},{6,96},{7,112},{8,8},{9,2... | collective-permute-start | bytes 196616 | tf_op jit(solution)/shard_map/ppermute | solution.py:360
  27.5 3.8 %collective-permute-start.1 = (bf16[32,16,512]{2,1,0:T(8,128)(2,1)S(1)}, bf16[32,16,512]{2,1,0:T(8,128)(2,1)S(1)}, u32[]{:S(2)}, u32[]{:S(2)}) collective-permute-start(bf16[32,16,512]{2,1,0:T(8,128)(2,1)S(1)} %slice.3), channel_id=1, source_target_pairs={{0,1},{1,0},{2,3},{3,2},{4,5},{5,4},{6,7},{7,6},{8,9},{9,8},{10,11... | collective-permute-start | bytes 1572872 | tf_op jit(solution)/shard_map/ppermute | solution.py:365
  32.5 16.4 %copy-start.1 = (bf16[16,1024]{1,0:T(8,128)(2,1)S(1)}, bf16[16,1024]{1,0:T(8,128)(2,1)}, u32[]{:S(2)}) copy-start(bf16[16,1024]{1,0:T(8,128)(2,1)} %param.11) | copy-start | bytes 98308
  32.5 39.1 %all-to-all-start.1 = ((bf16[16,128,128]{2,1,0:T(8,128)(2,1)}), bf16[16,128,128]{2,1,0:T(8,128)(2,1)S(1)}, u32[]{:S(2)}, u32[]{:S(2)}) async-start(bf16[16,128,128]{2,1,0:T(8,128)(2,1)} %bitcast.3), calls=%async_computation.1 | async-start | bytes 1048576 | tf_op jit(solution)/shard_map/all_to_all | solution.py:372
  72.6 25.1 %all-to-all-start.2 = ((f32[64,8,128]{2,1,0:T(8,128)}), f32[64,8,128]{2,1,0:T(8,128)S(1)}, u32[]{:S(2)}, u32[]{:S(2)}) async-start(f32[64,8,128]{2,1,0:T(8,128)} %get-tuple-element.24), calls=%async_computation.2 | async-start | bytes 524288 | tf_op jit(solution)/shard_map/all_to_all | solution.py:381
  88.0 3.9 %collective-permute-start.2 = (bf16[256,1024]{1,0:T(8,128)(2,1)S(1)}, bf16[256,1024]{1,0:T(8,128)(2,1)S(1)}, u32[]{:S(2)}, u32[]{:S(2)}) collective-permute-start(bf16[256,1024]{1,0:T(8,128)(2,1)S(1)} %all_gather.3.near_ref), channel_id=1, source_target_pairs={{0,1},{1,0},{2,3},{3,2},{4,5},{5,4},{6,7},{7,6},{8,9},{9,8},{10,11... | collective-permute-start | bytes 1572872 | tf_op jit(solution)/shard_map/ppermute | solution.py:382
  120.6 9.8 %collective-permute-start.3 = (bf16[8,128,128]{2,1,0:T(8,128)(2,1)}, bf16[8,128,128]{2,1,0:T(8,128)(2,1)S(1)}, u32[]{:S(2)}, u32[]{:S(2)}) collective-permute-start(bf16[8,128,128]{2,1,0:T(8,128)(2,1)} %all_to_all.30.mine_ref), channel_id=1, source_target_pairs={{0,8},{8,0},{1,9},{9,1},{2,10},{10,2},{3,11},{11,3},{4,12},{12,4},... | collective-permute-start | bytes 786440 | tf_op jit(solution)/shard_map/ppermute | solution.py:391
  122.5 14.4 %all-to-all-start.4 = ((bf16[8,128,128]{2,1,0:T(8,128)(2,1)}), bf16[8,128,128]{2,1,0:T(8,128)(2,1)S(1)}, u32[]{:S(2)}, u32[]{:S(2)}) async-start(bf16[8,128,128]{2,1,0:T(8,128)(2,1)} %all_to_all.30.mine_ref), calls=%async_computation.4 | async-start | bytes 524288 | tf_op jit(solution)/shard_map/all_to_all | solution.py:392
  136.8 13.8 %all-to-all-start.5 = ((bf16[32,16,256]{2,1,0:T(8,128)(2,1)}), bf16[32,16,256]{2,1,0:T(8,128)(2,1)S(1)}, u32[]{:S(2)}, u32[]{:S(2)}) async-start(bf16[32,16,256]{2,1,0:T(8,128)(2,1)} %bitcast.7), calls=%async_computation.5 | async-start | bytes 524288 | tf_op jit(solution)/shard_map/all_to_all | solution.py:402

commit v11 on v5

--- a/solution.py
+++ b/solution.py
@@ -9,9 +9,8 @@
 STEPS = 4
 
 
-def front_kernel(start_hbm, count_hbm, values_hbm, gain_hbm, out_hbm, start, count, values, gain, out, small, large, sent):
-    devices, sites, width = out.shape
-    span = width - gain.shape[1]
+def front_kernel(start_hbm, count_hbm, values_hbm, gain_hbm, out_hbm, start, count, values, gain, copies, out, small, large, sent, gains_sent):
+    devices, sites, span = out.shape
     wide, each = values.shape[1] // STEPS, devices // STEPS
     arriving = [
         pltpu.make_async_copy(start_hbm, start, small.at[0]),
@@ -24,6 +23,14 @@
         chunks.append(pltpu.make_async_copy(values_hbm.at[part], values.at[part], large.at[step]))
     for copy in arriving + chunks:
         copy.start()
+    arriving.pop().wait()
+    leaving = []
+    for at in range(each):
+        copies[at] = gain[...]
+    for step in range(STEPS):
+        part = (pl.ds(step * each, each), slice(None), pl.ds(span, gain.shape[1]))
+        leaving.append(pltpu.make_async_copy(copies, out_hbm.at[part], gains_sent.at[step]))
+        leaving[-1].start()
     for copy in arriving:
         copy.wait()
     site = lax.broadcasted_iota(jnp.int32, (sites, span), 0)
@@ -32,17 +39,14 @@
         first = jnp.where(site == s, start[s], first)
         end = jnp.where(site == s, start[s] + count[s], end)
     epoch = lax.broadcasted_iota(jnp.int32, (sites, span), 1)
-    gains = gain[...]
-    leaving = []
     for step in range(STEPS):
         chunks[step].wait()
         for to in range(step * each, (step + 1) * each):
             own = values[:, to * span:(to + 1) * span].astype(jnp.float32)
             inside = (epoch + to * span >= first) & (epoch + to * span < end)
-            out[to, :, :span] = jnp.where(inside, own, 0.0).astype(out.dtype)
-            out[to, :, span:] = gains
+            out[to] = jnp.where(inside, own, 0.0).astype(out.dtype)
         part = pl.ds(step * each, each)
-        leaving.append(pltpu.make_async_copy(out.at[part], out_hbm.at[part], sent.at[step]))
+        leaving.append(pltpu.make_async_copy(out.at[part], out_hbm.at[part, slice(None), pl.ds(0, span)], sent.at[step]))
         leaving[-1].start()
     for copy in leaving:
         copy.wait()
@@ -195,8 +199,9 @@
         scratch=[
             smem((sites,), jnp.int32), smem((sites,), jnp.int32),
             pltpu.VMEM((sites, epochs), bf16), pltpu.VMEM((sites, basis), bf16),
-            pltpu.VMEM((devices, sites, span + basis), bf16),
+            pltpu.VMEM((devices // STEPS, sites, basis), bf16), pltpu.VMEM((devices, sites, span), bf16),
             pltpu.SemaphoreType.DMA((3,)), pltpu.SemaphoreType.DMA((STEPS,)), pltpu.SemaphoreType.DMA((STEPS,)),
+            pltpu.SemaphoreType.DMA((STEPS,)),
         ],
     )
     got = lax.all_to_all(sent, plane, 0, 0, tiled=True)

time: 149 us -> 149 us (level)
  no operation moved by 1% of the time
where the time goes in v11:
time: 149 us
  starting transfers between devices  57.8 us (39%)
  blocking collectives  41.2 us (28%)
  waiting for transfers between devices  39.6 us (27%)
  Pallas kernels  6.86 us (5%)
  local copies, waits for them, and re-layouts  2.24 us (2%)
    all_to_all x1, blocking collectives, per_device(): mine = lax.all_to_all(rounded, 'zh', 0, 0, tiled=True)  22.2 us
    all_gather x1, blocking collectives, per_device(): near = lax.all_gather(near, ('x', 'y'), axis=0, tiled=True)  19 us
    all_to_all x1, starting transfers between devices, per_device(): lax.all_to_all(partial.reshape(blocks * parts, slab, share), planes, 0, 0...  13.8 us
    all_to_all x1, starting transfers between devices, per_device(): summaries = lax.all_to_all(summary, line, 0, 0, tiled=True)  13.6 us
    all_to_all x1, waiting for transfers between devices, per_device(): got = lax.all_to_all(sent, plane, 0, 0, tiled=True)  12.4 us
    all_to_all x1, starting transfers between devices, per_device(): got = lax.all_to_all(sent, plane, 0, 0, tiled=True)  10.5 us
    all_to_all x1, waiting for transfers between devices, per_device(): lax.all_to_all(predicted.reshape(devices, sites, span), plane, 0, 0, tile...  8.23 us
    all_to_all x1, starting transfers between devices, per_device(): own = lax.all_to_all(mine, col, 0, 0, tiled=True)  7.84 us
  transfers between devices with their start and end apart: 8, of which 7 were waited for; matrix products, arithmetic and copies ran while one was open for 1% of the time, Pallas kernels for 1%

profile of v11, /device:TPU:1, one launch (start us, length us, event | category | flops | bytes accessed | tf_op | source)
XLA Modules:
  0.0 148.6 jit_solution(14715984096534539114)
XLA Ops:
  0.6 0.0 copy-start
  0.6 2.2 %front.1 = bf16[32,16,1280]{2,1,0:T(8,128)(2,1)} custom-call(s32[16]{0:T(128)} %start_hbm.1, s32[16]{0:T(128)} %count_hbm.1, bf16[16,8192]{1,0:T(8,128)(2,1)} %values_hbm.1, bf16[16,1024]{1,0:T(8,128)(2,1)} %gain_hbm.1), custom_call_target="tpu_custom_call" | custom-call | tf_op jit(solution)/shard_map/front/pallas_call | solution.py:169
  2.8 10.5 %all-to-all-start = ((bf16[32,16,1280]{2,1,0:T(8,128)(2,1)}), bf16[32,16,1280]{2,1,0:T(8,128)(2,1)S(1)}, u32[]{:S(2)}, u32[]{:S(2)}) async-start(bf16[32,16,1280]{2,1,0:T(8,128)(2,1)} %front.1), calls=%async_computation | async-start | bytes 2621440 | tf_op jit(solution)/shard_map/all_to_all | solution.py:207
  13.3 0.0 copy-done
  13.4 3.1 %collective-permute-start = (f32[128,128]{1,0:T(8,128)S(1)}, f32[128,128]{1,0:T(8,128)S(1)}, u32[]{:S(2)}, u32[]{:S(2)}) collective-permute-start(f32[128,128]{1,0:T(8,128)S(1)} %constant_dynamic-slice_fusion), channel_id=1, source_target_pairs={{0,0},{1,16},{2,32},{3,48},{4,64},{5,80},{6,96},{7,112},{8,8},{9,2... | collective-permute-start | bytes 196616 | tf_op jit(solution)/shard_map/ppermute | solution.py:209
  16.5 0.8 dynamic-slice_bitcast_fusion.persist_ref
  17.3 0.0 copy-start.1
  17.3 3.5 %collective-permute-done.decay_ref = f32[128,128]{1,0:T(8,128)S(1)} collective-permute-done((f32[128,128]{1,0:T(8,128)S(1)}, f32[128,128]{1,0:T(8,128)S(1)}, u32[]{:S(2)}, u32[]{:S(2)}) %collective-permute-start) | collective-permute-done | bytes 65568 | tf_op jit(solution)/shard_map/ppermute | solution.py:209
  20.8 12.4 %all-to-all-done.got_ref = bf16[32,16,1280]{2,1,0:T(8,128)(2,1)S(1)} async-done(((bf16[32,16,1280]{2,1,0:T(8,128)(2,1)}), bf16[32,16,1280]{2,1,0:T(8,128)(2,1)S(1)}, u32[]{:S(2)}, u32[]{:S(2)}) %all-to-all-start) | async-done | bytes 1310752 | tf_op jit(solution)/shard_map/all_to_all | solution.py:207
  33.2 1.2 drive.1
  34.5 13.8 %all-to-all-start.1 = ((bf16[16,128,128]{2,1,0:T(8,128)(2,1)}), bf16[16,128,128]{2,1,0:T(8,128)(2,1)S(1)}, u32[]{:S(2)}, u32[]{:S(2)}) async-start(bf16[16,128,128]{2,1,0:T(8,128)(2,1)} %bitcast.3), calls=%async_computation.1 | async-start | bytes 1048576 | tf_op jit(solution)/shard_map/all_to_all | solution.py:214
  48.2 0.0 copy-done.1
  48.2 19.0 %all_gather.3.near_ref = bf16[256,1024]{1,0:T(8,128)(2,1)S(1)} all-gather(bf16[16,1024]{1,0:T(8,128)(2,1)S(1)} %copy-done.1), channel_id=1, replica_groups=mesh['x'=4,'zh'=8,'zl'=2,'y'=4,'core'=2] {'x','y'}, dimensions={0}, use_global_device_ids=true | all-gather | bytes 557056 | tf_op jit(solution)/shard_map/all_gather | solution.py:216
  67.2 3.9 %all-to-all-done.1.parts_ref = bf16[16,128,128]{2,1,0:T(8,128)(2,1)S(1)} async-done(((bf16[16,128,128]{2,1,0:T(8,128)(2,1)}), bf16[16,128,128]{2,1,0:T(8,128)(2,1)S(1)}, u32[]{:S(2)}, u32[]{:S(2)}) %all-to-all-start.1) | async-done | bytes 524320 | tf_op jit(solution)/shard_map/all_to_all | solution.py:214
  71.1 1.0 scan.1
  72.0 13.6 %all-to-all-start.2 = ((f32[64,8,128]{2,1,0:T(8,128)}), f32[64,8,128]{2,1,0:T(8,128)S(1)}, u32[]{:S(2)}, u32[]{:S(2)}) async-start(f32[64,8,128]{2,1,0:T(8,128)} %get-tuple-element.22), calls=%async_computation.2 | async-start | bytes 524288 | tf_op jit(solution)/shard_map/all_to_all | solution.py:223
  85.6 2.4 %collective-permute-start.1 = (bf16[256,1024]{1,0:T(8,128)(2,1)S(1)}, bf16[256,1024]{1,0:T(8,128)(2,1)S(1)}, u32[]{:S(2)}, u32[]{:S(2)}) collective-permute-start(bf16[256,1024]{1,0:T(8,128)(2,1)S(1)} %all_gather.3.near_ref), channel_id=1, source_target_pairs={{0,1},{1,0},{2,3},{3,2},{4,5},{5,4},{6,7},{7,6},{8,9},{9,8},{10,11... | collective-permute-start | bytes 1572872 | tf_op jit(solution)/shard_map/ppermute | solution.py:224
  88.0 1.5 %collective-permute-done.1.far_ref = bf16[256,1024]{1,0:T(8,128)(2,1)S(1)} collective-permute-done((bf16[256,1024]{1,0:T(8,128)(2,1)S(1)}, bf16[256,1024]{1,0:T(8,128)(2,1)S(1)}, u32[]{:S(2)}, u32[]{:S(2)}) %collective-permute-start.1) | collective-permute-done | bytes 524320 | tf_op jit(solution)/shard_map/ppermute | solution.py:224
  89.5 5.7 %all-to-all-done.2.slabs_ref = f32[64,8,128]{2,1,0:T(8,128)S(1)} async-done(((f32[64,8,128]{2,1,0:T(8,128)}), f32[64,8,128]{2,1,0:T(8,128)S(1)}, u32[]{:S(2)}, u32[]{:S(2)}) %all-to-all-start.2) | async-done | bytes 262176 | tf_op jit(solution)/shard_map/all_to_all | solution.py:223
  95.2 0.4 finish.1
  95.6 22.2 %all_to_all.30.mine_ref = bf16[8,128,128]{2,1,0:T(8,128)(2,1)} all-to-all(bf16[8,128,128]{2,1,0:T(8,128)(2,1)S(1)} %finish.1), channel_id=1, replica_groups=mesh['x'=4,'zh'=8,'zl'=2,'y'=4,'core'=2] {'zh'}, dimensions={0} | all-to-all | bytes 524288 | tf_op jit(solution)/shard_map/all_to_all | solution.py:232
  117.8 1.9 %collective-permute-start.2 = (bf16[8,128,128]{2,1,0:T(8,128)(2,1)}, bf16[8,128,128]{2,1,0:T(8,128)(2,1)S(1)}, u32[]{:S(2)}, u32[]{:S(2)}) collective-permute-start(bf16[8,128,128]{2,1,0:T(8,128)(2,1)} %all_to_all.30.mine_ref), channel_id=1, source_target_pairs={{0,8},{8,0},{1,9},{9,1},{2,10},{10,2},{3,11},{11,3},{4,12},{12,4},... | collective-permute-start | bytes 786440 | tf_op jit(solution)/shard_map/ppermute | solution.py:233
  119.7 7.8 %all-to-all-start.4 = ((bf16[8,128,128]{2,1,0:T(8,128)(2,1)}), bf16[8,128,128]{2,1,0:T(8,128)(2,1)S(1)}, u32[]{:S(2)}, u32[]{:S(2)}) async-start(bf16[8,128,128]{2,1,0:T(8,128)(2,1)} %all_to_all.30.mine_ref), calls=%async_computation.4 | async-start | bytes 524288 | tf_op jit(solution)/shard_map/all_to_all | solution.py:234
  127.6 0.1 pad_add_fusion.where_ref
  127.7 0.0 collective-permute-done.2.pair_ref
  127.7 2.1 %predict.1 = bf16[16,2,16,256]{3,2,1,0:T(8,128)(2,1)} custom-call(s32[2]{0:T(128)S(1)} %pad_add_fusion.where_ref, bf16[256,1024]{1,0:T(8,128)(2,1)S(1)} %all_gather.3.near_ref, bf16[256,1024]{1,0:T(8,128)(2,1)S(1)} %collective-permute-done.1.far_ref, bf16[8,128,128]{2,1,0:T(8,128)(2,1)} %all_to_all.30.mine_ref, ...), custom_call_target="tpu_custom_call" | custom-call | tf_op jit(solution)/shard_map/predict/pallas_call | solution.py:169
  129.8 4.3 %all-to-all-done.4 = bf16[8,128,128]{2,1,0:T(8,128)(2,1)S(1)} async-done(((bf16[8,128,128]{2,1,0:T(8,128)(2,1)}), bf16[8,128,128]{2,1,0:T(8,128)(2,1)S(1)}, u32[]{:S(2)}, u32[]{:S(2)}) %all-to-all-start.4) | async-done | bytes 262176 | tf_op jit(solution)/shard_map/all_to_all | solution.py:234
  134.1 4.8 %all-to-all-start.5 = ((bf16[32,16,256]{2,1,0:T(8,128)(2,1)}), bf16[32,16,256]{2,1,0:T(8,128)(2,1)S(1)}, u32[]{:S(2)}, u32[]{:S(2)}) async-start(bf16[32,16,256]{2,1,0:T(8,128)(2,1)} %bitcast.7), calls=%async_computation.5 | async-start | bytes 524288 | tf_op jit(solution)/shard_map/all_to_all | solution.py:244
  138.9 0.7 copy.10
  139.7 8.2 %all-to-all-done.5 = bf16[32,16,256]{2,1,0:T(8,128)(2,1)S(1)} async-done(((bf16[32,16,256]{2,1,0:T(8,128)(2,1)}), bf16[32,16,256]{2,1,0:T(8,128)(2,1)S(1)}, u32[]{:S(2)}, u32[]{:S(2)}) %all-to-all-start.5) | async-done | bytes 262176 | tf_op jit(solution)/shard_map/all_to_all | solution.py:244
  147.9 0.7 copy.11
  (2 shorter events, 0.0 us)
Async XLA Ops:
  0.6 12.7 %copy-start = (f32[128,1024]{1,0:T(8,128)S(1)}, f32[128,1024]{1,0:T(8,128)}, u32[]{:S(2)}) copy-start(f32[128,1024]{1,0:T(8,128)} %param.12) | copy-start | bytes 1572868
  2.8 30.4 %all-to-all-start = ((bf16[32,16,1280]{2,1,0:T(8,128)(2,1)}), bf16[32,16,1280]{2,1,0:T(8,128)(2,1)S(1)}, u32[]{:S(2)}, u32[]{:S(2)}) async-start(bf16[32,16,1280]{2,1,0:T(8,128)(2,1)} %front.1), calls=%async_computation | async-start | bytes 2621440 | tf_op jit(solution)/shard_map/all_to_all | solution.py:207
  13.4 7.4 %collective-permute-start = (f32[128,128]{1,0:T(8,128)S(1)}, f32[128,128]{1,0:T(8,128)S(1)}, u32[]{:S(2)}, u32[]{:S(2)}) collective-permute-start(f32[128,128]{1,0:T(8,128)S(1)} %constant_dynamic-slice_fusion), channel_id=1, source_target_pairs={{0,0},{1,16},{2,32},{3,48},{4,64},{5,80},{6,96},{7,112},{8,8},{9,2... | collective-permute-start | bytes 196616 | tf_op jit(solution)/shard_map/ppermute | solution.py:209
  17.3 30.9 %copy-start.1 = (bf16[16,1024]{1,0:T(8,128)(2,1)S(1)}, bf16[16,1024]{1,0:T(8,128)(2,1)}, u32[]{:S(2)}) copy-start(bf16[16,1024]{1,0:T(8,128)(2,1)} %param.11) | copy-start | bytes 98308
  34.5 36.6 %all-to-all-start.1 = ((bf16[16,128,128]{2,1,0:T(8,128)(2,1)}), bf16[16,128,128]{2,1,0:T(8,128)(2,1)S(1)}, u32[]{:S(2)}, u32[]{:S(2)}) async-start(bf16[16,128,128]{2,1,0:T(8,128)(2,1)} %bitcast.3), calls=%async_computation.1 | async-start | bytes 1048576 | tf_op jit(solution)/shard_map/all_to_all | solution.py:214
  72.0 23.2 %all-to-all-start.2 = ((f32[64,8,128]{2,1,0:T(8,128)}), f32[64,8,128]{2,1,0:T(8,128)S(1)}, u32[]{:S(2)}, u32[]{:S(2)}) async-start(f32[64,8,128]{2,1,0:T(8,128)} %get-tuple-element.22), calls=%async_computation.2 | async-start | bytes 524288 | tf_op jit(solution)/shard_map/all_to_all | solution.py:223
  85.6 3.9 %collective-permute-start.1 = (bf16[256,1024]{1,0:T(8,128)(2,1)S(1)}, bf16[256,1024]{1,0:T(8,128)(2,1)S(1)}, u32[]{:S(2)}, u32[]{:S(2)}) collective-permute-start(bf16[256,1024]{1,0:T(8,128)(2,1)S(1)} %all_gather.3.near_ref), channel_id=1, source_target_pairs={{0,1},{1,0},{2,3},{3,2},{4,5},{5,4},{6,7},{7,6},{8,9},{9,8},{10,11... | collective-permute-start | bytes 1572872 | tf_op jit(solution)/shard_map/ppermute | solution.py:224
  117.8 9.8 %collective-permute-start.2 = (bf16[8,128,128]{2,1,0:T(8,128)(2,1)}, bf16[8,128,128]{2,1,0:T(8,128)(2,1)S(1)}, u32[]{:S(2)}, u32[]{:S(2)}) collective-permute-start(bf16[8,128,128]{2,1,0:T(8,128)(2,1)} %all_to_all.30.mine_ref), channel_id=1, source_target_pairs={{0,8},{8,0},{1,9},{9,1},{2,10},{10,2},{3,11},{11,3},{4,12},{12,4},... | collective-permute-start | bytes 786440 | tf_op jit(solution)/shard_map/ppermute | solution.py:233
  119.7 14.4 %all-to-all-start.4 = ((bf16[8,128,128]{2,1,0:T(8,128)(2,1)}), bf16[8,128,128]{2,1,0:T(8,128)(2,1)S(1)}, u32[]{:S(2)}, u32[]{:S(2)}) async-start(bf16[8,128,128]{2,1,0:T(8,128)(2,1)} %all_to_all.30.mine_ref), calls=%async_computation.4 | async-start | bytes 524288 | tf_op jit(solution)/shard_map/all_to_all | solution.py:234
  134.1 13.8 %all-to-all-start.5 = ((bf16[32,16,256]{2,1,0:T(8,128)(2,1)}), bf16[32,16,256]{2,1,0:T(8,128)(2,1)S(1)}, u32[]{:S(2)}, u32[]{:S(2)}) async-start(bf16[32,16,256]{2,1,0:T(8,128)(2,1)} %bitcast.7), calls=%async_computation.5 | async-start | bytes 524288 | tf_op jit(solution)/shard_map/all_to_all | solution.py:244
